TPU v7x, 32 devices: a whole 2x2x4 slice. The times are simulated.
32 devices in a mesh: section: 8 (over z, x), lane: 4 (over y, core).
Axes of the slice: x: 2, y: 2, z: 4, core: 2. Of those that a mesh axis runs over, the one named last changes fastest.
Arguments:
- value_weight: float32 [8, 1024, 256], P('section', 'lane'), may hold values from -0.1875 to 0.1875
- out_weight: float32 [8, 2048, 1024], P('section', 'lane'), may hold values from -0.125 to 0.125
- value_moment: float32 [8, 1024, 256], P('section', 'lane'), may hold values from -6 to 6
- out_moment: float32 [8, 2048, 1024], P('section', 'lane'), may hold values from -6 to 6
- inputs_saved: bfloat16 [2, 2, 8, 512, 1024], P(None, None, 'section', 'lane'), may hold values from -6 to 6
- queries_saved: bfloat16 [2, 2, 8, 512, 2048], P(None, None, 'section', 'lane'), may hold values from -100 to 100
- keys_saved: bfloat16 [2, 2, 8, 512, 256], P(None, None, 'section', 'lane'), may hold values from -5 to 5
- grad_now: bfloat16 [2, 8, 512, 1024], P(None, 'section', 'lane'), may hold values from -6 to 6
- grad_new: bfloat16 [2, 512, 1024], P(None, 'lane'), may hold values from -6 to 6
- bound_now: int32 [2, 8, 4], P(None, None, 'lane'), may hold values from 1 to 127
- bound_new: int32 [2, 4], P(None, 'lane'), may hold values from 1 to 127
Outputs:
- grad_inputs: bfloat16 [2, 2, 8, 512, 1024], P(None, None, 'section', 'lane')
- grad_queries: bfloat16 [2, 2, 8, 512, 2048], P(None, None, 'section', 'lane')
- grad_keys: bfloat16 [2, 2, 8, 512, 256], P(None, None, 'section', 'lane')
- value_weight_new: float32 [8, 1024, 256], P('section', 'lane')
- out_weight_new: float32 [8, 2048, 1024], P('section', 'lane')
- value_moment_new: float32 [8, 1024, 256], P('section', 'lane')
- out_moment_new: float32 [8, 2048, 1024], P('section', 'lane')
All inputs are finite; a program needn't handle non-finite values.
Results may differ from a plain program's by a relative error of at most 0.018.
Values may be sent and summed in bfloat16 or wider, within the bound.
No kernel may reach another device: no remote copies, remote signals or barrier semaphores. Data moves between devices by JAX's collectives and lax.ppermute only.
A program may use at most 128 MiB of HBM per device.

v0:
```python
import math

import jax
import jax.numpy as jnp
from jax import lax
from jax.sharding import PartitionSpec as P

QUERY_HEAD_COUNT = 16
KEY_VALUE_HEADS = 2
HEAD_SIZE = 128
QW = 2048
KVW = 256


decay_rate = 0.9
learn_rate = 0.01


def for_sending(x):
    return jax.tree.map(lambda a: a.astype(jnp.bfloat16) if a.dtype == jnp.float32 else a, x)


def shifted(x, axis, by):
    size = lax.axis_size(axis)
    pairs = [(i, i + by) for i in range(size) if 0 <= i + by < size]
    return lax.ppermute(x, axis, pairs)


def backward(inputs, query_rows, key_rows, cotangent, bound, w_value, w_out):
    token_rows = inputs.shape[0]
    query_group = QUERY_HEAD_COUNT // KEY_VALUE_HEADS
    scale_factor = 1.0 / math.sqrt(HEAD_SIZE)
    value_matrix = jnp.dot(inputs, w_value, preferred_element_type=jnp.float32).astype(jnp.bfloat16)
    heads_of_query = query_rows.reshape(token_rows, KEY_VALUE_HEADS, query_group, HEAD_SIZE)
    heads_of_key = key_rows.reshape(token_rows, KEY_VALUE_HEADS, HEAD_SIZE)
    heads_of_value = value_matrix.reshape(token_rows, KEY_VALUE_HEADS, HEAD_SIZE)
    scores = (
        jnp.einsum(
            "ihgd,jhd->hgij", heads_of_query, heads_of_key, preferred_element_type=jnp.float32
        )
        * scale_factor
    )
    places = jnp.arange(token_rows)
    second = places >= bound
    allowed = (places[None, :] <= places[:, None]) & (second[:, None] == second[None, :])
    scores = jnp.where(allowed[None, None], scores, -1e30)
    top_score = jnp.max(scores, axis=-1, keepdims=True)
    expo = jnp.exp(scores - top_score)
    probs = expo / jnp.sum(expo, axis=-1, keepdims=True)
    probs_low = probs.astype(jnp.bfloat16)
    attended = (
        jnp.einsum("hgij,jhd->ihgd", probs_low, heads_of_value, preferred_element_type=jnp.float32)
        .astype(jnp.bfloat16)
        .reshape(token_rows, QW)
    )
    attended_gradient = jnp.einsum(
        "td,cd->tc", cotangent, w_out, preferred_element_type=jnp.float32
    ).astype(jnp.bfloat16)
    head_gradient = attended_gradient.reshape(token_rows, KEY_VALUE_HEADS, query_group, HEAD_SIZE)
    grad_values = (
        jnp.einsum("hgij,ihgd->jhd", probs_low, head_gradient, preferred_element_type=jnp.float32)
        .astype(jnp.bfloat16)
        .reshape(token_rows, KVW)
    )
    grad_inputs = (
        cotangent.astype(jnp.float32)
        + jnp.einsum("tc,dc->td", grad_values, w_value, preferred_element_type=jnp.float32)
    ).astype(jnp.bfloat16)
    grad_probs = jnp.einsum(
        "ihgd,jhd->hgij", head_gradient, heads_of_value, preferred_element_type=jnp.float32
    )
    delta = jnp.sum(probs * grad_probs, axis=-1, keepdims=True)
    grad_scores = (probs * (grad_probs - delta) * scale_factor).astype(jnp.bfloat16)
    grad_queries = (
        jnp.einsum("hgij,jhd->ihgd", grad_scores, heads_of_key, preferred_element_type=jnp.float32)
        .astype(jnp.bfloat16)
        .reshape(token_rows, QW)
    )
    grad_keys = (
        jnp.einsum(
            "hgij,ihgd->jhd", grad_scores, heads_of_query, preferred_element_type=jnp.float32
        )
        .astype(jnp.bfloat16)
        .reshape(token_rows, KVW)
    )
    grad_wvalue = jnp.einsum("td,tc->dc", inputs, grad_values, preferred_element_type=jnp.float32)
    grad_wout = jnp.einsum("tc,td->cd", attended, cotangent, preferred_element_type=jnp.float32)
    return (grad_inputs, grad_queries, grad_keys, grad_wvalue, grad_wout)


def fold_columns(array, sections):
    count, width = array.shape
    return array.reshape(count, sections, width // sections).transpose(1, 0, 2)


def unfold_columns(array):
    sections, count, width = array.shape
    return array.transpose(1, 0, 2).reshape(count, sections * width)


def mirror_weights(value_rows, out_rows):
    sections = lax.axis_size("section")
    spread_value, spread_out = (
        lax.all_to_all(
            fold_columns(value_rows, sections), "section", split_axis=0, concat_axis=0, tiled=True
        ),
        lax.all_to_all(
            fold_columns(out_rows, sections), "section", split_axis=0, concat_axis=0, tiled=True
        ),
    )
    got_value, got_out = (
        lax.all_to_all(spread_value[::-1], "section", split_axis=0, concat_axis=0, tiled=True),
        lax.all_to_all(spread_out[::-1], "section", split_axis=0, concat_axis=0, tiled=True),
    )
    return (unfold_columns(got_value), unfold_columns(got_out))


def mirror_gradients(value_rows, out_rows):
    sections = lax.axis_size("section")
    spread_value, spread_out = (
        lax.all_to_all(
            fold_columns(value_rows, sections).astype(jnp.bfloat16),
            "section",
            split_axis=0,
            concat_axis=0,
            tiled=True,
        ).astype(jnp.float32),
        lax.all_to_all(
            fold_columns(out_rows, sections).astype(jnp.bfloat16),
            "section",
            split_axis=0,
            concat_axis=0,
            tiled=True,
        ).astype(jnp.float32),
    )
    got_value, got_out = (
        lax.all_to_all(
            for_sending(spread_value[::-1]), "section", split_axis=0, concat_axis=0, tiled=True
        ),
        lax.all_to_all(
            for_sending(spread_out[::-1]), "section", split_axis=0, concat_axis=0, tiled=True
        ),
    )
    return (unfold_columns(got_value), unfold_columns(got_out))


def shards(
    value_weight,
    out_weight,
    value_moment,
    out_moment,
    inputs_saved,
    queries_saved,
    keys_saved,
    grad_now,
    grad_new,
    bound_now,
    bound_new,
):
    sections = lax.axis_size("section")
    relay_lanes = lax.axis_size("lane")
    place = lax.axis_index("section")
    own_value = value_weight[0].astype(jnp.bfloat16)
    own_out = out_weight[0].astype(jnp.bfloat16)
    mirror_value, mirror_out = mirror_weights(own_value, own_out)
    value_first, output_first, value_second, output_second = (
        lax.all_gather(own_value, "lane", axis=0, tiled=True),
        lax.all_gather(own_out, "lane", axis=0, tiled=True),
        lax.all_gather(mirror_value, "lane", axis=0, tiled=True),
        lax.all_gather(mirror_out, "lane", axis=0, tiled=True),
    )
    early_first = backward(
        inputs_saved[0, 0, 0],
        queries_saved[0, 0, 0],
        keys_saved[0, 0, 0],
        grad_now[0, 0],
        bound_now[0, place, 0],
        value_first,
        output_first,
    )
    early_second = backward(
        inputs_saved[1, 0, 0],
        queries_saved[1, 0, 0],
        keys_saved[1, 0, 0],
        grad_now[1, 0],
        bound_now[1, place, 0],
        value_second,
        output_second,
    )
    arrived_first = shifted(early_first[0], "section", -1)
    arrived_second = shifted(early_second[0], "section", 1)
    at_tail = place == sections - 1
    cot_first = jnp.where(at_tail, grad_new[0], arrived_first)
    bound_first = jnp.where(
        at_tail, bound_new[0, 0], bound_now[0, jnp.minimum(place + 1, sections - 1), 0]
    )
    at_head = place == 0
    cot_second = jnp.where(at_head, grad_new[1], arrived_second)
    bound_second = jnp.where(at_head, bound_new[1, 0], bound_now[1, jnp.maximum(place - 1, 0), 0])
    late_first = backward(
        inputs_saved[0, 1, 0],
        queries_saved[0, 1, 0],
        keys_saved[0, 1, 0],
        cot_first,
        bound_first,
        value_first,
        output_first,
    )
    late_second = backward(
        inputs_saved[1, 1, 0],
        queries_saved[1, 1, 0],
        keys_saved[1, 1, 0],
        cot_second,
        bound_second,
        value_second,
        output_second,
    )
    term_value_first = early_first[3] + late_first[3]
    term_out_first = early_first[4] + late_first[4]
    term_value_second = early_second[3] + late_second[3]
    term_out_second = early_second[4] + late_second[4]
    sum_value_first, sum_out_first, sum_value_second, sum_out_second = (
        lax.psum_scatter(
            term_value_first.astype(jnp.bfloat16), "lane", scatter_dimension=0, tiled=True
        ).astype(jnp.float32),
        lax.psum_scatter(
            term_out_first.astype(jnp.bfloat16), "lane", scatter_dimension=0, tiled=True
        ).astype(jnp.float32),
        lax.psum_scatter(
            term_value_second.astype(jnp.bfloat16), "lane", scatter_dimension=0, tiled=True
        ).astype(jnp.float32),
        lax.psum_scatter(
            term_out_second.astype(jnp.bfloat16), "lane", scatter_dimension=0, tiled=True
        ).astype(jnp.float32),
    )
    back_value, back_out = mirror_gradients(sum_value_second, sum_out_second)
    mean_value = (sum_value_first + back_value) / relay_lanes
    mean_out = (sum_out_first + back_out) / relay_lanes
    value_moment_new = decay_rate * value_moment + mean_value[None]
    out_moment_new = decay_rate * out_moment + mean_out[None]
    value_weight_new = value_weight - learn_rate * value_moment_new
    out_weight_new = out_weight - learn_rate * out_moment_new
    grad_inputs = jnp.stack(
        [jnp.stack([early_first[0], late_first[0]]), jnp.stack([early_second[0], late_second[0]])]
    )[:, :, None]
    grad_queries = jnp.stack(
        [jnp.stack([early_first[1], late_first[1]]), jnp.stack([early_second[1], late_second[1]])]
    )[:, :, None]
    grad_keys = jnp.stack(
        [jnp.stack([early_first[2], late_first[2]]), jnp.stack([early_second[2], late_second[2]])]
    )[:, :, None]
    return (
        grad_inputs,
        grad_queries,
        grad_keys,
        value_weight_new,
        out_weight_new,
        value_moment_new,
        out_moment_new,
    )


def solution(mesh):
    return jax.shard_map(
        shards,
        mesh=mesh,
        in_specs=(
            P("section", "lane", None),
            P("section", "lane", None),
            P("section", "lane", None),
            P("section", "lane", None),
            P(None, None, "section", "lane", None),
            P(None, None, "section", "lane", None),
            P(None, None, "section", "lane", None),
            P(None, "section", "lane", None),
            P(None, "lane", None),
            P(None, None, "lane"),
            P(None, "lane"),
        ),
        out_specs=(
            P(None, None, "section", "lane", None),
            P(None, None, "section", "lane", None),
            P(None, None, "section", "lane", None),
            P("section", "lane", None),
            P("section", "lane", None),
            P("section", "lane", None),
            P("section", "lane", None),
        ),
        check_vma=False,
    )
```

profile of v0, /device:TPU:10, one launch (start us, length us, event | category | flops | bytes accessed | tf_op | source)
XLA Modules:
  0.0 311.6 jit_solution(10690880016942901694)
XLA Ops:
  7.2 2.6 copy.193
  11.5 29.6 %all_to_all.40 = bf16[8,512,128]{2,1,0:T(8,128)(2,1)S(1)} all-to-all(bf16[8,512,128]{2,1,0:T(8,128)(2,1)S(1)} %copy.205), channel_id=1, replica_groups=mesh['section'=8,'lane'=4] {'section'}, dimensions={0} | all-to-all | bytes 2097152 | tf_op jit(solution)/shard_map/all_to_all | solution.py:107
  41.2 28.8 %all_to_all.41 = bf16[8,512,128]{2,1,0:T(8,128)(2,1)S(1)} all-to-all(bf16[8,512,128]{2,1,0:T(8,128)(2,1)S(1)} %rev.12), channel_id=1, replica_groups=mesh['section'=8,'lane'=4] {'section'}, dimensions={0} | all-to-all | bytes 2097152 | tf_op jit(solution)/shard_map/all_to_all | solution.py:113
  72.2 5.8 %all-to-all-start.2 = ((bf16[8,256,32]{1,2,0:T(8,128)(2,1)}), bf16[8,256,32]{1,2,0:T(8,128)(2,1)S(1)}, u32[]{:S(2)}, u32[]{:S(2)}) async-start(bf16[8,256,32]{1,2,0:T(8,128)(2,1)} %bitcast.38), calls=%async_computation.2 | async-start | bytes 262144 | tf_op jit(solution)/shard_map/all_to_all | solution.py:104
  93.7 6.0 %all-to-all-start.3 = ((bf16[8,256,32]{1,2,0:T(8,128)(2,1)}), bf16[8,256,32]{1,2,0:T(8,128)(2,1)S(1)}, u32[]{:S(2)}, u32[]{:S(2)}) async-start(bf16[8,256,32]{1,2,0:T(8,128)(2,1)} %rev.13), calls=%async_computation.3 | async-start | bytes 262144 | tf_op jit(solution)/shard_map/all_to_all | solution.py:112
  103.5 7.4 %all-gather.1 = bf16[1,1024,256]{1,2,0:T(8,128)(2,1)S(1)} all-gather(bf16[1,256,256]{1,2,0:T(8,128)(2,1)} %convert_element_type.265), channel_id=3, replica_groups=mesh['section'=8,'lane'=4] {'lane'}, dimensions={1}, use_global_device_ids=true | all-gather | bytes 655360 | tf_op jit(solution)/shard_map/all_gather | solution.py:167
  110.9 7.3 %all_gather.15 = bf16[1024,256]{0,1:T(8,128)(2,1)S(1)} all-gather(bf16[256,256]{0,1:T(8,128)(2,1)S(1)} %bitcast.414), channel_id=1, replica_groups=mesh['section'=8,'lane'=4] {'lane'}, dimensions={0}, use_global_device_ids=true | all-gather | bytes 655360 | tf_op jit(solution)/shard_map/all_gather | solution.py:169
  120.7 3.0 fusion.62
  125.0 2.5 collective-permute-start
  127.5 2.9 fusion.57
  131.4 4.3 %collective-permute-start.1 = (bf16[128,1024]{1,0:T(8,128)(2,1)S(1)}, bf16[128,1024]{1,0:T(8,128)(2,1)}, u32[]{:S(2)}, u32[]{:S(2)}) collective-permute-start(bf16[128,1024]{1,0:T(8,128)(2,1)S(1)} %fusion.66), channel_id=1, source_target_pairs={{0,4},{4,8},{8,12},{12,16},{16,20},{20,24},{24,28},{1,5},{5,9},{9,... | collective-permute-start | bytes 786440 | tf_op jit(solution)/shard_map/ppermute | solution.py:26
  138.4 3.7 %collective-permute-done.1 = bf16[128,1024]{1,0:T(8,128)(2,1)} collective-permute-done((bf16[128,1024]{1,0:T(8,128)(2,1)S(1)}, bf16[128,1024]{1,0:T(8,128)(2,1)}, u32[]{:S(2)}, u32[]{:S(2)}) %collective-permute-start.1) | collective-permute-done | bytes 262176 | tf_op jit(solution)/shard_map/ppermute | solution.py:26
  143.4 3.0 fusion.58
  152.6 3.3 %add_convert_fusion = bf16[2048,1024]{1,0:T(8,128)(2,1)} fusion(f32[2048,1024]{1,0:T(8,128)S(1)} %fusion.121, bf16[128,2048]{0,1:T(8,128)(2,1)S(1)} %bitcast.410, bf16[128,1024]{1,0:T(8,128)(2,1)S(1)} %get-tuple-element.44), kind=kOutput, calls=%fused_computation.8 | convolution fusion | flops 541065216 | bytes 13369344 | tf_op jit(solution)/shard_map/tc,td->cd/dot_general | solution.py:87
  159.0 2.9 fusion.182
  176.8 2.9 fusion.59
  185.4 3.2 %add_convert_fusion.1 = bf16[2048,1024]{1,0:T(8,128)(2,1)} fusion(f32[2048,1024]{1,0:T(8,128)S(1)} %fusion.124, bf16[128,2048]{0,1:T(8,128)(2,1)S(1)} %bitcast.411, bf16[128,1024]{1,0:T(8,128)(2,1)S(1)} %get-tuple-element.43), kind=kOutput, calls=%fused_computation.9 | convolution fusion | flops 541065216 | bytes 13369344 | tf_op jit(solution)/shard_map/tc,td->cd/dot_general | solution.py:87
  190.8 3.2 %convolution_convert_fusion.5 = bf16[2,8,128,128]{2,3,1,0:T(8,128)(2,1)} fusion(bf16[128,2,128,1]{0,2,3,1:T(8,128)(2,1)} %bitcast.445, f32[2,8,128,128]{2,3,1,0:T(8,128)S(1)} %convolution_bitcast_fusion.3, f32[2,8,128,128]{2,3,1,0:T(8,128)} %copy-done.21, f32[2,8,128]{2,1,0:T(8,128)} %copy-done.51), kind=kOutput, calls=%fused_computation.69 | convolution fusion | flops 69208192 | bytes 2695168 | tf_op jit(solution)/shard_map/hgij,jhd->ihgd/dot_general | solution.py:75
  194.0 6.9 %all-to-all-start.4 = ((bf16[8,256,32]{1,2,0:T(8,128)(2,1)}), bf16[8,256,32]{1,2,0:T(8,128)(2,1)S(1)}, u32[]{:S(2)}, u32[]{:S(2)}) async-start(bf16[8,256,32]{1,2,0:T(8,128)(2,1)} %bitcast.439), calls=%async_computation.6 | async-start | bytes 262144 | tf_op jit(solution)/shard_map/all_to_all | solution.py:121
  200.9 18.4 %reduce-scatter.11.cloned.1.call-done = bf16[512,1024]{1,0:T(8,128)(2,1)} async-done(((bf16[2048,1024]{1,0:T(8,128)(2,1)}), bf16[512,1024]{1,0:T(8,128)(2,1)}) %reduce-scatter.11.cloned.1.call-update) | async-done | bytes 1048592 | tf_op jit(solution)/shard_map/reduce_scatter | solution.py:232
  219.3 2.4 bitcast_bitcast_fusion
  222.4 6.0 %all-to-all-start.6 = ((bf16[8,512,128]{2,1,0:T(8,128)(2,1)}), bf16[8,512,128]{2,1,0:T(8,128)(2,1)S(1)}, u32[]{:S(2)}, u32[]{:S(2)}) async-start(bf16[8,512,128]{2,1,0:T(8,128)(2,1)} %bitcast_bitcast_fusion), calls=%async_computation.10 | async-start | bytes 2097152 | tf_op jit(solution)/shard_map/all_to_all | solution.py:128
  228.5 3.4 %fusion.71 = bf16[2,128,128]{1,2,0:T(8,128)(2,1)} fusion(bf16[128,2,8,128]{0,3,2,1:T(8,128)(2,1)S(1)} %bitcast.420, f32[2,8,128,128]{2,3,1,0:T(8,128)} %copy-done.22, f32[2,8,128,128]{2,3,1,0:T(8,128)} %copy-done.21, f32[2,8,128]{2,1,0:T(8,128)} %copy-done.51), kind=kOutput, calls=%fused_computation.100 | convolution fusion | flops 68978816 | bytes 2695168 | tf_op jit(solution)/shard_map/hgij,ihgd->jhd/dot_general | solution.py:80
  236.9 3.6 %convolution_convert_fusion.3 = bf16[2,8,128,128]{2,3,1,0:T(8,128)(2,1)} fusion(bf16[128,2,128,1]{0,2,3,1:T(8,128)(2,1)} %bitcast.443, f32[2,8,128,128]{2,3,1,0:T(8,128)} %convolution_bitcast_fusion.1, f32[2,8,128,128]{2,3,1,0:T(8,128)} %get-tuple-element.58, f32[2,8,128]{2,1,0:T(8,128)S(1)} %get-tuple-element.57), kind=kOutput, calls=%fused_computation.67 | convolution fusion | flops 69208192 | bytes 2695168 | tf_op jit(solution)/shard_map/hgij,jhd->ihgd/dot_general | solution.py:75
  242.6 3.3 %fusion.73 = bf16[2,128,128]{1,2,0:T(8,128)(2,1)} fusion(bf16[128,2,8,128]{0,3,2,1:T(8,128)(2,1)S(1)} %bitcast.418, f32[2,8,128,128]{2,3,1,0:T(8,128)} %convolution_bitcast_fusion.1, f32[2,8,128,128]{2,3,1,0:T(8,128)} %get-tuple-element.58, f32[2,8,128]{2,1,0:T(8,128)S(1)} %get-tuple-element.57), kind=kOutput, calls=%fused_computation.102 | convolution fusion | flops 68978816 | bytes 2695168 | tf_op jit(solution)/shard_map/hgij,ihgd->jhd/dot_general | solution.py:80
  248.9 3.7 %convolution_convert_fusion.4 = bf16[2,8,128,128]{2,3,1,0:T(8,128)(2,1)} fusion(bf16[128,2,128,1]{0,2,3,1:T(8,128)(2,1)} %bitcast.447, f32[2,8,128,128]{2,3,1,0:T(8,128)} %convolution_bitcast_fusion.2, f32[2,8,128,128]{2,3,1,0:T(8,128)} %get-tuple-element.62, f32[2,8,128]{2,1,0:T(8,128)} %get-tuple-element.61), kind=kOutput, calls=%fused_computation.68 | convolution fusion | flops 69208192 | bytes 2695168 | tf_op jit(solution)/shard_map/hgij,jhd->ihgd/dot_general | solution.py:75
  252.6 4.2 %fusion.72 = bf16[2,128,128]{1,2,0:T(8,128)(2,1)} fusion(bf16[128,2,8,128]{0,3,2,1:T(8,128)(2,1)S(1)} %bitcast.422, f32[2,8,128,128]{2,3,1,0:T(8,128)} %convolution_bitcast_fusion.2, f32[2,8,128,128]{2,3,1,0:T(8,128)} %get-tuple-element.62, f32[2,8,128]{2,1,0:T(8,128)S(1)} %copy-done.52), kind=kOutput, calls=%fused_computation.101 | convolution fusion | flops 68978816 | bytes 2695168 | tf_op jit(solution)/shard_map/hgij,ihgd->jhd/dot_general | solution.py:80
  259.7 6.0 %all-to-all-start.5 = ((bf16[8,256,32]{1,2,0:T(8,128)(2,1)}), bf16[8,256,32]{1,2,0:T(8,128)(2,1)S(1)}, u32[]{:S(2)}, u32[]{:S(2)}) async-start(bf16[8,256,32]{1,2,0:T(8,128)(2,1)} %rev.19), calls=%async_computation.7 | async-start | bytes 262144 | tf_op jit(solution)/shard_map/all_to_all | solution.py:137
  265.7 3.8 %convolution_convert_fusion.2 = bf16[2,8,128,128]{2,3,1,0:T(8,128)(2,1)} fusion(bf16[128,2,128,1]{0,2,3,1:T(8,128)(2,1)} %bitcast.441, f32[2,8,128,128]{2,3,1,0:T(8,128)} %convolution_bitcast_fusion, f32[2,8,128,128]{2,3,1,0:T(8,128)} %copy-done.20, f32[2,8,128]{2,1,0:T(8,128)S(1)} %get-tuple-element.59), kind=kOutput, calls=%fused_computation.66 | convolution fusion | flops 69208192 | bytes 2695168 | tf_op jit(solution)/shard_map/hgij,jhd->ihgd/dot_general | solution.py:75
  270.8 5.8 %all-to-all-start.7 = ((bf16[8,512,128]{2,1,0:T(8,128)(2,1)}), bf16[8,512,128]{2,1,0:T(8,128)(2,1)S(1)}, u32[]{:S(2)}, u32[]{:S(2)}) async-start(bf16[8,512,128]{2,1,0:T(8,128)(2,1)} %rev.18), calls=%async_computation.11 | async-start | bytes 2097152 | tf_op jit(solution)/shard_map/all_to_all | solution.py:140
  276.7 3.8 %fusion.74 = bf16[2,128,128]{1,2,0:T(8,128)(2,1)} fusion(bf16[128,2,8,128]{0,3,2,1:T(8,128)(2,1)} %bitcast.416, f32[2,8,128,128]{2,3,1,0:T(8,128)} %convolution_bitcast_fusion, f32[2,8,128,128]{2,3,1,0:T(8,128)} %copy-done.20, f32[2,8,128]{2,1,0:T(8,128)S(1)} %get-tuple-element.59), kind=kOutput, calls=%fused_computation.103 | convolution fusion | flops 68978816 | bytes 2695168 | tf_op jit(solution)/shard_map/hgij,ihgd->jhd/dot_general | solution.py:80
  300.0 4.7 %multiply_subtract_fusion = (f32[1,512,1024]{2,1,0:T(8,128)}, f32[1,512,1024]{2,1,0:T(8,128)}) fusion(f32[1,512,1024]{2,1,0:T(8,128)S(1)} %copy-done, bf16[512,1024]{1,0:T(8,128)(2,1)} %reduce-scatter.9.cloned.1.call-done, f32[1,512,1024]{2,1,0:T(8,128)} %param.14, bf16[8,512,128]{2,1,0:T(8,128)(2,1)S(1)} %all-to-all-done.7), kind=kLoop, calls=%fused_computation.24 | loop fusion | flops 4194304 | bytes 10485760 | tf_op jit(solution)/shard_map/sub | solution.py:242
  (231 shorter events, 95.8 us)
Async XLA Ops:
  7.2 113.5 %all-gather.7.cloned.1.call-start = ((), (), s32[]{:S(2)}) async-start(), calls=%async_computation.17 | async-start | bytes 5242880 | tf_op jit(solution)/shard_map/all_gather | solution.py:168
  9.8 117.7 %all-gather.5.cloned.1.call-start = ((), (), s32[]{:S(2)}) async-start(), calls=%async_computation.12 | async-start | bytes 5242880 | tf_op jit(solution)/shard_map/all_gather | solution.py:170
  41.1 30.2 %copy-start.41 = (f32[1,256,256]{2,1,0:T(8,128)S(1)}, f32[1,256,256]{2,1,0:T(8,128)}, u32[]{:S(2)}) copy-start(f32[1,256,256]{2,1,0:T(8,128)} %param.11) | copy-start | bytes 786436
  70.0 9.8 %copy-start.14 = (bf16[2,2,1,128,2048]{4,3,2,1,0:T(8,128)(2,1)S(1)}, bf16[2,2,1,128,2048]{4,3,2,1,0:T(8,128)(2,1)}, u32[]{:S(2)}) copy-start(bf16[2,2,1,128,2048]{4,3,2,1,0:T(8,128)(2,1)} %param.16) | copy-start | bytes 6291460
  71.4 12.9 %copy-start.4 = (f32[1,256,256]{1,2,0:T(8,128)}, f32[1,256,256]{1,2,0:T(8,128)S(1)}, u32[]{:S(2)}) copy-start(f32[1,256,256]{1,2,0:T(8,128)S(1)} %copy.199) | copy-start | bytes 786436
  72.2 20.9 %all-to-all-start.2 = ((bf16[8,256,32]{1,2,0:T(8,128)(2,1)}), bf16[8,256,32]{1,2,0:T(8,128)(2,1)S(1)}, u32[]{:S(2)}, u32[]{:S(2)}) async-start(bf16[8,256,32]{1,2,0:T(8,128)(2,1)} %bitcast.38), calls=%async_computation.2 | async-start | bytes 262144 | tf_op jit(solution)/shard_map/all_to_all | solution.py:104
  79.7 9.4 %copy-start.50 = (bf16[1,1,1,128,256]{3,4,2,1,0:T(8,128)(2,1)}, bf16[1,1,1,128,256]{3,4,2,1,0:T(8,128)(2,1)S(1)}, u32[]{:S(2)}) copy-start(bf16[1,1,1,128,256]{3,4,2,1,0:T(8,128)(2,1)S(1)} %copy.316) | copy-start | bytes 196612
  91.3 11.0 %copy-start.20 = (f32[2,8,128,128]{2,3,1,0:T(8,128)}, f32[2,8,128,128]{2,3,1,0:T(8,128)S(1)}, u32[]{:S(2)}) copy-start(f32[2,8,128,128]{2,3,1,0:T(8,128)S(1)} %get-tuple-element.60) | copy-start | bytes 3145732
  93.7 17.1 %all-to-all-start.3 = ((bf16[8,256,32]{1,2,0:T(8,128)(2,1)}), bf16[8,256,32]{1,2,0:T(8,128)(2,1)S(1)}, u32[]{:S(2)}, u32[]{:S(2)}) async-start(bf16[8,256,32]{1,2,0:T(8,128)(2,1)} %rev.13), calls=%async_computation.3 | async-start | bytes 262144 | tf_op jit(solution)/shard_map/all_to_all | solution.py:112
  99.7 20.9 %copy-start.1 = (bf16[2,1,128,1024]{3,2,1,0:T(8,128)(2,1)S(1)}, bf16[2,1,128,1024]{3,2,1,0:T(8,128)(2,1)}, u32[]{:S(2)}) copy-start(bf16[2,1,128,1024]{3,2,1,0:T(8,128)(2,1)} %param.18) | copy-start | bytes 1572868
  99.7 94.3 %reduce-scatter.7.cloned.1.call-start = ((), (), s32[]{:S(2)}) async-start(), calls=%async_computation.14 | async-start | bytes 655360 | tf_op jit(solution)/shard_map/reduce_scatter | solution.py:229
  125.0 13.4 %collective-permute-start = (bf16[128,1024]{1,0:T(8,128)(2,1)S(1)}, bf16[128,1024]{1,0:T(8,128)(2,1)}, u32[]{:S(2)}, u32[]{:S(2)}) collective-permute-start(bf16[128,1024]{1,0:T(8,128)(2,1)S(1)} %fusion.65), channel_id=1, source_target_pairs={{4,0},{8,4},{12,8},{16,12},{20,16},{24,20},{28,24},{5,1},{9,5},{13... | collective-permute-start | bytes 786440 | tf_op jit(solution)/shard_map/ppermute | solution.py:26
  131.4 15.0 %copy-start.24 = (bf16[128,1024]{1,0:T(8,128)(2,1)}, bf16[128,1024]{1,0:T(8,128)(2,1)S(1)}, u32[]{:S(2)}) copy-start(bf16[128,1024]{1,0:T(8,128)(2,1)S(1)} %fusion.66) | copy-start | bytes 786436
  131.4 10.7 %collective-permute-start.1 = (bf16[128,1024]{1,0:T(8,128)(2,1)S(1)}, bf16[128,1024]{1,0:T(8,128)(2,1)}, u32[]{:S(2)}, u32[]{:S(2)}) collective-permute-start(bf16[128,1024]{1,0:T(8,128)(2,1)S(1)} %fusion.66), channel_id=1, source_target_pairs={{0,4},{4,8},{8,12},{12,16},{16,20},{20,24},{24,28},{1,5},{5,9},{9,... | collective-permute-start | bytes 786440 | tf_op jit(solution)/shard_map/ppermute | solution.py:26
  137.1 10.2 %copy-start.35 = (bf16[2,8,128,128]{3,1,0,2:T(8,128)(2,1)S(1)}, bf16[2,8,128,128]{3,1,0,2:T(8,128)(2,1)}, u32[]{:S(2)}) copy-start(bf16[2,8,128,128]{3,1,0,2:T(8,128)(2,1)} %copy.216) | copy-start | bytes 1572868
  143.3 9.2 %copy-start.2 = (bf16[128,1024]{1,0:T(8,128)(2,1)}, bf16[128,1024]{1,0:T(8,128)(2,1)S(1)}, u32[]{:S(2)}) copy-start(bf16[128,1024]{1,0:T(8,128)(2,1)S(1)} %get-tuple-element.44) | copy-start | bytes 786436
  149.8 69.6 %reduce-scatter.11.cloned.1.call-start = ((), (), s32[]{:S(2)}) async-start(), calls=%async_computation.16 | async-start | bytes 5242880 | tf_op jit(solution)/shard_map/reduce_scatter | solution.py:232
  155.9 138.7 %reduce-scatter.5.cloned.1.call-start = ((), (), s32[]{:S(2)}) async-start(), calls=%async_computation.13 | async-start | bytes 655360 | tf_op jit(solution)/shard_map/reduce_scatter | solution.py:223
  157.7 15.1 %copy-start.33 = (bf16[1,1,1,128,2048]{3,4,2,1,0:T(8,128)(2,1)}, bf16[1,1,1,128,2048]{3,4,2,1,0:T(8,128)(2,1)S(1)}, u32[]{:S(2)}) copy-start(bf16[1,1,1,128,2048]{3,4,2,1,0:T(8,128)(2,1)S(1)} %copy.319) | copy-start | bytes 1572868
  182.9 117.1 %reduce-scatter.9.cloned.1.call-start = ((), (), s32[]{:S(2)}) async-start(), calls=%async_computation.15 | async-start | bytes 5242880 | tf_op jit(solution)/shard_map/reduce_scatter | solution.py:226
  190.7 28.6 %copy-start.22 = (f32[2,8,128,128]{2,3,1,0:T(8,128)}, f32[2,8,128,128]{2,3,1,0:T(8,128)S(1)}, u32[]{:S(2)}) copy-start(f32[2,8,128,128]{2,3,1,0:T(8,128)S(1)} %convolution_bitcast_fusion.3) | copy-start | bytes 3145732
  190.7 37.7 %copy-start.32 = (bf16[1,1,1,128,2048]{3,4,2,1,0:T(8,128)(2,1)S(1)}, bf16[1,1,1,128,2048]{3,4,2,1,0:T(8,128)(2,1)}, u32[]{:S(2)}) copy-start(bf16[1,1,1,128,2048]{3,4,2,1,0:T(8,128)(2,1)} %copy-done.31) | copy-start | bytes 1572868
  194.0 27.8 %all-to-all-start.4 = ((bf16[8,256,32]{1,2,0:T(8,128)(2,1)}), bf16[8,256,32]{1,2,0:T(8,128)(2,1)S(1)}, u32[]{:S(2)}, u32[]{:S(2)}) async-start(bf16[8,256,32]{1,2,0:T(8,128)(2,1)} %bitcast.439), calls=%async_computation.6 | async-start | bytes 262144 | tf_op jit(solution)/shard_map/all_to_all | solution.py:121
  221.8 13.8 %copy-start.7 = (bf16[16,8,16,128]{3,2,1,0:T(8,128)(2,1)S(1)}, bf16[16,8,16,128]{3,2,1,0:T(8,128)(2,1)}, u32[]{:S(2)}) copy-start(bf16[16,8,16,128]{3,2,1,0:T(8,128)(2,1)} %copy-done.6) | copy-start | bytes 1572868
  222.4 37.2 %all-to-all-start.6 = ((bf16[8,512,128]{2,1,0:T(8,128)(2,1)}), bf16[8,512,128]{2,1,0:T(8,128)(2,1)S(1)}, u32[]{:S(2)}, u32[]{:S(2)}) async-start(bf16[8,512,128]{2,1,0:T(8,128)(2,1)} %bitcast_bitcast_fusion), calls=%async_computation.10 | async-start | bytes 2097152 | tf_op jit(solution)/shard_map/all_to_all | solution.py:128
  231.9 10.7 %copy-start.30 = (bf16[1,1,1,128,2048]{3,4,2,1,0:T(8,128)(2,1)S(1)}, bf16[1,1,1,128,2048]{3,4,2,1,0:T(8,128)(2,1)}, u32[]{:S(2)}) copy-start(bf16[1,1,1,128,2048]{3,4,2,1,0:T(8,128)(2,1)} %copy-done.29) | copy-start | bytes 1572868
  259.7 11.2 %all-to-all-start.5 = ((bf16[8,256,32]{1,2,0:T(8,128)(2,1)}), bf16[8,256,32]{1,2,0:T(8,128)(2,1)S(1)}, u32[]{:S(2)}, u32[]{:S(2)}) async-start(bf16[8,256,32]{1,2,0:T(8,128)(2,1)} %rev.19), calls=%async_computation.7 | async-start | bytes 262144 | tf_op jit(solution)/shard_map/all_to_all | solution.py:137
  270.5 9.9 %copy-start.36 = (bf16[2,8,128,128]{2,3,1,0:T(8,128)(2,1)S(1)}, bf16[2,8,128,128]{2,3,1,0:T(8,128)(2,1)}, u32[]{:S(2)}) copy-start(bf16[2,8,128,128]{2,3,1,0:T(8,128)(2,1)} %convolution_convert_fusion.4) | copy-start | bytes 1572868
  270.8 29.2 %all-to-all-start.7 = ((bf16[8,512,128]{2,1,0:T(8,128)(2,1)}), bf16[8,512,128]{2,1,0:T(8,128)(2,1)S(1)}, u32[]{:S(2)}, u32[]{:S(2)}) async-start(bf16[8,512,128]{2,1,0:T(8,128)(2,1)} %rev.18), calls=%async_computation.11 | async-start | bytes 2097152 | tf_op jit(solution)/shard_map/all_to_all | solution.py:140
  276.7 11.8 %copy-start.3 = (bf16[128,1024]{1,0:T(8,128)(2,1)S(1)}, bf16[128,1024]{1,0:T(8,128)(2,1)}, u32[]{:S(2)}) copy-start(bf16[128,1024]{1,0:T(8,128)(2,1)} %copy-done.2) | copy-start | bytes 786436
  276.7 12.9 %copy-start.25 = (bf16[128,1024]{1,0:T(8,128)(2,1)S(1)}, bf16[128,1024]{1,0:T(8,128)(2,1)}, u32[]{:S(2)}) copy-start(bf16[128,1024]{1,0:T(8,128)(2,1)} %copy-done.24) | copy-start | bytes 786436
  281.4 11.4 %copy-start.16 = (bf16[1,128,2048]{2,1,0:T(8,128)(2,1)S(1)}, bf16[1,128,2048]{2,1,0:T(8,128)(2,1)}, u32[]{:S(2)}) copy-start(bf16[1,128,2048]{2,1,0:T(8,128)(2,1)} %copy.223) | copy-start | bytes 1572868
  (37 other events, 164.0 us)
Sparse Core Ops, SparseCore 0:
  10.1 35.6 all-gather.6
  71.4 35.1 all-gather.4
  149.9 22.3 reduce-scatter.6
  174.8 44.5 reduce-scatter.10
  221.7 21.6 reduce-scatter.4
  245.9 44.5 reduce-scatter.8
where the time goes:
time: 316 us; the launch traced here: 312 us
  matrix products  81.4 us (26%)
  blocking collectives  73.1 us (23%)
  local copies, waits for them, and re-layouts  54.4 us (17%)
  starting transfers between devices  43.6 us (14%)
  waiting for transfers between devices  22.5 us (7%)
  other arithmetic  19.2 us (6%)
  between operations  17.4 us (6%)
    all_to_all x1, blocking collectives, mirror_weights(): lax.all_to_all(fold_columns(out_rows, sections), 'section', split_axis=0,...  29.6 us
    all_to_all x1, blocking collectives, mirror_weights(): lax.all_to_all(spread_out[::-1], 'section', split_axis=0, concat_axis=0,...  28.8 us
    reduce_scatter x1, waiting for transfers between devices, shards(): lax.psum_scatter(term_out_second.astype(jnp.bfloat16), 'lane', scatter_di...  18.4 us
    unnamed x127, local copies, waits for them, and re-layouts  16.7 us
    dot_general x4, matrix products, backward(): jnp.einsum('hgij,ihgd->jhd', grad_scores, heads_of_query, preferred_eleme...  14.6 us
    dot_general x4, matrix products, backward(): jnp.einsum('hgij,jhd->ihgd', grad_scores, heads_of_key, preferred_element...  14.4 us
    dot_general x4, matrix products, backward(): jnp.einsum('td,cd->tc', cotangent, w_out, preferred_element_type=jnp.floa...  11.8 us
    dot_general x4, matrix products, backward(): jnp.einsum('tc,td->cd', attended, cotangent, preferred_element_type=jnp.f...  10 us
  transfers between devices with their start and end apart: 14, of which 3 were waited for; matrix products, arithmetic and copies ran while one was open for 44% of the time, Pallas kernels for 0%

commit v1 on v0

v1 whole, which is shorter than its diff:
```python
import functools
import math

import jax
import jax.numpy as jnp
from jax import lax
from jax.experimental import pallas as pl
from jax.experimental.pallas import tpu as pltpu
from jax.sharding import PartitionSpec as P

HEAD = 128
KV_HEADS = 2

decay_rate = 0.9
learn_rate = 0.01

BF = jnp.bfloat16
F32 = jnp.float32
SCALE = 1.0 / math.sqrt(HEAD)


def mm(a, b, ca, cb):
    return lax.dot_general(a, b, (((ca,), (cb,)), ((), ())), preferred_element_type=F32)


def after(x, *others):
    return lax.optimization_barrier((x, *others))[0]


def piece(array, *lead):
    rest = array.shape[len(lead) :]
    return array, pl.BlockSpec((None,) * len(lead) + rest, lambda i, *s: lead + (0,) * len(rest))


def whole_out(shape):
    return pl.BlockSpec(shape, lambda i, *s: (0,) * len(shape))


def call(kernel, name, scalars, operands, shapes, flops, size, steps=1, outs=None, scratch=(), aliases=None):
    arrays, specs = zip(*operands)
    grid = pltpu.PrefetchScalarGridSpec(
        num_scalar_prefetch=len(scalars),
        grid=(steps,),
        in_specs=list(specs),
        out_specs=outs or [whole_out(s.shape) for s in shapes],
        scratch_shapes=scratch,
    )
    aliases = {len(scalars) + i: o for i, o in (aliases or {}).items()}
    return pl.pallas_call(
        kernel,
        grid_spec=grid,
        out_shape=shapes,
        input_output_aliases=aliases,
        compiler_params=pltpu.CompilerParams(vmem_limit_bytes=20 * 1024 * 1024),
        cost_estimate=pl.CostEstimate(flops=1, bytes_accessed=1, transcendentals=0),
        name=name,
    )(*scalars, *arrays)


def sds(shape, dtype=BF):
    return jax.ShapeDtypeStruct(shape, dtype)


def head_start(meta, i, per):
    place = jnp.bitwise_xor(meta[1], i // per) * per + i % per
    return place * HEAD


def columns(ref, start, size):
    return ref[:, pl.ds(pl.multiple_of(start, HEAD), size)]


def value_kernel(lanes, meta, x, *refs):
    parts, (full, out) = refs[:lanes], refs[lanes:]
    rows = parts[0].shape[1]
    for r in range(2):
        for k in range(lanes):
            at = jnp.bitwise_xor(meta[3], k) * rows
            full[r, pl.ds(pl.multiple_of(at, rows), rows), :] = parts[k][r]
        for t in range(x.shape[1]):
            out[r, t] = mm(x[r, t, 0], full[r], 1, 0).astype(BF)


def values_of(meta, inputs, parts):
    ticks, tok, d = inputs.shape[1], inputs.shape[3], inputs.shape[4]
    kvw = parts[0].shape[2]
    return call(
        functools.partial(value_kernel, len(parts)),
        "values",
        [meta],
        [piece(inputs)] + [piece(p) for p in parts],
        [sds((2, d, kvw)), sds((2, ticks, tok, kvw))],
        4 * ticks * tok * d * kvw,
        4 << 20,
    )


def queries_of(half, heads, per, meta, q):
    base = half * heads * HEAD
    return jnp.concatenate([columns(q, base + head_start(meta, i, per), HEAD) for i in range(heads)], axis=0)


def front_kernel(r, per, heads, sections, meta, bounds, q, k, v, probs, mine, send):
    t = pl.program_id(0)
    tok = q.shape[0]
    place = meta[2]
    near = jnp.clip(place + t * (1 - 2 * r), 0, sections - 1)
    at = jnp.where((t == 1) & (meta[4 + r] == 1), 2 * sections + r, r * sections + near)
    bound = bounds[at]
    key_at = lax.broadcasted_iota(jnp.int32, (tok, tok), 0)
    query_at = lax.broadcasted_iota(jnp.int32, (tok, tok), 1)
    seen = (key_at <= query_at) & ((query_at >= bound) == (key_at >= bound))
    seen = jnp.concatenate([seen.astype(F32)] * heads, axis=1) > 0.5
    for s in range(2):
        half = meta[0] if s == 0 else 1 - meta[0]
        out = mine if s == 0 else send
        key, val = columns(k, half * HEAD, HEAD), columns(v, half * HEAD, HEAD)
        x = jnp.where(seen, mm(key, queries_of(half, heads, per, meta, q), 1, 1) * SCALE, -1e30)
        e = jnp.exp(x - jnp.max(x, axis=0, keepdims=True))
        p = (e * (1.0 / jnp.sum(e, axis=0, keepdims=True))).astype(BF)
        probs[s] = p
        for i in range(heads):
            out[:, i * HEAD : (i + 1) * HEAD] = mm(p[:, i * tok : (i + 1) * tok], val, 0, 0).astype(BF)


def front(r, per, heads, sections, meta, bounds, queries, keys, values):
    ticks, tok = queries.shape[1], queries.shape[3]
    width = heads * HEAD
    operands = [
        (queries, pl.BlockSpec((None, None, None, tok, 2 * width), lambda t, *s: (r, t, 0, 0, 0))),
        (keys, pl.BlockSpec((None, None, None, tok, 2 * HEAD), lambda t, *s: (r, t, 0, 0, 0))),
        (values, pl.BlockSpec((None, None, tok, 2 * HEAD), lambda t, *s: (r, t, 0, 0))),
    ]
    outs = [
        pl.BlockSpec((None, 2, tok, heads * tok), lambda t, *s: (t, 0, 0, 0)),
        pl.BlockSpec((None, tok, width), lambda t, *s: (t, 0, 0)),
        pl.BlockSpec((None, tok, width), lambda t, *s: (t, 0, 0)),
    ]
    shapes = [sds((ticks, 2, tok, heads * tok)), sds((ticks, tok, width)), sds((ticks, tok, width))]
    return call(
        functools.partial(front_kernel, r, per, heads, sections),
        "front",
        [meta, bounds],
        operands,
        shapes,
        2 * ticks * 2 * heads * 2 * tok * tok * HEAD * 4,
        8 << 20,
        ticks,
        outs,
    )


def chosen(meta, r, refs):
    return refs[0][...] if len(refs) == 1 else jnp.where(meta[4 + r] == 1, refs[1][...], refs[0][...])


def ahead_kernel(r, t, parts, per, meta, *refs):
    own, par, weights = refs[: t + 1], refs[t + 1 : 2 * t + 2], refs[2 * t + 2 : -2]
    tok = own[0].shape[0]
    g = jnp.concatenate([chosen(meta, r, own), chosen(meta, r, par)], axis=0)
    for k in range(parts):
        ga = mm(g, weights[k][...], 1, 1).astype(BF)
        for j in range(per):
            for s in range(2):
                at = (k * per + j) * tok
                refs[s - 2][at : at + tok, :] = ga[s * tok : (s + 1) * tok, j * HEAD : (j + 1) * HEAD]


def ahead(r, t, per, meta, own, par, weights):
    tok, d = own[0][0].shape[-2:]
    shape = (len(weights) * per * tok, HEAD)
    return call(
        functools.partial(ahead_kernel, r, t, len(weights), per),
        "ahead",
        [meta],
        own + par + [piece(w) for w in weights],
        [sds(shape)] * 2,
        4 * d * shape[0] * HEAD * 2,
        4 << 20,
    )


def middle_kernel(r, t, meta, *refs):
    own = refs[: t + 1]
    probs, mine, came, w, gv_out, gi_out = refs[t + 1 :]
    h = meta[0] == 0
    a = mm(probs[0], mine[...], 1, 0).astype(BF)
    b = mm(probs[1], came[...], 1, 0).astype(BF)
    gv = jnp.concatenate([jnp.where(h, a, b), jnp.where(h, b, a)], axis=1)
    gv_out[...] = gv
    gi_out[...] = (chosen(meta, r, own).astype(F32) + mm(gv, w[...], 1, 1)).astype(BF)


def middle(r, t, meta, own, probs, mine, came, w_value):
    tok, d = own[0][0].shape[-2:]
    return call(
        functools.partial(middle_kernel, r, t),
        "middle",
        [meta],
        own + [piece(probs, t), piece(mine), piece(came), piece(w_value, r)],
        [sds((tok, 2 * HEAD)), sds((tok, d))],
        4 * tok * d * 2 * HEAD,
        2 << 20,
    )


def back_kernel(per, heads, filled, meta, q, k, v, probs, mine0, came0, mine1, came1, *refs):
    gq, gk = refs[2:] if filled else refs
    tok = q.shape[2]
    width = heads * HEAD
    for t, pair in enumerate(((mine0, came0), (mine1, came1))):
        for s in range(2):
            half = meta[0] if s == 0 else 1 - meta[0]
            base = half * width
            key, val = columns(k.at[t, 0], half * HEAD, HEAD), columns(v.at[t], half * HEAD, HEAD)
            gp = mm(val, pair[s][...], 1, 1)
            p = probs[t, s].astype(F32)
            delta = jnp.sum(p * gp, axis=0, keepdims=True)
            gs = (p * ((gp - delta) * SCALE)).astype(BF)
            for i in range(heads):
                at = pl.multiple_of(base + head_start(meta, i, per), HEAD)
                out = mm(gs[:, i * tok : (i + 1) * tok], key, 0, 0).astype(BF)
                gq.at[t, 0][:, pl.ds(at, HEAD)] = out
            out = mm(gs, queries_of(half, heads, per, meta, q.at[t, 0]), 1, 0).astype(BF)
            gk.at[t, 0][:, pl.ds(pl.multiple_of(half * HEAD, HEAD), HEAD)] = out


def back(r, per, heads, meta, queries, keys, values, probs, gas, filled=()):
    arrays = (queries, keys)
    specs = [pl.BlockSpec((None,) + a.shape[1:], lambda i, m: (r, 0, 0, 0, 0)) for a in arrays]
    operands = list(zip(arrays, specs)) + [piece(values, r), piece(probs)] + [piece(a) for a in gas]
    operands += [(a, pl.BlockSpec(memory_space=pl.ANY)) for a in filled]
    first = len(operands) - 2
    return call(
        functools.partial(back_kernel, per, heads, bool(filled)),
        "back",
        [meta],
        operands,
        [sds(a.shape) for a in arrays],
        2 * 2 * 2 * heads * 3 * queries.shape[3] ** 2 * HEAD * 4,
        8 << 20,
        outs=specs,
        aliases={first: 0, first + 1: 1} if filled else {},
    )


def outer_kernel(r, meta, mine, came, *refs):
    out = refs[-1]
    total = mm(mine[0], refs[0][...], 0, 0)
    total = total + mm(came[0], refs[1][...], 0, 0)
    total = total + mm(mine[1], chosen(meta, r, refs[2:4]), 0, 0)
    total = total + mm(came[1], chosen(meta, r, refs[4:6]), 0, 0)
    out[...] = total.astype(out.dtype)


def outer(r, k, rows, meta, mine, came, gs, dtype):
    ticks, tok = mine.shape[0], mine.shape[1]
    d = gs[0][0].shape[-1]
    step = min(rows, 256)
    first = k * (rows // step)
    block = pl.BlockSpec((ticks, tok, step), lambda i, m: (0, 0, first + i))
    outs = [pl.BlockSpec((step, d), lambda i, m: (i, 0))]
    return call(
        functools.partial(outer_kernel, r),
        "outer",
        [meta],
        [(mine, block), (came, block)] + gs,
        [sds((rows, d), dtype)],
        4 * ticks * tok * rows * d,
        4 << 20,
        rows // step,
        outs,
    )[0]


def value_grad_kernel(meta, x, gv00, gv01, gv10, gv11, own, *refs):
    sent, total = refs[:-1], refs[-1]
    rows = own.shape[1]
    for r, gvs in enumerate(((gv00, gv01), (gv10, gv11))):
        total[...] = mm(x[r, 0, 0], gvs[0][...], 0, 0) + mm(x[r, 1, 0], gvs[1][...], 0, 0)
        for k, out in enumerate((own, *sent)):
            at = jnp.bitwise_xor(meta[3], k) * rows
            out[r] = total[pl.ds(pl.multiple_of(at, rows), rows), :].astype(out.dtype)


def value_grads(meta, lanes, inputs, gvs):
    d = inputs.shape[4]
    kvw = KV_HEADS * HEAD
    rows = d // lanes
    shapes = [sds((2, rows, kvw), F32)] + [sds((2, rows, kvw))] * (lanes - 1)
    return call(
        value_grad_kernel,
        "value_grads",
        [meta],
        [piece(a) for a in (inputs, *gvs)],
        shapes,
        4 * 2 * inputs.shape[3] * d * kvw,
        4 << 20,
        scratch=[pltpu.VMEM((d, kvw), F32)],
    )


def shards(
    value_weight,
    out_weight,
    value_moment,
    out_moment,
    inputs_saved,
    queries_saved,
    keys_saved,
    grad_now,
    grad_new,
    bound_now,
    bound_new,
):
    sections = lax.axis_size("section")
    lanes = lax.axis_size("lane")
    place = lax.axis_index("section")
    lane = lax.axis_index("lane")
    half = lanes // KV_HEADS
    h, c = lane // half, lane % half
    rows = out_weight.shape[1]
    per = rows // HEAD
    heads = per * half
    at_end = (place == sections - 1, place == 0)
    meta = jnp.stack([h, c, place, lane, *at_end]).astype(jnp.int32)

    def at_lane(x, k):
        return lax.ppermute(x, "lane", [(i, i ^ k) for i in range(lanes)])

    def partner(x):
        return at_lane(x, half)

    def mirrored(x):
        return lax.ppermute(x, "section", [(i, sections - 1 - i) for i in range(sections)])

    def relayed(x, r, k=0):
        by = 1 if r else -1
        pairs = [
            (i * lanes + j, (i + by) * lanes + (j ^ k))
            for i in range(sections)
            for j in range(lanes)
            if 0 <= i + by < sections
        ]
        return lax.ppermute(x, ("section", "lane"), pairs)

    def at_ends(x):
        pairs = [(i * lanes + j, i * lanes + (j ^ half)) for i in (0, sections - 1) for j in range(lanes)]
        return lax.ppermute(x, ("section", "lane"), pairs)

    own_value = value_weight[0].astype(BF)
    mirror_value = mirrored(own_value)
    own_out = [after(out_weight, own_value)[0].astype(BF)]
    mirror_out = [mirrored(after(own_out[0], mirror_value))]

    def with_mates(pieces):
        spread = [[p] + [at_lane(p, k) for k in range(1, half)] for p in pieces]
        return [s[k] for k in range(half) for s in spread]

    parts_out = [with_mates(own_out)]
    g_par = partner(after(grad_now, mirror_value)[:, 0])
    fresh_par = at_ends(lax.dynamic_index_in_dim(grad_new, jnp.where(place == 0, 1, 0), keepdims=False))
    bounds = jnp.concatenate([bound_now.reshape(-1), bound_new.reshape(-1)])

    own, par = {}, {}
    for r in range(2):
        own[r, 0], par[r, 0] = [piece(grad_now, r, 0)], [piece(g_par, r)]
    ga, gv, gi = {}, {}, {}
    probs, mine, came = [None] * 2, [None] * 2, [None] * 2

    def run_ahead(r, t, *deps):
        weights = list(after(tuple(parts_out[r]), *deps)) if deps else parts_out[r]
        here, send = ahead(r, t, per, meta, own[r, t], par[r, t], weights)
        ga[r, t] = (here, partner(send))

    def run_front(r, v):
        probs[r], mine[r], send = front(r, per, heads, sections, meta, bounds, queries_saved, keys_saved, v)
        came[r] = partner(send)

    def run_middle(r, t, *deps):
        p = after(probs[r], *deps) if deps else probs[r]
        gv[r, t], gi[r, t] = middle(r, t, meta, own[r, t], p, *ga[r, t], w_value)

    def run_relay(r, *deps):
        sent = after(gi[r, 0], *deps) if deps else gi[r, 0]
        own[r, 1] = [piece(relayed(sent, r)), piece(grad_new, r)]
        par[r, 1] = [piece(relayed(sent, r, half)), piece(fresh_par)]

    def run_outer(r, *deps):
        m = after(mine[r], *deps) if deps else mine[r]
        gs = own[r, 0] + par[r, 0] + own[r, 1] + par[r, 1]
        away = [outer(r, k, rows, meta, m, came[r], gs, BF) for k in range(1, half)]
        total = outer(r, 0, rows, meta, after(m, *away) if away else m, came[r], gs, F32)
        for k, part in enumerate(away):
            total = total + at_lane(part, k + 1).astype(F32)
        return total

    both_value = jnp.stack([own_value, mirror_value])
    parts_value = [both_value] + [at_lane(both_value, k) for k in range(1, lanes)]
    run_ahead(0, 0)
    w_value, values = values_of(meta, inputs_saved, parts_value)
    run_front(0, values)
    run_middle(0, 0)
    run_front(1, after(values, gi[0, 0]))
    parts_out.append(with_mates(after(tuple(mirror_out), probs[1], came[0], came[1])))
    run_ahead(1, 0)
    run_middle(1, 0)
    run_relay(1)
    run_relay(0, gi[1, 0])
    relays = [own[0, 1][0][0], par[0, 1][0][0]]
    total1 = run_outer(1, *relays)
    cut = rows // 2
    send_out = total1.astype(BF)
    back_first = mirrored(send_out[:cut])
    run_ahead(0, 1, send_out)
    run_ahead(1, 1, ga[0, 1][0])
    total0 = run_outer(0, ga[1, 1][0])
    sums_out = [total0, total1]
    run_middle(0, 1, total0)
    run_middle(1, 1, gi[0, 1])
    back_second = mirrored(after(send_out, back_first, gi[1, 1])[cut:])
    gas = [[*ga[r, 0], *ga[r, 1]] for r in range(2)]
    out = back(0, per, heads, meta, queries_saved, keys_saved, values, after(probs[0], gi[1, 1]), gas[0])
    gvs = [gv[r, t] for r in range(2) for t in range(2)]
    total, *sent = value_grads(meta, lanes, inputs_saved, gvs)
    for k, part in enumerate(sent):
        total = total + at_lane(part, k + 1).astype(F32)
    sums_value = [total[0], total[1]]
    back_value = mirrored(total[1].astype(BF))
    grad_queries, grad_keys = back(
        1, per, heads, meta, queries_saved, keys_saved, values, after(probs[1], sent[0]), gas[1], out
    )
    grad_inputs = jnp.stack([jnp.stack([gi[r, t] for t in range(2)]) for r in range(2)])[:, :, None]
    back_out = jnp.concatenate([back_first, back_second], axis=0)
    back_out = after(back_out, grad_queries)
    mean_value = (sums_value[0] + back_value.astype(F32)) / lanes
    mean_out = (sums_out[0] + back_out.astype(F32)) / lanes
    value_moment_new = decay_rate * value_moment + mean_value[None]
    out_moment_new = decay_rate * out_moment + mean_out[None]
    value_weight_new = value_weight - learn_rate * value_moment_new
    out_weight_new = out_weight - learn_rate * out_moment_new

    return (
        grad_inputs,
        grad_queries,
        grad_keys,
        value_weight_new,
        out_weight_new,
        value_moment_new,
        out_moment_new,
    )


def solution(mesh):
    saved = P(None, None, "section", "lane", None)
    weight = P("section", "lane", None)
    return jax.shard_map(
        shards,
        mesh=mesh,
        in_specs=(
            weight,
            weight,
            weight,
            weight,
            saved,
            saved,
            saved,
            P(None, "section", "lane", None),
            P(None, "lane", None),
            P(None, None, "lane"),
            P(None, "lane"),
        ),
        out_specs=(saved, saved, saved, weight, weight, weight, weight),
        check_vma=False,
    )
```

time: 316 us -> 192 us (0.61)
  matrix products: 81.4 us -> 0 us
  blocking collectives: 73.1 us -> 0 us
  waiting for transfers between devices: 22.5 us -> 92 us
  local copies, waits for them, and re-layouts: 54.4 us -> 8.08 us
  Pallas kernels: 0 us -> 44.7 us
  between operations: 17.4 us -> 1.27 us
  starting transfers between devices: 43.6 us -> 33.2 us
  other arithmetic: 19.2 us -> 11 us
    ppermute x2 -> x27, waiting for transfers between devices: 3.66 us -> 92 us  [the longest x17 46.6 us: at_lane(): return lax.ppermute(x, 'lane', [(i, i ^ k) for i in range(lanes)])]
    dot_general x40 -> x0, matrix products: 75.9 us -> none  [the longest x4 14.6 us: backward(): jnp.einsum('hgij,ihgd->jhd', grad_scores, heads_of_query, preferred_eleme...]
    all_to_all x2 -> x0, blocking collectives: 58.4 us -> none  [the longest x1 29.6 us: mirror_weights(): lax.all_to_all(fold_columns(out_rows, sections), 'section', split_axis=0,...]
    pallas_call x0 -> x18, Pallas kernels: none -> 44.7 us  [call(): pl.pallas_call(kernel, grid_spec=grid, out_shape=shapes, input_output_ali...]
    all_to_all x6 -> x0, starting transfers between devices: 36.5 us -> none  [the longest x1 6.93 us: mirror_gradients(): lax.all_to_all(fold_columns(value_rows, sections).astype(jnp.bfloat16), '...]
    ppermute x2 -> x27, starting transfers between devices: 6.73 us -> 33.2 us  [the longest x4 13.7 us: relayed(): return lax.ppermute(x, ('section', 'lane'), pairs)]
    reduce_scatter x4 -> x0, waiting for transfers between devices: 18.4 us -> none  [the longest x1 18.4 us: shards(): lax.psum_scatter(term_out_second.astype(jnp.bfloat16), 'lane', scatter_di...]
    all_gather x2 -> x0, blocking collectives: 14.7 us -> none  [the longest x1 7.39 us: shards(): lax.all_gather(own_value, 'lane', axis=0, tiled=True)]
  transfers between devices with their start and end apart: 14 -> 27, of which waited for: 3 -> 15; matrix products, arithmetic and copies ran while one was open for 44% -> 3% of each run, Pallas kernels for 0% -> 16%
where the time goes in v1:
time: 192 us; the launch traced here: 190 us
  waiting for transfers between devices  92 us (48%)
  Pallas kernels  44.7 us (23%)
  starting transfers between devices  33.2 us (17%)
  other arithmetic  11 us (6%)
  local copies, waits for them, and re-layouts  8.08 us (4%)
    ppermute x17, waiting for transfers between devices, at_lane(): return lax.ppermute(x, 'lane', [(i, i ^ k) for i in range(lanes)])  46.6 us
    pallas_call x18, Pallas kernels, call(): pl.pallas_call(kernel, grid_spec=grid, out_shape=shapes, input_output_ali...  44.7 us
    ppermute x5, waiting for transfers between devices, mirrored(): lax.ppermute(x, 'section', [(i, sections - 1 - i) for i in range(sections)])  31.7 us
    ppermute x4, waiting for transfers between devices, relayed(): return lax.ppermute(x, ('section', 'lane'), pairs)  13.7 us
    ppermute x4, starting transfers between devices, relayed(): return lax.ppermute(x, ('section', 'lane'), pairs)  13.7 us
    ppermute x17, starting transfers between devices, at_lane(): return lax.ppermute(x, 'lane', [(i, i ^ k) for i in range(lanes)])  12 us
    unnamed x87, local copies, waits for them, and re-layouts  7.79 us
    ppermute x5, starting transfers between devices, mirrored(): lax.ppermute(x, 'section', [(i, sections - 1 - i) for i in range(sections)])  6.93 us
  transfers between devices with their start and end apart: 27, of which 15 were waited for; matrix products, arithmetic and copies ran while one was open for 3% of the time, Pallas kernels for 16%

profile of v1, /device:TPU:10, one launch (start us, length us, event | category | flops | bytes accessed | tf_op | source)
XLA Modules:
  0.0 190.3 jit_solution(11531698429706998575)
XLA Ops:
  1.7 2.7 %convert_bitcast_fusion.refs_2_.refs_4_ = bf16[512,1024]{1,0:T(8,128)(2,1)} fusion(f32[1,512,1024]{2,1,0:T(8,128)} %param.12), kind=kLoop, calls=%fused_computation.6 | loop fusion | flops 524288 | bytes 3145728 | tf_op jit(solution)/shard_map/convert_element_type | solution.py:353
  6.0 8.0 %collective-permute-done = bf16[256,256]{1,0:T(8,128)(2,1)S(1)} collective-permute-done((bf16[256,256]{1,0:T(8,128)(2,1)S(1)}, bf16[256,256]{1,0:T(8,128)(2,1)S(1)}, u32[]{:S(2)}, u32[]{:S(2)}) %collective-permute-start) | collective-permute-done | bytes 131104 | tf_op jit(solution)/shard_map/ppermute | solution.py:335
  18.6 10.2 %collective-permute-done.4.refs_1_ = bf16[2,128,1024]{2,1,0:T(8,128)(2,1)S(1)} collective-permute-done((bf16[2,128,1024]{2,1,0:T(8,128)(2,1)S(1)}, bf16[2,128,1024]{2,1,0:T(8,128)(2,1)S(1)}, u32[]{:S(2)}, u32[]{:S(2)}) %collective-permute-start.4) | collective-permute-done | bytes 524320 | tf_op jit(solution)/shard_map/ppermute | solution.py:329
  29.0 3.8 %ahead.4 = (bf16[1024,128]{1,0:T(8,128)(2,1)S(1)}, bf16[1024,128]{1,0:T(8,128)(2,1)}) custom-call(s32[6]{0:T(128)S(1)} %stack.69.meta, bf16[2,1,128,1024]{3,2,1,0:T(8,128)(2,1)S(1)} %copy-done.2, bf16[2,128,1024]{2,1,0:T(8,128)(2,1)S(1)} %collective-permute-done.4.refs_1_, bf16[512,1024]{1,0:T(8,128)(2,1)} %convert_bitcast_fusion.refs_2_.refs_4_, ...), custom_call_target="tpu_custom_call" | custom-call | flops 1 | bytes 1 | tf_op jit(solution)/shard_map/ahead/pallas_call | solution.py:49
  36.3 3.9 %collective-permute-done.2.refs_2_ = bf16[2,256,256]{2,1,0:T(8,128)(2,1)} collective-permute-done((bf16[2,256,256]{2,1,0:T(8,128)(2,1)}, bf16[2,256,256]{2,1,0:T(8,128)(2,1)}, u32[]{:S(2)}, u32[]{:S(2)}) %collective-permute-start.2) | collective-permute-done | bytes 262176 | tf_op jit(solution)/shard_map/ppermute | solution.py:329
  41.5 2.2 %values.1 = (bf16[2,1024,256]{2,1,0:T(8,128)(2,1)S(1)}, bf16[2,2,128,256]{3,2,1,0:T(8,128)(2,1)S(1)}) custom-call(s32[6]{0:T(128)S(1)} %stack.69.meta, bf16[2,2,1,128,1024]{4,3,2,1,0:T(8,128)(2,1)S(1)} %copy-done.16, bf16[2,256,256]{2,1,0:T(8,128)(2,1)} %pad_maximum_fusion.1.refs_0_, bf16[2,256,256]{2,1,0:T(8,128)(2,1)} %collective-permute-done.1.refs_1_, ...), custom_call_target="tpu_custom_call" | custom-call | flops 1 | bytes 1 | tf_op jit(solution)/shard_map/values/pallas_call | solution.py:49
  43.7 2.7 %front.2 = (bf16[2,2,128,1024]{3,2,1,0:T(8,128)(2,1)S(1)}, bf16[2,128,1024]{2,1,0:T(8,128)(2,1)S(1)}, bf16[2,128,1024]{2,1,0:T(8,128)(2,1)S(1)}) custom-call(s32[6]{0:T(128)S(1)} %stack.69.meta, s32[18]{0:T(128)S(1)} %pad_add_fusion.bounds, bf16[2,2,1,128,2048]{4,3,2,1,0:T(8,128)(2,1)S(1)} %copy-done.1, bf16[2,2,1,128,256]{4,3,2,1,0:T(8,128)(2,1)S(1)} %copy-done.13, ...), custom_call_target="tpu_custom_call" | custom-call | flops 1 | bytes 1 | tf_op jit(solution)/shard_map/front/pallas_call | solution.py:49
  50.1 2.7 %front.3 = (bf16[2,2,128,1024]{3,2,1,0:T(8,128)(2,1)S(1)}, bf16[2,128,1024]{2,1,0:T(8,128)(2,1)S(1)}, bf16[2,128,1024]{2,1,0:T(8,128)(2,1)S(1)}) custom-call(s32[6]{0:T(128)S(1)} %stack.69.meta, s32[18]{0:T(128)S(1)} %pad_add_fusion.bounds, bf16[2,2,1,128,2048]{4,3,2,1,0:T(8,128)(2,1)S(1)} %copy-done.1, bf16[2,2,1,128,256]{4,3,2,1,0:T(8,128)(2,1)S(1)} %copy-done.13, ...), custom_call_target="tpu_custom_call" | custom-call | flops 1 | bytes 1 | tf_op jit(solution)/shard_map/front/pallas_call | solution.py:49
  54.2 7.1 %collective-permute-done.8.came = bf16[2,128,1024]{2,1,0:T(8,128)(2,1)S(1)} collective-permute-done((bf16[2,128,1024]{2,1,0:T(8,128)(2,1)S(1)}, bf16[2,128,1024]{2,1,0:T(8,128)(2,1)S(1)}, u32[]{:S(2)}, u32[]{:S(2)}) %collective-permute-start.8) | collective-permute-done | bytes 524320 | tf_op jit(solution)/shard_map/ppermute | solution.py:329
  61.4 2.2 %collective-permute-done.7.refs_2_.refs_4_ = bf16[512,1024]{1,0:T(8,128)(2,1)} collective-permute-done((bf16[512,1024]{1,0:T(8,128)(2,1)}, bf16[512,1024]{1,0:T(8,128)(2,1)}, u32[]{:S(2)}, u32[]{:S(2)}) %collective-permute-start.7) | collective-permute-done | bytes 1048608 | tf_op jit(solution)/shard_map/ppermute | solution.py:335
  63.5 5.5 %collective-permute-done.9.came = bf16[2,128,1024]{2,1,0:T(8,128)(2,1)S(1)} collective-permute-done((bf16[2,128,1024]{2,1,0:T(8,128)(2,1)S(1)}, bf16[2,128,1024]{2,1,0:T(8,128)(2,1)S(1)}, u32[]{:S(2)}, u32[]{:S(2)}) %collective-permute-start.9) | collective-permute-done | bytes 524320 | tf_op jit(solution)/shard_map/ppermute | solution.py:329
  69.0 2.9 %collective-permute-done.10.refs_3_.refs_5_ = bf16[512,1024]{1,0:T(8,128)(2,1)S(1)} collective-permute-done((bf16[512,1024]{1,0:T(8,128)(2,1)}, bf16[512,1024]{1,0:T(8,128)(2,1)S(1)}, u32[]{:S(2)}, u32[]{:S(2)}) %collective-permute-start.10) | collective-permute-done | bytes 1048608 | tf_op jit(solution)/shard_map/ppermute | solution.py:329
  71.9 3.2 %ahead.5 = (bf16[1024,128]{1,0:T(8,128)(2,1)S(1)}, bf16[1024,128]{1,0:T(8,128)(2,1)}) custom-call(s32[6]{0:T(128)S(1)} %stack.69.meta, bf16[2,1,128,1024]{3,2,1,0:T(8,128)(2,1)S(1)} %copy-done.2, bf16[2,128,1024]{2,1,0:T(8,128)(2,1)S(1)} %collective-permute-done.4.refs_1_, bf16[512,1024]{1,0:T(8,128)(2,1)} %collective-permute-done.7.refs_2_.refs_4_, ...), custom_call_target="tpu_custom_call" | custom-call | flops 1 | bytes 1 | tf_op jit(solution)/shard_map/ahead/pallas_call | solution.py:49
  77.4 7.1 %collective-permute-done.11.refs_3_.came0 = bf16[1024,128]{1,0:T(8,128)(2,1)} collective-permute-done((bf16[1024,128]{1,0:T(8,128)(2,1)}, bf16[1024,128]{1,0:T(8,128)(2,1)}, u32[]{:S(2)}, u32[]{:S(2)}) %collective-permute-start.11) | collective-permute-done | bytes 262176 | tf_op jit(solution)/shard_map/ppermute | solution.py:329
  89.9 3.4 %collective-permute-start.16 = (bf16[128,1024]{1,0:T(8,128)(2,1)S(1)}, bf16[128,1024]{1,0:T(8,128)(2,1)S(1)}, u32[]{:S(2)}, u32[]{:S(2)}) collective-permute-start(bf16[128,1024]{1,0:T(8,128)(2,1)S(1)} %copy-done.35), channel_id=1, source_target_pairs={{4,2},{5,3},{6,0},{7,1},{8,6},{9,7},{10,4},{11,5},{12,10},{13,11},... | collective-permute-start | bytes 786440 | tf_op jit(solution)/shard_map/ppermute | solution.py:345
  93.3 2.3 %collective-permute-start.12 = (bf16[128,1024]{1,0:T(8,128)(2,1)S(1)}, bf16[128,1024]{1,0:T(8,128)(2,1)S(1)}, u32[]{:S(2)}, u32[]{:S(2)}) collective-permute-start(bf16[128,1024]{1,0:T(8,128)(2,1)S(1)} %copy-done.35), channel_id=1, source_target_pairs={{4,0},{5,1},{6,2},{7,3},{8,4},{9,5},{10,6},{11,7},{12,8},{13,9},{1... | collective-permute-start | bytes 786440 | tf_op jit(solution)/shard_map/ppermute | solution.py:345
  96.3 4.4 %collective-permute-start.14 = (bf16[128,1024]{1,0:T(8,128)(2,1)S(1)}, bf16[128,1024]{1,0:T(8,128)(2,1)S(1)}, u32[]{:S(2)}, u32[]{:S(2)}) collective-permute-start(bf16[128,1024]{1,0:T(8,128)(2,1)S(1)} %get-tuple-element.75), channel_id=1, source_target_pairs={{0,6},{1,7},{2,4},{3,5},{4,10},{5,11},{6,8},{7,9},{8,14},{9,15},{1... | collective-permute-start | bytes 786440 | tf_op jit(solution)/shard_map/ppermute | solution.py:345
  100.8 3.6 %collective-permute-start.13 = (bf16[128,1024]{1,0:T(8,128)(2,1)S(1)}, bf16[128,1024]{1,0:T(8,128)(2,1)S(1)}, u32[]{:S(2)}, u32[]{:S(2)}) collective-permute-start(bf16[128,1024]{1,0:T(8,128)(2,1)S(1)} %get-tuple-element.75), channel_id=1, source_target_pairs={{0,4},{1,5},{2,6},{3,7},{4,8},{5,9},{6,10},{7,11},{8,12},{9,13},{1... | collective-permute-start | bytes 786440 | tf_op jit(solution)/shard_map/ppermute | solution.py:345
  104.4 7.0 %collective-permute-done.16.refs_2_.refs_4_ = bf16[128,1024]{1,0:T(8,128)(2,1)S(1)} collective-permute-done((bf16[128,1024]{1,0:T(8,128)(2,1)S(1)}, bf16[128,1024]{1,0:T(8,128)(2,1)S(1)}, u32[]{:S(2)}, u32[]{:S(2)}) %collective-permute-start.16) | collective-permute-done | bytes 262176 | tf_op jit(solution)/shard_map/ppermute | solution.py:345
  111.3 3.9 %collective-permute-done.12.refs_0_.refs_2_ = bf16[128,1024]{1,0:T(8,128)(2,1)S(1)} collective-permute-done((bf16[128,1024]{1,0:T(8,128)(2,1)S(1)}, bf16[128,1024]{1,0:T(8,128)(2,1)S(1)}, u32[]{:S(2)}, u32[]{:S(2)}) %collective-permute-start.12) | collective-permute-done | bytes 262176 | tf_op jit(solution)/shard_map/ppermute | solution.py:345
  115.2 2.8 %collective-permute-done.13.refs_2_.refs_0_ = bf16[128,1024]{1,0:T(8,128)(2,1)S(1)} collective-permute-done((bf16[128,1024]{1,0:T(8,128)(2,1)S(1)}, bf16[128,1024]{1,0:T(8,128)(2,1)S(1)}, u32[]{:S(2)}, u32[]{:S(2)}) %collective-permute-start.13) | collective-permute-done | bytes 262176 | tf_op jit(solution)/shard_map/ppermute | solution.py:345
  118.1 2.1 %outer.4 = bf16[512,1024]{1,0:T(8,128)(2,1)S(1)} custom-call(s32[6]{0:T(128)S(1)} %stack.69.meta, bf16[2,128,1024]{2,1,0:T(8,128)(2,1)S(1)} %copy-done.25, bf16[2,128,1024]{2,1,0:T(8,128)(2,1)S(1)} %copy-done.27, bf16[2,1,128,1024]{3,2,1,0:T(8,128)(2,1)S(1)} %copy-done.2, bf16[2,128,1024]{2,1,0:T(8,128)(2,1)S(1)} %copy-done.4, ...), custom_call_target="tpu_custom_call" | custom-call | flops 1 | bytes 1 | tf_op jit(solution)/shard_map/outer/pallas_call | solution.py:49
  120.3 2.1 %outer.5 = f32[512,1024]{1,0:T(8,128)S(1)} custom-call(s32[6]{0:T(128)S(1)} %stack.69.meta, bf16[2,128,1024]{2,1,0:T(8,128)(2,1)S(1)} %copy-done.25, bf16[2,128,1024]{2,1,0:T(8,128)(2,1)S(1)} %copy-done.27, bf16[2,1,128,1024]{3,2,1,0:T(8,128)(2,1)S(1)} %copy-done.2, bf16[2,128,1024]{2,1,0:T(8,128)(2,1)S(1)} %copy-done.4, ...), custom_call_target="tpu_custom_call" | custom-call | flops 1 | bytes 1 | tf_op jit(solution)/shard_map/outer/pallas_call | solution.py:49
  123.3 2.8 %ahead.6 = (bf16[1024,128]{1,0:T(8,128)(2,1)S(1)}, bf16[1024,128]{1,0:T(8,128)(2,1)S(1)}) custom-call(s32[6]{0:T(128)S(1)} %stack.69.meta, bf16[128,1024]{1,0:T(8,128)(2,1)S(1)} %collective-permute-done.12.refs_0_.refs_2_, bf16[2,128,1024]{2,1,0:T(8,128)(2,1)S(1)} %copy-done, bf16[128,1024]{1,0:T(8,128)(2,1)S(1)} %collective-permute-done.16.refs_2_.refs_4_, ...), custom_call_target="tpu_custom_call" | custom-call | flops 1 | bytes 1 | tf_op jit(solution)/shard_map/ahead/pallas_call | solution.py:49
  126.2 2.5 %ahead.7 = (bf16[1024,128]{1,0:T(8,128)(2,1)S(1)}, bf16[1024,128]{1,0:T(8,128)(2,1)S(1)}) custom-call(s32[6]{0:T(128)S(1)} %stack.69.meta, bf16[128,1024]{1,0:T(8,128)(2,1)S(1)} %collective-permute-done.13.refs_2_.refs_0_, bf16[2,128,1024]{2,1,0:T(8,128)(2,1)S(1)} %copy-done, bf16[128,1024]{1,0:T(8,128)(2,1)S(1)} %collective-permute-done.14.refs_4_.refs_2_, ...), custom_call_target="tpu_custom_call" | custom-call | flops 1 | bytes 1 | tf_op jit(solution)/shard_map/ahead/pallas_call | solution.py:49
  128.8 2.1 %outer.6 = bf16[512,1024]{1,0:T(8,128)(2,1)S(1)} custom-call(s32[6]{0:T(128)S(1)} %stack.69.meta, bf16[2,128,1024]{2,1,0:T(8,128)(2,1)S(1)} %copy-done.21, bf16[2,128,1024]{2,1,0:T(8,128)(2,1)S(1)} %copy-done.23, bf16[2,1,128,1024]{3,2,1,0:T(8,128)(2,1)S(1)} %copy-done.2, bf16[2,128,1024]{2,1,0:T(8,128)(2,1)S(1)} %copy-done.4, ...), custom_call_target="tpu_custom_call" | custom-call | flops 1 | bytes 1 | tf_op jit(solution)/shard_map/outer/pallas_call | solution.py:49
  136.4 9.4 %collective-permute-done.19.refs_4_.came1 = bf16[1024,128]{1,0:T(8,128)(2,1)S(1)} collective-permute-done((bf16[1024,128]{1,0:T(8,128)(2,1)S(1)}, bf16[1024,128]{1,0:T(8,128)(2,1)S(1)}, u32[]{:S(2)}, u32[]{:S(2)}) %collective-permute-start.19) | collective-permute-done | bytes 262176 | tf_op jit(solution)/shard_map/ppermute | solution.py:329
  151.8 19.6 %collective-permute-done.25 = bf16[256,1024]{1,0:T(8,128)(2,1)S(1)} collective-permute-done((bf16[256,1024]{1,0:T(8,128)(2,1)S(1)}, bf16[256,1024]{1,0:T(8,128)(2,1)S(1)}, u32[]{:S(2)}, u32[]{:S(2)}) %collective-permute-start.25) | collective-permute-done | bytes 524320 | tf_op jit(solution)/shard_map/ppermute | solution.py:335
  171.5 4.4 %back.2 = (bf16[2,2,1,128,2048]{4,3,2,1,0:T(8,128)(2,1)}, bf16[2,2,1,128,256]{4,3,2,1,0:T(8,128)(2,1)}) custom-call(s32[6]{0:T(128)S(1)} %stack.69.meta, bf16[2,2,1,128,2048]{4,3,2,1,0:T(8,128)(2,1)S(1)} %copy-done.1, bf16[2,2,1,128,256]{4,3,2,1,0:T(8,128)(2,1)S(1)} %copy-done.13, bf16[2,2,128,256]{3,2,1,0:T(8,128)(2,1)S(1)} %copy-done.15, ...), custom_call_target="tpu_custom_call" | custom-call | flops 1 | bytes 1 | tf_op jit(solution)/shard_map/back/pallas_call | solution.py:49
  175.9 4.3 %back.3 = (bf16[2,2,1,128,2048]{4,3,2,1,0:T(8,128)(2,1)}, bf16[2,2,1,128,256]{4,3,2,1,0:T(8,128)(2,1)}) custom-call(s32[6]{0:T(128)S(1)} %stack.69.meta, bf16[2,2,1,128,2048]{4,3,2,1,0:T(8,128)(2,1)S(1)} %copy-done.1, bf16[2,2,1,128,256]{4,3,2,1,0:T(8,128)(2,1)S(1)} %copy-done.13, ...), custom_call_target="tpu_custom_call", output_to_operand_aliasing={{0}: (9, {}), {1}: (10, {})} | custom-call | flops 1 | bytes 1 | tf_op jit(solution)/shard_map/back/pallas_call | solution.py:49
  180.5 3.0 %collective-permute-start.24 = (bf16[256,256]{1,0:T(8,128)(2,1)S(1)}, bf16[256,256]{1,0:T(8,128)(2,1)S(1)}, u32[]{:S(2)}, u32[]{:S(2)}) collective-permute-start(bf16[256,256]{1,0:T(8,128)(2,1)S(1)} %fusion.4), channel_id=1, source_target_pairs={{0,28},{4,24},{8,20},{12,16},{16,12},{20,8},{24,4},{28,0},{1,29},{... | collective-permute-start | bytes 393224 | tf_op jit(solution)/shard_map/ppermute | solution.py:335
  187.4 2.8 %multiply_subtract_fusion = (f32[1,512,1024]{2,1,0:T(8,128)}, f32[1,512,1024]{2,1,0:T(8,128)}) fusion(f32[1,512,1024]{2,1,0:T(8,128)S(1)} %copy-done.36, f32[512,1024]{1,0:T(8,128)S(1)} %convert_add_fusion, bf16[512,1024]{1,0:T(8,128)(2,1)S(1)} %pad_maximum_fusion, f32[1,512,1024]{2,1,0:T(8,128)S(1)} %copy-done.39), kind=kLoop, calls=%fused_computation.1 | loop fusion | flops 3670016 | bytes 11534336 | tf_op jit(solution)/shard_map/sub | solution.py:441
  (148 shorter events, 42.2 us)
Async XLA Ops:
  4.4 31.1 %copy-start.41 = (s32[2,8,1]{1,2,0:T(1,128)S(1)}, s32[2,8,1]{1,2,0:T(1,128)}, u32[]{:S(2)}) copy-start(s32[2,8,1]{1,2,0:T(1,128)} %param.20) | copy-start | bytes 196
  4.4 31.8 %copy-start.42 = (s32[2,1]{0,1:T(1,128)S(1)}, s32[2,1]{0,1:T(1,128)}, u32[]{:S(2)}) copy-start(s32[2,1]{0,1:T(1,128)} %param.21) | copy-start | bytes 28
  4.4 24.6 %collective-permute-start.5 = (bf16[512,1024]{1,0:T(8,128)(2,1)}, bf16[512,1024]{1,0:T(8,128)(2,1)}, u32[]{:S(2)}, u32[]{:S(2)}) collective-permute-start(bf16[512,1024]{1,0:T(8,128)(2,1)} %convert_bitcast_fusion.refs_2_.refs_4_), channel_id=1, source_target_pairs={{0,1},{1,0},{2,3},{3,2},{4,5},{5,4},{6,7},{7,6},{8,9},{9,8},{10,11... | collective-permute-start | bytes 3145736 | tf_op jit(solution)/shard_map/ppermute | solution.py:329
  4.4 9.6 %collective-permute-start = (bf16[256,256]{1,0:T(8,128)(2,1)S(1)}, bf16[256,256]{1,0:T(8,128)(2,1)S(1)}, u32[]{:S(2)}, u32[]{:S(2)}) collective-permute-start(bf16[256,256]{1,0:T(8,128)(2,1)S(1)} %convert_bitcast_fusion.1), channel_id=1, source_target_pairs={{0,28},{4,24},{8,20},{12,16},{16,12},{20,8},{24,4},{28,0},{1,29},{... | collective-permute-start | bytes 393224 | tf_op jit(solution)/shard_map/ppermute | solution.py:335
  14.0 14.8 %collective-permute-start.4 = (bf16[2,128,1024]{2,1,0:T(8,128)(2,1)S(1)}, bf16[2,128,1024]{2,1,0:T(8,128)(2,1)S(1)}, u32[]{:S(2)}, u32[]{:S(2)}) collective-permute-start(bf16[2,128,1024]{2,1,0:T(8,128)(2,1)S(1)} %bitcast.49), channel_id=1, source_target_pairs={{0,2},{1,3},{2,0},{3,1},{4,6},{5,7},{6,4},{7,5},{8,10},{9,11},{10,... | collective-permute-start | bytes 1572872 | tf_op jit(solution)/shard_map/ppermute | solution.py:329
  15.6 48.0 %collective-permute-start.7 = (bf16[512,1024]{1,0:T(8,128)(2,1)}, bf16[512,1024]{1,0:T(8,128)(2,1)}, u32[]{:S(2)}, u32[]{:S(2)}) collective-permute-start(bf16[512,1024]{1,0:T(8,128)(2,1)} %convert_bitcast_fusion.refs_2_.refs_4_), channel_id=1, source_target_pairs={{0,28},{4,24},{8,20},{12,16},{16,12},{20,8},{24,4},{28,0},{1,29},{... | collective-permute-start | bytes 3145736 | tf_op jit(solution)/shard_map/ppermute | solution.py:335
  17.9 18.4 %collective-permute-start.3 = (bf16[2,256,256]{2,1,0:T(8,128)(2,1)}, bf16[2,256,256]{2,1,0:T(8,128)(2,1)}, u32[]{:S(2)}, u32[]{:S(2)}) collective-permute-start(bf16[2,256,256]{2,1,0:T(8,128)(2,1)} %pad_maximum_fusion.1.refs_0_), channel_id=1, source_target_pairs={{0,3},{1,2},{2,1},{3,0},{4,7},{5,6},{6,5},{7,4},{8,11},{9,10},{10,... | collective-permute-start | bytes 786440 | tf_op jit(solution)/shard_map/ppermute | solution.py:329
  17.9 22.3 %collective-permute-start.2 = (bf16[2,256,256]{2,1,0:T(8,128)(2,1)}, bf16[2,256,256]{2,1,0:T(8,128)(2,1)}, u32[]{:S(2)}, u32[]{:S(2)}) collective-permute-start(bf16[2,256,256]{2,1,0:T(8,128)(2,1)} %pad_maximum_fusion.1.refs_0_), channel_id=1, source_target_pairs={{0,2},{1,3},{2,0},{3,1},{4,6},{5,7},{6,4},{7,5},{8,10},{9,11},{10,... | collective-permute-start | bytes 786440 | tf_op jit(solution)/shard_map/ppermute | solution.py:329
  28.9 43.0 %copy-start.3 = (bf16[2,128,1024]{2,1,0:T(8,128)(2,1)}, bf16[2,128,1024]{2,1,0:T(8,128)(2,1)S(1)}, u32[]{:S(2)}) copy-start(bf16[2,128,1024]{2,1,0:T(8,128)(2,1)S(1)} %collective-permute-done.4.refs_1_) | copy-start | bytes 1572868
  28.9 11.3 %collective-permute-start.1 = (bf16[2,256,256]{2,1,0:T(8,128)(2,1)}, bf16[2,256,256]{2,1,0:T(8,128)(2,1)}, u32[]{:S(2)}, u32[]{:S(2)}) collective-permute-start(bf16[2,256,256]{2,1,0:T(8,128)(2,1)} %pad_maximum_fusion.1.refs_0_), channel_id=1, source_target_pairs={{0,1},{1,0},{2,3},{3,2},{4,5},{5,4},{6,7},{7,6},{8,9},{9,8},{10,11... | collective-permute-start | bytes 786440 | tf_op jit(solution)/shard_map/ppermute | solution.py:329
  33.5 14.5 %collective-permute-start.6 = (bf16[1024,128]{1,0:T(8,128)(2,1)}, bf16[1024,128]{1,0:T(8,128)(2,1)}, u32[]{:S(2)}, u32[]{:S(2)}) collective-permute-start(bf16[1024,128]{1,0:T(8,128)(2,1)} %get-tuple-element.64), channel_id=1, source_target_pairs={{0,2},{1,3},{2,0},{3,1},{4,6},{5,7},{6,4},{7,5},{8,10},{9,11},{10,... | collective-permute-start | bytes 786440 | tf_op jit(solution)/shard_map/ppermute | solution.py:329
  46.4 14.9 %collective-permute-start.8 = (bf16[2,128,1024]{2,1,0:T(8,128)(2,1)S(1)}, bf16[2,128,1024]{2,1,0:T(8,128)(2,1)S(1)}, u32[]{:S(2)}, u32[]{:S(2)}) collective-permute-start(bf16[2,128,1024]{2,1,0:T(8,128)(2,1)S(1)} %get-tuple-element.70), channel_id=1, source_target_pairs={{0,2},{1,3},{2,0},{3,1},{4,6},{5,7},{6,4},{7,5},{8,10},{9,11},{10,... | collective-permute-start | bytes 1572872 | tf_op jit(solution)/shard_map/ppermute | solution.py:329
  53.7 15.3 %collective-permute-start.9 = (bf16[2,128,1024]{2,1,0:T(8,128)(2,1)S(1)}, bf16[2,128,1024]{2,1,0:T(8,128)(2,1)S(1)}, u32[]{:S(2)}, u32[]{:S(2)}) collective-permute-start(bf16[2,128,1024]{2,1,0:T(8,128)(2,1)S(1)} %get-tuple-element.71), channel_id=1, source_target_pairs={{0,2},{1,3},{2,0},{3,1},{4,6},{5,7},{6,4},{7,5},{8,10},{9,11},{10,... | collective-permute-start | bytes 1572872 | tf_op jit(solution)/shard_map/ppermute | solution.py:329
  69.0 2.9 %collective-permute-start.10 = (bf16[512,1024]{1,0:T(8,128)(2,1)}, bf16[512,1024]{1,0:T(8,128)(2,1)S(1)}, u32[]{:S(2)}, u32[]{:S(2)}) collective-permute-start(bf16[512,1024]{1,0:T(8,128)(2,1)} %collective-permute-done.7.refs_2_.refs_4_), channel_id=1, source_target_pairs={{0,1},{1,0},{2,3},{3,2},{4,5},{5,4},{6,7},{7,6},{8,9},{9,8},{10,11... | collective-permute-start | bytes 3145736 | tf_op jit(solution)/shard_map/ppermute | solution.py:329
  75.8 8.7 %collective-permute-start.11 = (bf16[1024,128]{1,0:T(8,128)(2,1)}, bf16[1024,128]{1,0:T(8,128)(2,1)}, u32[]{:S(2)}, u32[]{:S(2)}) collective-permute-start(bf16[1024,128]{1,0:T(8,128)(2,1)} %get-tuple-element.74), channel_id=1, source_target_pairs={{0,2},{1,3},{2,0},{3,1},{4,6},{5,7},{6,4},{7,5},{8,10},{9,11},{10,... | collective-permute-start | bytes 786440 | tf_op jit(solution)/shard_map/ppermute | solution.py:329
  77.4 40.7 %copy-start.4 = (bf16[2,128,1024]{2,1,0:T(8,128)(2,1)S(1)}, bf16[2,128,1024]{2,1,0:T(8,128)(2,1)}, u32[]{:S(2)}) copy-start(bf16[2,128,1024]{2,1,0:T(8,128)(2,1)} %copy-done.3) | copy-start | bytes 1572868
  87.9 30.1 %copy-start.27 = (bf16[2,128,1024]{2,1,0:T(8,128)(2,1)S(1)}, bf16[2,128,1024]{2,1,0:T(8,128)(2,1)}, u32[]{:S(2)}) copy-start(bf16[2,128,1024]{2,1,0:T(8,128)(2,1)} %copy-done.26) | copy-start | bytes 1572868
  89.9 21.4 %collective-permute-start.16 = (bf16[128,1024]{1,0:T(8,128)(2,1)S(1)}, bf16[128,1024]{1,0:T(8,128)(2,1)S(1)}, u32[]{:S(2)}, u32[]{:S(2)}) collective-permute-start(bf16[128,1024]{1,0:T(8,128)(2,1)S(1)} %copy-done.35), channel_id=1, source_target_pairs={{4,2},{5,3},{6,0},{7,1},{8,6},{9,7},{10,4},{11,5},{12,10},{13,11},... | collective-permute-start | bytes 786440 | tf_op jit(solution)/shard_map/ppermute | solution.py:345
  93.3 21.9 %collective-permute-start.12 = (bf16[128,1024]{1,0:T(8,128)(2,1)S(1)}, bf16[128,1024]{1,0:T(8,128)(2,1)S(1)}, u32[]{:S(2)}, u32[]{:S(2)}) collective-permute-start(bf16[128,1024]{1,0:T(8,128)(2,1)S(1)} %copy-done.35), channel_id=1, source_target_pairs={{4,0},{5,1},{6,2},{7,3},{8,4},{9,5},{10,6},{11,7},{12,8},{13,9},{1... | collective-permute-start | bytes 786440 | tf_op jit(solution)/shard_map/ppermute | solution.py:345
  95.7 19.6 %collective-permute-start.15 = (bf16[128,1024]{1,0:T(8,128)(2,1)S(1)}, bf16[128,1024]{1,0:T(8,128)(2,1)S(1)}, u32[]{:S(2)}, u32[]{:S(2)}) collective-permute-start(bf16[128,1024]{1,0:T(8,128)(2,1)S(1)} %dynamic-slice_bitcast_fusion), channel_id=1, source_target_pairs={{0,2},{1,3},{2,0},{3,1},{28,30},{29,31},{30,28},{31,29}} | collective-permute-start | bytes 786440 | tf_op jit(solution)/shard_map/ppermute | solution.py:349
  96.3 18.9 %collective-permute-start.14 = (bf16[128,1024]{1,0:T(8,128)(2,1)S(1)}, bf16[128,1024]{1,0:T(8,128)(2,1)S(1)}, u32[]{:S(2)}, u32[]{:S(2)}) collective-permute-start(bf16[128,1024]{1,0:T(8,128)(2,1)S(1)} %get-tuple-element.75), channel_id=1, source_target_pairs={{0,6},{1,7},{2,4},{3,5},{4,10},{5,11},{6,8},{7,9},{8,14},{9,15},{1... | collective-permute-start | bytes 786440 | tf_op jit(solution)/shard_map/ppermute | solution.py:345
  100.8 17.3 %collective-permute-start.13 = (bf16[128,1024]{1,0:T(8,128)(2,1)S(1)}, bf16[128,1024]{1,0:T(8,128)(2,1)S(1)}, u32[]{:S(2)}, u32[]{:S(2)}) collective-permute-start(bf16[128,1024]{1,0:T(8,128)(2,1)S(1)} %get-tuple-element.75), channel_id=1, source_target_pairs={{0,4},{1,5},{2,6},{3,7},{4,8},{5,9},{6,10},{7,11},{8,12},{9,13},{1... | collective-permute-start | bytes 786440 | tf_op jit(solution)/shard_map/ppermute | solution.py:345
  120.2 2.7 %collective-permute-start.17 = (bf16[512,1024]{1,0:T(8,128)(2,1)S(1)}, bf16[512,1024]{1,0:T(8,128)(2,1)S(1)}, u32[]{:S(2)}, u32[]{:S(2)}) collective-permute-start(bf16[512,1024]{1,0:T(8,128)(2,1)S(1)} %outer.4), channel_id=1, source_target_pairs={{0,1},{1,0},{2,3},{3,2},{4,5},{5,4},{6,7},{7,6},{8,9},{9,8},{10,11... | collective-permute-start | bytes 3145736 | tf_op jit(solution)/shard_map/ppermute | solution.py:329
  130.9 5.2 %collective-permute-start.18 = (bf16[512,1024]{1,0:T(8,128)(2,1)S(1)}, bf16[512,1024]{1,0:T(8,128)(2,1)S(1)}, u32[]{:S(2)}, u32[]{:S(2)}) collective-permute-start(bf16[512,1024]{1,0:T(8,128)(2,1)S(1)} %outer.6), channel_id=1, source_target_pairs={{0,1},{1,0},{2,3},{3,2},{4,5},{5,4},{6,7},{7,6},{8,9},{9,8},{10,11... | collective-permute-start | bytes 3145736 | tf_op jit(solution)/shard_map/ppermute | solution.py:329
  131.1 40.2 %collective-permute-start.25 = (bf16[256,1024]{1,0:T(8,128)(2,1)S(1)}, bf16[256,1024]{1,0:T(8,128)(2,1)S(1)}, u32[]{:S(2)}, u32[]{:S(2)}) collective-permute-start(bf16[256,1024]{1,0:T(8,128)(2,1)S(1)} %slice.19), channel_id=1, source_target_pairs={{0,28},{4,24},{8,20},{12,16},{16,12},{20,8},{24,4},{28,0},{1,29},{... | collective-permute-start | bytes 1572872 | tf_op jit(solution)/shard_map/ppermute | solution.py:335
  131.9 15.0 %collective-permute-start.20 = (bf16[1024,128]{1,0:T(8,128)(2,1)S(1)}, bf16[1024,128]{1,0:T(8,128)(2,1)S(1)}, u32[]{:S(2)}, u32[]{:S(2)}) collective-permute-start(bf16[1024,128]{1,0:T(8,128)(2,1)S(1)} %get-tuple-element.93), channel_id=1, source_target_pairs={{0,2},{1,3},{2,0},{3,1},{4,6},{5,7},{6,4},{7,5},{8,10},{9,11},{10,... | collective-permute-start | bytes 786440 | tf_op jit(solution)/shard_map/ppermute | solution.py:329
  132.4 13.4 %collective-permute-start.19 = (bf16[1024,128]{1,0:T(8,128)(2,1)S(1)}, bf16[1024,128]{1,0:T(8,128)(2,1)S(1)}, u32[]{:S(2)}, u32[]{:S(2)}) collective-permute-start(bf16[1024,128]{1,0:T(8,128)(2,1)S(1)} %get-tuple-element.90), channel_id=1, source_target_pairs={{0,2},{1,3},{2,0},{3,1},{4,6},{5,7},{6,4},{7,5},{8,10},{9,11},{10,... | collective-permute-start | bytes 786440 | tf_op jit(solution)/shard_map/ppermute | solution.py:329
  149.5 30.8 %collective-permute-start.22 = (bf16[2,256,256]{2,1,0:T(8,128)(2,1)S(1)}, bf16[2,256,256]{2,1,0:T(8,128)(2,1)S(1)}, u32[]{:S(2)}, u32[]{:S(2)}) collective-permute-start(bf16[2,256,256]{2,1,0:T(8,128)(2,1)S(1)} %get-tuple-element.107), channel_id=1, source_target_pairs={{0,2},{1,3},{2,0},{3,1},{4,6},{5,7},{6,4},{7,5},{8,10},{9,11},{10,... | collective-permute-start | bytes 786440 | tf_op jit(solution)/shard_map/ppermute | solution.py:329
  150.1 30.2 %collective-permute-start.23 = (bf16[2,256,256]{2,1,0:T(8,128)(2,1)S(1)}, bf16[2,256,256]{2,1,0:T(8,128)(2,1)S(1)}, u32[]{:S(2)}, u32[]{:S(2)}) collective-permute-start(bf16[2,256,256]{2,1,0:T(8,128)(2,1)S(1)} %get-tuple-element.108), channel_id=1, source_target_pairs={{0,3},{1,2},{2,1},{3,0},{4,7},{5,6},{6,5},{7,4},{8,11},{9,10},{10,... | collective-permute-start | bytes 786440 | tf_op jit(solution)/shard_map/ppermute | solution.py:329
  150.2 30.1 %collective-permute-start.21 = (bf16[2,256,256]{2,1,0:T(8,128)(2,1)S(1)}, bf16[2,256,256]{2,1,0:T(8,128)(2,1)S(1)}, u32[]{:S(2)}, u32[]{:S(2)}) collective-permute-start(bf16[2,256,256]{2,1,0:T(8,128)(2,1)S(1)} %get-tuple-element.99), channel_id=1, source_target_pairs={{0,1},{1,0},{2,3},{3,2},{4,5},{5,4},{6,7},{7,6},{8,9},{9,8},{10,11... | collective-permute-start | bytes 786440 | tf_op jit(solution)/shard_map/ppermute | solution.py:329
  171.4 15.9 %collective-permute-start.26 = (bf16[256,1024]{1,0:T(8,128)(2,1)S(1)}, bf16[256,1024]{1,0:T(8,128)(2,1)S(1)}, u32[]{:S(2)}, u32[]{:S(2)}) collective-permute-start(bf16[256,1024]{1,0:T(8,128)(2,1)S(1)} %slice.16), channel_id=1, source_target_pairs={{0,28},{4,24},{8,20},{12,16},{16,12},{20,8},{24,4},{28,0},{1,29},{... | collective-permute-start | bytes 1572872 | tf_op jit(solution)/shard_map/ppermute | solution.py:335
  180.5 5.9 %collective-permute-start.24 = (bf16[256,256]{1,0:T(8,128)(2,1)S(1)}, bf16[256,256]{1,0:T(8,128)(2,1)S(1)}, u32[]{:S(2)}, u32[]{:S(2)}) collective-permute-start(bf16[256,256]{1,0:T(8,128)(2,1)S(1)} %fusion.4), channel_id=1, source_target_pairs={{0,28},{4,24},{8,20},{12,16},{16,12},{20,8},{24,4},{28,0},{1,29},{... | collective-permute-start | bytes 393224 | tf_op jit(solution)/shard_map/ppermute | solution.py:335
  (38 other events, 324.9 us)

commit v2 on v1

--- a/solution.py
+++ b/solution.py
@@ -23,10 +23,6 @@
     return lax.dot_general(a, b, (((ca,), (cb,)), ((), ())), preferred_element_type=F32)
 
 
-def after(x, *others):
-    return lax.optimization_barrier((x, *others))[0]
-
-
 def piece(array, *lead):
     rest = array.shape[len(lead) :]
     return array, pl.BlockSpec((None,) * len(lead) + rest, lambda i, *s: lead + (0,) * len(rest))
@@ -36,7 +32,13 @@
     return pl.BlockSpec(shape, lambda i, *s: (0,) * len(shape))
 
 
-def call(kernel, name, scalars, operands, shapes, flops, size, steps=1, outs=None, scratch=(), aliases=None):
+def call(kernel, name, scalars, operands, shapes, steps=1, outs=None, scratch=(), aliases=None, deps=()):
+    count = len(scalars) + len(operands)
+
+    def body(*refs):
+        kernel(*refs[:count], *refs[count + len(deps) :])
+
+    operands = list(operands) + [(a, pl.BlockSpec(memory_space=pl.ANY)) for a in deps]
     arrays, specs = zip(*operands)
     grid = pltpu.PrefetchScalarGridSpec(
         num_scalar_prefetch=len(scalars),
@@ -47,7 +49,7 @@
     )
     aliases = {len(scalars) + i: o for i, o in (aliases or {}).items()}
     return pl.pallas_call(
-        kernel,
+        body,
         grid_spec=grid,
         out_shape=shapes,
         input_output_aliases=aliases,
@@ -70,28 +72,47 @@
     return ref[:, pl.ds(pl.multiple_of(start, HEAD), size)]
 
 
+def hold_kernel(x, out):
+    pass
+
+
+def hold(x, deps):
+    anywhere = pl.BlockSpec(memory_space=pl.ANY)
+    shape = [sds(x.shape, x.dtype)]
+    return call(hold_kernel, "hold", [], [(x, anywhere)], shape, outs=[anywhere], aliases={0: 0}, deps=deps)[0]
+
+
+def cast_kernel(x, out):
+    out[...] = x[...].astype(BF)
+
+
+def lowered(i, rows, x, deps=()):
+    d = x.shape[2]
+    block = pl.BlockSpec((None, rows, d), lambda _: (0, i, 0))
+    return call(cast_kernel, "lowered", [], [(x, block)], [sds((rows, d))], deps=deps)[0]
+
+
 def value_kernel(lanes, meta, x, *refs):
-    parts, (full, out) = refs[:lanes], refs[lanes:]
-    rows = parts[0].shape[1]
+    parts, (full, out) = refs[:-2], refs[-2:]
+    rows = parts[0].shape[0]
     for r in range(2):
         for k in range(lanes):
             at = jnp.bitwise_xor(meta[3], k) * rows
-            full[r, pl.ds(pl.multiple_of(at, rows), rows), :] = parts[k][r]
+            full[r, pl.ds(pl.multiple_of(at, rows), rows), :] = parts[r * lanes + k][...]
         for t in range(x.shape[1]):
             out[r, t] = mm(x[r, t, 0], full[r], 1, 0).astype(BF)
 
 
-def values_of(meta, inputs, parts):
+def values_of(meta, inputs, parts, deps=()):
     ticks, tok, d = inputs.shape[1], inputs.shape[3], inputs.shape[4]
-    kvw = parts[0].shape[2]
-    return call(
-        functools.partial(value_kernel, len(parts)),
+    kvw = parts[0].shape[1]
+    return call(
+        functools.partial(value_kernel, len(parts) // 2),
         "values",
         [meta],
         [piece(inputs)] + [piece(p) for p in parts],
         [sds((2, d, kvw)), sds((2, ticks, tok, kvw))],
-        4 * ticks * tok * d * kvw,
-        4 << 20,
+        deps=deps,
     )
 
 
@@ -123,7 +144,7 @@
             out[:, i * HEAD : (i + 1) * HEAD] = mm(p[:, i * tok : (i + 1) * tok], val, 0, 0).astype(BF)
 
 
-def front(r, per, heads, sections, meta, bounds, queries, keys, values):
+def front(r, per, heads, sections, meta, bounds, queries, keys, values, deps=()):
     ticks, tok = queries.shape[1], queries.shape[3]
     width = heads * HEAD
     operands = [
@@ -143,10 +164,9 @@
         [meta, bounds],
         operands,
         shapes,
-        2 * ticks * 2 * heads * 2 * tok * tok * HEAD * 4,
-        8 << 20,
         ticks,
         outs,
+        deps=deps,
     )
 
 
@@ -166,8 +186,8 @@
                 refs[s - 2][at : at + tok, :] = ga[s * tok : (s + 1) * tok, j * HEAD : (j + 1) * HEAD]
 
 
-def ahead(r, t, per, meta, own, par, weights):
-    tok, d = own[0][0].shape[-2:]
+def ahead(r, t, per, meta, own, par, weights, deps=()):
+    tok, d = own[0][1].block_shape[-2:]
     shape = (len(weights) * per * tok, HEAD)
     return call(
         functools.partial(ahead_kernel, r, t, len(weights), per),
@@ -175,32 +195,34 @@
         [meta],
         own + par + [piece(w) for w in weights],
         [sds(shape)] * 2,
-        4 * d * shape[0] * HEAD * 2,
-        4 << 20,
+        deps=deps,
     )
 
 
 def middle_kernel(r, t, meta, *refs):
     own = refs[: t + 1]
-    probs, mine, came, w, gv_out, gi_out = refs[t + 1 :]
+    probs, mine, came, w, gv_out, gi_out, *joined = refs[t + 1 :]
     h = meta[0] == 0
     a = mm(probs[0], mine[...], 1, 0).astype(BF)
     b = mm(probs[1], came[...], 1, 0).astype(BF)
     gv = jnp.concatenate([jnp.where(h, a, b), jnp.where(h, b, a)], axis=1)
     gv_out[...] = gv
-    gi_out[...] = (chosen(meta, r, own).astype(F32) + mm(gv, w[...], 1, 1)).astype(BF)
-
-
-def middle(r, t, meta, own, probs, mine, came, w_value):
-    tok, d = own[0][0].shape[-2:]
+    gi = (chosen(meta, r, own).astype(F32) + mm(gv, w[...], 1, 1)).astype(BF)
+    gi_out[...] = gi
+    if joined:
+        joined[0][:, : gi.shape[1]] = gi
+        joined[0][:, gi.shape[1] :] = gv
+
+
+def middle(r, t, meta, own, probs, mine, came, w_value, joined, deps=()):
+    tok, d = own[0][1].block_shape[-2:]
     return call(
         functools.partial(middle_kernel, r, t),
         "middle",
         [meta],
         own + [piece(probs, t), piece(mine), piece(came), piece(w_value, r)],
-        [sds((tok, 2 * HEAD)), sds((tok, d))],
-        4 * tok * d * 2 * HEAD,
-        2 << 20,
+        [sds((tok, 2 * HEAD)), sds((tok, d))] + [sds((tok, d + 2 * HEAD))] * joined,
+        deps=deps,
     )
 
 
@@ -225,7 +247,7 @@
             gk.at[t, 0][:, pl.ds(pl.multiple_of(half * HEAD, HEAD), HEAD)] = out
 
 
-def back(r, per, heads, meta, queries, keys, values, probs, gas, filled=()):
+def back(r, per, heads, meta, queries, keys, values, probs, gas, filled=(), deps=()):
     arrays = (queries, keys)
     specs = [pl.BlockSpec((None,) + a.shape[1:], lambda i, m: (r, 0, 0, 0, 0)) for a in arrays]
     operands = list(zip(arrays, specs)) + [piece(values, r), piece(probs)] + [piece(a) for a in gas]
@@ -237,10 +259,9 @@
         [meta],
         operands,
         [sds(a.shape) for a in arrays],
-        2 * 2 * 2 * heads * 3 * queries.shape[3] ** 2 * HEAD * 4,
-        8 << 20,
         outs=specs,
         aliases={first: 0, first + 1: 1} if filled else {},
+        deps=deps,
     )
 
 
@@ -253,9 +274,9 @@
     out[...] = total.astype(out.dtype)
 
 
-def outer(r, k, rows, meta, mine, came, gs, dtype):
+def outer(r, k, rows, meta, mine, came, gs, dtype, deps=()):
     ticks, tok = mine.shape[0], mine.shape[1]
-    d = gs[0][0].shape[-1]
+    d = gs[0][1].block_shape[-1]
     step = min(rows, 256)
     first = k * (rows // step)
     block = pl.BlockSpec((ticks, tok, step), lambda i, m: (0, 0, first + i))
@@ -266,11 +287,34 @@
         [meta],
         [(mine, block), (came, block)] + gs,
         [sds((rows, d), dtype)],
-        4 * ticks * tok * rows * d,
-        4 << 20,
         rows // step,
         outs,
+        deps=deps,
     )[0]
+
+
+def update_kernel(lanes, meta, own, back, moment, weight, moment_out, weight_out):
+    grad = (own[...] + back[...].astype(F32)) / lanes
+    new = decay_rate * moment[...] + grad
+    moment_out[...] = new
+    weight_out[...] = weight[...] - learn_rate * new
+
+
+def update(lanes, meta, own, back, moment, weight, deps=()):
+    rows, d = own.shape
+    step = min(rows, 128)
+    flat = pl.BlockSpec((step, d), lambda i, m: (i, 0))
+    deep = pl.BlockSpec((None, step, d), lambda i, m: (0, i, 0))
+    return call(
+        functools.partial(update_kernel, lanes),
+        "update",
+        [meta],
+        [(own, flat), (back, flat), (moment, deep), (weight, deep)],
+        [sds(moment.shape, F32)] * 2,
+        rows // step,
+        [deep, deep],
+        deps=deps,
+    )
 
 
 def value_grad_kernel(meta, x, gv00, gv01, gv10, gv11, own, *refs):
@@ -283,7 +327,7 @@
             out[r] = total[pl.ds(pl.multiple_of(at, rows), rows), :].astype(out.dtype)
 
 
-def value_grads(meta, lanes, inputs, gvs):
+def value_grads(meta, lanes, inputs, gvs, deps=()):
     d = inputs.shape[4]
     kvw = KV_HEADS * HEAD
     rows = d // lanes
@@ -294,9 +338,8 @@
         [meta],
         [piece(a) for a in (inputs, *gvs)],
         shapes,
-        4 * 2 * inputs.shape[3] * d * kvw,
-        4 << 20,
         scratch=[pltpu.VMEM((d, kvw), F32)],
+        deps=deps,
     )
 
 
@@ -348,98 +391,112 @@
         pairs = [(i * lanes + j, i * lanes + (j ^ half)) for i in (0, sections - 1) for j in range(lanes)]
         return lax.ppermute(x, ("section", "lane"), pairs)
 
+    def spread(x, count):
+        return [x] + [at_lane(x, k) for k in range(1, count)]
+
+    def summed(away, total):
+        for k, part in enumerate(away):
+            if part.shape[0] == rows:
+                step = part.shape[0] // 4
+                pieces = [at_lane(part[i : i + step], k + 1) for i in range(0, part.shape[0], step)]
+                part = jnp.concatenate(pieces, axis=0)
+            else:
+                part = at_lane(part, k + 1)
+            total = total + part.astype(F32)
+        return total
+
     own_value = value_weight[0].astype(BF)
     mirror_value = mirrored(own_value)
-    own_out = [after(out_weight, own_value)[0].astype(BF)]
-    mirror_out = [mirrored(after(own_out[0], mirror_value))]
-
-    def with_mates(pieces):
-        spread = [[p] + [at_lane(p, k) for k in range(1, half)] for p in pieces]
-        return [s[k] for k in range(half) for s in spread]
+    own_out = lowered(0, rows, out_weight)
+    mirror_out = mirrored(hold(own_out, [mirror_value]))
+    parts_value = spread(own_value, lanes) + spread(mirror_value, lanes)
+    cut = rows // 4
+
+    def with_mates(x):
+        pieces = [x[i : i + cut] for i in range(0, rows, cut)]
+        table = [spread(p, half) for p in pieces]
+        if cut % HEAD:
+            return [jnp.concatenate([row[k] for row in table], axis=0) for k in range(half)]
+        return [row[k] for k in range(half) for row in table]
 
     parts_out = [with_mates(own_out)]
-    g_par = partner(after(grad_now, mirror_value)[:, 0])
     fresh_par = at_ends(lax.dynamic_index_in_dim(grad_new, jnp.where(place == 0, 1, 0), keepdims=False))
+    g_par = partner(grad_now[:, 0])
     bounds = jnp.concatenate([bound_now.reshape(-1), bound_new.reshape(-1)])
 
     own, par = {}, {}
+    ga, gv, gi = {}, {}, {}
+    probs, mine, came = [None] * 2, [None] * 2, [None] * 2
     for r in range(2):
         own[r, 0], par[r, 0] = [piece(grad_now, r, 0)], [piece(g_par, r)]
-    ga, gv, gi = {}, {}, {}
-    probs, mine, came = [None] * 2, [None] * 2, [None] * 2
-
-    def run_ahead(r, t, *deps):
-        weights = list(after(tuple(parts_out[r]), *deps)) if deps else parts_out[r]
-        here, send = ahead(r, t, per, meta, own[r, t], par[r, t], weights)
-        ga[r, t] = (here, partner(send))
-
-    def run_front(r, v):
-        probs[r], mine[r], send = front(r, per, heads, sections, meta, bounds, queries_saved, keys_saved, v)
-        came[r] = partner(send)
-
-    def run_middle(r, t, *deps):
-        p = after(probs[r], *deps) if deps else probs[r]
-        gv[r, t], gi[r, t] = middle(r, t, meta, own[r, t], p, *ga[r, t], w_value)
-
-    def run_relay(r, *deps):
-        sent = after(gi[r, 0], *deps) if deps else gi[r, 0]
-        own[r, 1] = [piece(relayed(sent, r)), piece(grad_new, r)]
-        par[r, 1] = [piece(relayed(sent, r, half)), piece(fresh_par)]
-
-    def run_outer(r, *deps):
-        m = after(mine[r], *deps) if deps else mine[r]
+
+    def run_front(r, deps=()):
+        probs[r], mine[r], send = front(
+            r, per, heads, sections, meta, bounds, queries_saved, keys_saved, values, deps
+        )
+        came[r] = jnp.stack([partner(send[t]) for t in range(2)])
+
+    def run_ahead(r, t, deps=()):
+        here, send = ahead(r, t, heads // len(parts_out[r]), meta, own[r, t], par[r, t], parts_out[r], deps)
+        if (r, t) == (1, 1):
+            step = send.shape[0] // 2
+            ga[r, t] = (here, jnp.concatenate([partner(send[:step]), partner(send[step:])], axis=0))
+        else:
+            ga[r, t] = (here, partner(send))
+
+    def run_middle(r, t, deps=()):
+        gv[r, t], gi[r, t], *joined = middle(
+            r, t, meta, own[r, t], probs[r], *ga[r, t], w_value, 0, deps
+        )
+        return joined
+
+    def run_relay(r):
+        own[r, 1] = [piece(relayed(gi[r, 0], r)), piece(grad_new, r)]
+        par[r, 1] = [piece(relayed(gi[r, 0], r, half)), piece(fresh_par)]
+
+    def run_outer(r, deps=()):
         gs = own[r, 0] + par[r, 0] + own[r, 1] + par[r, 1]
-        away = [outer(r, k, rows, meta, m, came[r], gs, BF) for k in range(1, half)]
-        total = outer(r, 0, rows, meta, after(m, *away) if away else m, came[r], gs, F32)
-        for k, part in enumerate(away):
-            total = total + at_lane(part, k + 1).astype(F32)
-        return total
-
-    both_value = jnp.stack([own_value, mirror_value])
-    parts_value = [both_value] + [at_lane(both_value, k) for k in range(1, lanes)]
+        away = [outer(r, k, rows, meta, mine[r], came[r], gs, BF, deps) for k in range(1, half)]
+        total = outer(r, 0, rows, meta, mine[r], came[r], gs, F32, [*deps, *away])
+        return summed(away, total)
+
     run_ahead(0, 0)
-    w_value, values = values_of(meta, inputs_saved, parts_value)
-    run_front(0, values)
-    run_middle(0, 0)
-    run_front(1, after(values, gi[0, 0]))
-    parts_out.append(with_mates(after(tuple(mirror_out), probs[1], came[0], came[1])))
+    w_value, values = values_of(meta, inputs_saved, parts_value, [ga[0, 0][0], fresh_par])
+    run_front(0)
+    run_front(1, [probs[0]])
+    run_middle(0, 0, [probs[1]])
+    mirror_out = hold(mirror_out, [came[0], came[1], gi[0, 0]])
+    parts_out.append(with_mates(mirror_out))
     run_ahead(1, 0)
     run_middle(1, 0)
     run_relay(1)
-    run_relay(0, gi[1, 0])
+    gi[0, 0] = hold(gi[0, 0], [gi[1, 0]])
+    run_relay(0)
     relays = [own[0, 1][0][0], par[0, 1][0][0]]
-    total1 = run_outer(1, *relays)
-    cut = rows // 2
+    total1 = run_outer(1, relays)
     send_out = total1.astype(BF)
-    back_first = mirrored(send_out[:cut])
-    run_ahead(0, 1, send_out)
-    run_ahead(1, 1, ga[0, 1][0])
-    total0 = run_outer(0, ga[1, 1][0])
-    sums_out = [total0, total1]
-    run_middle(0, 1, total0)
-    run_middle(1, 1, gi[0, 1])
-    back_second = mirrored(after(send_out, back_first, gi[1, 1])[cut:])
-    gas = [[*ga[r, 0], *ga[r, 1]] for r in range(2)]
-    out = back(0, per, heads, meta, queries_saved, keys_saved, values, after(probs[0], gi[1, 1]), gas[0])
+    back_out = mirrored(send_out)
+    run_ahead(1, 1, [send_out])
+    run_ahead(0, 1, [ga[1, 1][0]])
+    run_middle(1, 1, [ga[0, 1][0]])
+    run_middle(0, 1, [gi[1, 1]])
     gvs = [gv[r, t] for r in range(2) for t in range(2)]
     total, *sent = value_grads(meta, lanes, inputs_saved, gvs)
-    for k, part in enumerate(sent):
-        total = total + at_lane(part, k + 1).astype(F32)
-    sums_value = [total[0], total[1]]
+    gas = [[*ga[r, 0], *ga[r, 1]] for r in range(2)]
+    total0 = run_outer(0, [total])
+    out = back(1, per, heads, meta, queries_saved, keys_saved, values, probs[1], gas[1], deps=[total0])
+    total = [summed([part[r] for part in sent], total[r]) for r in range(2)]
     back_value = mirrored(total[1].astype(BF))
     grad_queries, grad_keys = back(
-        1, per, heads, meta, queries_saved, keys_saved, values, after(probs[1], sent[0]), gas[1], out
+        0, per, heads, meta, queries_saved, keys_saved, values, probs[0], gas[0], out
     )
     grad_inputs = jnp.stack([jnp.stack([gi[r, t] for t in range(2)]) for r in range(2)])[:, :, None]
-    back_out = jnp.concatenate([back_first, back_second], axis=0)
-    back_out = after(back_out, grad_queries)
-    mean_value = (sums_value[0] + back_value.astype(F32)) / lanes
-    mean_out = (sums_out[0] + back_out.astype(F32)) / lanes
+    out_moment_new, out_weight_new = update(
+        lanes, meta, total0, back_out, out_moment, out_weight, [grad_keys]
+    )
+    mean_value = (total[0] + back_value.astype(F32)) / lanes
     value_moment_new = decay_rate * value_moment + mean_value[None]
-    out_moment_new = decay_rate * out_moment + mean_out[None]
     value_weight_new = value_weight - learn_rate * value_moment_new
-    out_weight_new = out_weight - learn_rate * out_moment_new
-
     return (
         grad_inputs,
         grad_queries,

time: 192 us -> 177 us (0.922)
  waiting for transfers between devices: 92 us -> 75.8 us
  starting transfers between devices: 33.2 us -> 43 us
  other arithmetic: 11 us -> 4.74 us
  Pallas kernels: 44.7 us -> 41.2 us
  local copies, waits for them, and re-layouts: 8.08 us -> 10.2 us
    ppermute x17 -> x38, starting transfers between devices: 12 us -> 23.1 us  [at_lane(): return lax.ppermute(x, 'lane', [(i, i ^ k) for i in range(lanes)])]
    ppermute x5 -> x4, waiting for transfers between devices: 31.7 us -> 21.9 us  [mirrored(): lax.ppermute(x, 'section', [(i, sections - 1 - i) for i in range(sections)])]
    ppermute x17 -> x38, waiting for transfers between devices: 46.6 us -> 39.4 us  [at_lane(): return lax.ppermute(x, 'lane', [(i, i ^ k) for i in range(lanes)])]
    pallas_call x18 -> x23, Pallas kernels: 44.7 us -> 41.2 us  [call(): pl.pallas_call(body, grid_spec=grid, out_shape=shapes, input_output_alias...]
    sub x1 -> x0, other arithmetic: 2.84 us -> none  [shards(): out_weight_new = out_weight - learn_rate * out_moment_new]
    convert_element_type x1, other arithmetic: 2.73 us -> 0.07 us  [shards(): back_value = mirrored(total[1].astype(BF))]
    slice x2 -> x5, local copies, waits for them, and re-layouts: 0.07 us -> 2.34 us  [the longest x2 2.16 us: with_mates(): pieces = [x[i:i + cut] for i in range(0, rows, cut)]]
    ppermute x5 -> x4, starting transfers between devices: 6.93 us -> 5.49 us  [mirrored(): lax.ppermute(x, 'section', [(i, sections - 1 - i) for i in range(sections)])]
  transfers between devices with their start and end apart: 27 -> 47, of which waited for: 15 -> 20; matrix products, arithmetic and copies ran while one was open for 3% -> 3% of each run, Pallas kernels for 16% -> 18%
where the time goes in v2:
time: 177 us; the launch traced here: 176 us
  waiting for transfers between devices  75.8 us (43%)
  starting transfers between devices  43 us (24%)
  Pallas kernels  41.2 us (23%)
  local copies, waits for them, and re-layouts  10.2 us (6%)
  other arithmetic  4.74 us (3%)
    pallas_call x23, Pallas kernels, call(): pl.pallas_call(body, grid_spec=grid, out_shape=shapes, input_output_alias...  41.2 us
    ppermute x38, waiting for transfers between devices, at_lane(): return lax.ppermute(x, 'lane', [(i, i ^ k) for i in range(lanes)])  39.4 us
    ppermute x38, starting transfers between devices, at_lane(): return lax.ppermute(x, 'lane', [(i, i ^ k) for i in range(lanes)])  23.1 us
    ppermute x4, waiting for transfers between devices, mirrored(): lax.ppermute(x, 'section', [(i, sections - 1 - i) for i in range(sections)])  21.9 us
    ppermute x4, waiting for transfers between devices, relayed(): return lax.ppermute(x, ('section', 'lane'), pairs)  14.5 us
    ppermute x4, starting transfers between devices, relayed(): return lax.ppermute(x, ('section', 'lane'), pairs)  13.7 us
    unnamed x46, local copies, waits for them, and re-layouts  6.85 us
    ppermute x4, starting transfers between devices, mirrored(): lax.ppermute(x, 'section', [(i, sections - 1 - i) for i in range(sections)])  5.49 us
  transfers between devices with their start and end apart: 47, of which 20 were waited for; matrix products, arithmetic and copies ran while one was open for 3% of the time, Pallas kernels for 18%

profile of v2, /device:TPU:10, one launch (start us, length us, event | category | flops | bytes accessed | tf_op | source)
XLA Modules:
  0.0 176.1 jit_solution(5779883239940290231)
XLA Ops:
  19.1 4.1 %collective-permute-done.7.refs_2_.refs_4_ = bf16[2,128,1024]{2,1,0:T(8,128)(2,1)S(1)} collective-permute-done((bf16[2,128,1024]{2,1,0:T(8,128)(2,1)}, bf16[2,128,1024]{2,1,0:T(8,128)(2,1)S(1)}, u32[]{:S(2)}, u32[]{:S(2)}) %collective-permute-start.7) | collective-permute-done | bytes 524320 | tf_op jit(solution)/shard_map/ppermute | solution.py:372
  25.7 3.0 %ahead.4 = (bf16[1024,128]{1,0:T(8,128)(2,1)S(1)}, bf16[1024,128]{1,0:T(8,128)(2,1)S(1)}) custom-call(s32[6]{0:T(128)S(1)} %stack.80.refs_0_, bf16[2,1,128,1024]{3,2,1,0:T(8,128)(2,1)S(1)} %copy-done.1, bf16[2,128,1024]{2,1,0:T(8,128)(2,1)S(1)} %collective-permute-done.7.refs_2_.refs_4_, bf16[128,1024]{1,0:T(8,128)(2,1)} %get-tuple-element.99.refs_3_.refs_5_, ...), custom_call_target="tpu_custom_call" | custom-call | flops 1 | bytes 1 | tf_op jit(solution)/shard_map/ahead/pallas_call | solution.py:51
  28.8 1.7 collective-permute-start.13
  30.5 2.1 %values.1 = (bf16[2,1024,256]{2,1,0:T(8,128)(2,1)S(1)}, bf16[2,2,128,256]{3,2,1,0:T(8,128)(2,1)S(1)}) custom-call(s32[6]{0:T(128)S(1)} %stack.80.refs_0_, bf16[2,2,1,128,1024]{4,3,2,1,0:T(8,128)(2,1)S(1)} %copy-done.6, bf16[256,256]{1,0:T(8,128)(2,1)S(1)} %convert_bitcast_fusion.refs_2_, bf16[256,256]{1,0:T(8,128)(2,1)S(1)} %copy-done.17, ...), custom_call_target="tpu_custom_call" | custom-call | flops 1 | bytes 1 | tf_op jit(solution)/shard_map/values/pallas_call | solution.py:51
  32.6 2.7 %front.2 = (bf16[2,2,128,1024]{3,2,1,0:T(8,128)(2,1)S(1)}, bf16[2,128,1024]{2,1,0:T(8,128)(2,1)S(1)}, bf16[2,128,1024]{2,1,0:T(8,128)(2,1)S(1)}) custom-call(s32[6]{0:T(128)S(1)} %stack.80.refs_0_, s32[18]{0:T(128)S(1)} %pad_add_fusion.refs_1_, bf16[2,2,1,128,2048]{4,3,2,1,0:T(8,128)(2,1)S(1)} %copy-done.2, bf16[2,2,1,128,256]{4,3,2,1,0:T(8,128)(2,1)S(1)} %copy-done.5, ...), custom_call_target="tpu_custom_call" | custom-call | flops 1 | bytes 1 | tf_op jit(solution)/shard_map/front/pallas_call | solution.py:51
  37.4 2.7 %front.3 = (bf16[2,2,128,1024]{3,2,1,0:T(8,128)(2,1)S(1)}, bf16[2,128,1024]{2,1,0:T(8,128)(2,1)S(1)}, bf16[2,128,1024]{2,1,0:T(8,128)(2,1)S(1)}) custom-call(s32[6]{0:T(128)S(1)} %stack.80.refs_0_, s32[18]{0:T(128)S(1)} %pad_add_fusion.refs_1_, bf16[2,2,1,128,2048]{4,3,2,1,0:T(8,128)(2,1)S(1)} %copy-done.2, bf16[2,2,1,128,256]{4,3,2,1,0:T(8,128)(2,1)S(1)} %copy-done.5, ...), custom_call_target="tpu_custom_call" | custom-call | flops 1 | bytes 1 | tf_op jit(solution)/shard_map/front/pallas_call | solution.py:51
  44.6 5.6 %collective-permute-done.16 = bf16[128,1024]{1,0:T(8,128)(2,1)S(1)} collective-permute-done((bf16[128,1024]{1,0:T(8,128)(2,1)S(1)}, bf16[128,1024]{1,0:T(8,128)(2,1)S(1)}, u32[]{:S(2)}, u32[]{:S(2)}) %collective-permute-start.16) | collective-permute-done | bytes 262176 | tf_op jit(solution)/shard_map/ppermute | solution.py:372
  50.3 5.6 %collective-permute-done.17 = bf16[128,1024]{1,0:T(8,128)(2,1)S(1)} collective-permute-done((bf16[128,1024]{1,0:T(8,128)(2,1)S(1)}, bf16[128,1024]{1,0:T(8,128)(2,1)S(1)}, u32[]{:S(2)}, u32[]{:S(2)}) %collective-permute-start.17) | collective-permute-done | bytes 262176 | tf_op jit(solution)/shard_map/ppermute | solution.py:372
  55.9 4.3 %collective-permute-done.18 = bf16[128,1024]{1,0:T(8,128)(2,1)S(1)} collective-permute-done((bf16[128,1024]{1,0:T(8,128)(2,1)S(1)}, bf16[128,1024]{1,0:T(8,128)(2,1)S(1)}, u32[]{:S(2)}, u32[]{:S(2)}) %collective-permute-start.18) | collective-permute-done | bytes 262176 | tf_op jit(solution)/shard_map/ppermute | solution.py:372
  60.2 4.2 %collective-permute-done.14.refs_0_ = bf16[512,1024]{1,0:T(8,128)(2,1)} collective-permute-done((bf16[512,1024]{1,0:T(8,128)(2,1)S(1)}, bf16[512,1024]{1,0:T(8,128)(2,1)}, u32[]{:S(2)}, u32[]{:S(2)}) %collective-permute-start.14) | collective-permute-done | bytes 1048608 | tf_op jit(solution)/shard_map/ppermute | solution.py:378
  68.4 1.8 %ahead.5 = (bf16[1024,128]{1,0:T(8,128)(2,1)S(1)}, bf16[1024,128]{1,0:T(8,128)(2,1)S(1)}) custom-call(s32[6]{0:T(128)S(1)} %stack.80.refs_0_, bf16[2,1,128,1024]{3,2,1,0:T(8,128)(2,1)S(1)} %copy-done.1, bf16[2,128,1024]{2,1,0:T(8,128)(2,1)S(1)} %collective-permute-done.7.refs_2_.refs_4_, bf16[128,1024]{1,0:T(8,128)(2,1)S(1)} %get-tuple-element.95.refs_3_.refs_5_, ...), custom_call_target="tpu_custom_call" | custom-call | flops 1 | bytes 1 | tf_op jit(solution)/shard_map/ahead/pallas_call | solution.py:51
  71.9 6.8 %collective-permute-done.23.refs_4_.refs_6_ = bf16[1024,128]{1,0:T(8,128)(2,1)S(1)} collective-permute-done((bf16[1024,128]{1,0:T(8,128)(2,1)S(1)}, bf16[1024,128]{1,0:T(8,128)(2,1)S(1)}, u32[]{:S(2)}, u32[]{:S(2)}) %collective-permute-start.23) | collective-permute-done | bytes 262176 | tf_op jit(solution)/shard_map/ppermute | solution.py:372
  79.7 4.4 %collective-permute-start.25 = (bf16[128,1024]{1,0:T(8,128)(2,1)S(1)}, bf16[128,1024]{1,0:T(8,128)(2,1)S(1)}, u32[]{:S(2)}, u32[]{:S(2)}) collective-permute-start(bf16[128,1024]{1,0:T(8,128)(2,1)S(1)} %hold.5), channel_id=1, source_target_pairs={{4,2},{5,3},{6,0},{7,1},{8,6},{9,7},{10,4},{11,5},{12,10},{13,11},... | collective-permute-start | bytes 786440 | tf_op jit(solution)/shard_map/ppermute | solution.py:388
  84.1 1.9 %collective-permute-start.24 = (bf16[128,1024]{1,0:T(8,128)(2,1)S(1)}, bf16[128,1024]{1,0:T(8,128)(2,1)S(1)}, u32[]{:S(2)}, u32[]{:S(2)}) collective-permute-start(bf16[128,1024]{1,0:T(8,128)(2,1)S(1)} %hold.5), channel_id=1, source_target_pairs={{4,0},{5,1},{6,2},{7,3},{8,4},{9,5},{10,6},{11,7},{12,8},{13,9},{1... | collective-permute-start | bytes 786440 | tf_op jit(solution)/shard_map/ppermute | solution.py:388
  86.0 4.7 %collective-permute-start.27 = (bf16[128,1024]{1,0:T(8,128)(2,1)S(1)}, bf16[128,1024]{1,0:T(8,128)(2,1)S(1)}, u32[]{:S(2)}, u32[]{:S(2)}) collective-permute-start(bf16[128,1024]{1,0:T(8,128)(2,1)S(1)} %get-tuple-element.52.refs_1_), channel_id=1, source_target_pairs={{0,6},{1,7},{2,4},{3,5},{4,10},{5,11},{6,8},{7,9},{8,14},{9,15},{1... | collective-permute-start | bytes 786440 | tf_op jit(solution)/shard_map/ppermute | solution.py:388
  90.8 2.6 %collective-permute-start.26 = (bf16[128,1024]{1,0:T(8,128)(2,1)S(1)}, bf16[128,1024]{1,0:T(8,128)(2,1)S(1)}, u32[]{:S(2)}, u32[]{:S(2)}) collective-permute-start(bf16[128,1024]{1,0:T(8,128)(2,1)S(1)} %get-tuple-element.52.refs_1_), channel_id=1, source_target_pairs={{0,4},{1,5},{2,6},{3,7},{4,8},{5,9},{6,10},{7,11},{8,12},{9,13},{1... | collective-permute-start | bytes 786440 | tf_op jit(solution)/shard_map/ppermute | solution.py:388
  93.4 12.6 %collective-permute-done.24.refs_9_.refs_1_.refs_5_ = bf16[128,1024]{1,0:T(8,128)(2,1)S(1)} collective-permute-done((bf16[128,1024]{1,0:T(8,128)(2,1)S(1)}, bf16[128,1024]{1,0:T(8,128)(2,1)S(1)}, u32[]{:S(2)}, u32[]{:S(2)}) %collective-permute-start.24) | collective-permute-done | bytes 262176 | tf_op jit(solution)/shard_map/ppermute | solution.py:388
  106.0 1.9 %collective-permute-done.26.refs_5_.refs_1_ = bf16[128,1024]{1,0:T(8,128)(2,1)S(1)} collective-permute-done((bf16[128,1024]{1,0:T(8,128)(2,1)S(1)}, bf16[128,1024]{1,0:T(8,128)(2,1)S(1)}, u32[]{:S(2)}, u32[]{:S(2)}) %collective-permute-start.26) | collective-permute-done | bytes 262176 | tf_op jit(solution)/shard_map/ppermute | solution.py:388
  107.9 2.1 %outer.4.refs_11_ = bf16[512,1024]{1,0:T(8,128)(2,1)S(1)} custom-call(s32[6]{0:T(128)S(1)} %stack.80.refs_0_, bf16[2,128,1024]{2,1,0:T(8,128)(2,1)S(1)} %get-tuple-element.53.refs_1_, bf16[2,128,1024]{2,1,0:T(8,128)(2,1)S(1)} %pad_maximum_fusion.1.refs_2_, bf16[2,1,128,1024]{3,2,1,0:T(8,128)(2,1)S(1)} %copy-done.1, ...), custom_call_target="tpu_custom_call" | custom-call | flops 1 | bytes 1 | tf_op jit(solution)/shard_map/outer/pallas_call | solution.py:51
  111.2 2.1 %outer.5 = f32[512,1024]{1,0:T(8,128)S(1)} custom-call(s32[6]{0:T(128)S(1)} %stack.80.refs_0_, bf16[2,128,1024]{2,1,0:T(8,128)(2,1)S(1)} %get-tuple-element.53.refs_1_, bf16[2,128,1024]{2,1,0:T(8,128)(2,1)S(1)} %pad_maximum_fusion.1.refs_2_, bf16[2,1,128,1024]{3,2,1,0:T(8,128)(2,1)S(1)} %copy-done.1, ...), custom_call_target="tpu_custom_call" | custom-call | flops 1 | bytes 1 | tf_op jit(solution)/shard_map/outer/pallas_call | solution.py:51
  113.7 1.8 %ahead.6 = (bf16[1024,128]{1,0:T(8,128)(2,1)S(1)}, bf16[1024,128]{1,0:T(8,128)(2,1)S(1)}) custom-call(s32[6]{0:T(128)S(1)} %stack.80.refs_0_, bf16[128,1024]{1,0:T(8,128)(2,1)S(1)} %collective-permute-done.26.refs_5_.refs_1_, bf16[2,128,1024]{2,1,0:T(8,128)(2,1)S(1)} %copy-done, bf16[128,1024]{1,0:T(8,128)(2,1)S(1)} %collective-permute-done.27.refs_7_.refs_3_, ...), custom_call_target="tpu_custom_call" | custom-call | flops 1 | bytes 1 | tf_op jit(solution)/shard_map/ahead/pallas_call | solution.py:51
  118.3 3.1 %ahead.7 = (bf16[1024,128]{1,0:T(8,128)(2,1)S(1)}, bf16[1024,128]{1,0:T(8,128)(2,1)S(1)}) custom-call(s32[6]{0:T(128)S(1)} %stack.80.refs_0_, bf16[128,1024]{1,0:T(8,128)(2,1)S(1)} %collective-permute-done.24.refs_9_.refs_1_.refs_5_, bf16[2,128,1024]{2,1,0:T(8,128)(2,1)S(1)} %copy-done, ...), custom_call_target="tpu_custom_call" | custom-call | flops 1 | bytes 1 | tf_op jit(solution)/shard_map/ahead/pallas_call | solution.py:51
  122.0 2.5 %collective-permute-done.34 = bf16[512,128]{1,0:T(8,128)(2,1)S(1)} collective-permute-done((bf16[512,128]{1,0:T(8,128)(2,1)S(1)}, bf16[512,128]{1,0:T(8,128)(2,1)S(1)}, u32[]{:S(2)}, u32[]{:S(2)}) %collective-permute-start.34) | collective-permute-done | bytes 131104 | tf_op jit(solution)/shard_map/ppermute | solution.py:372
  125.6 3.9 %collective-permute-done.32.refs_5_.refs_8_ = bf16[1024,128]{1,0:T(8,128)(2,1)S(1)} collective-permute-done((bf16[1024,128]{1,0:T(8,128)(2,1)S(1)}, bf16[1024,128]{1,0:T(8,128)(2,1)S(1)}, u32[]{:S(2)}, u32[]{:S(2)}) %collective-permute-start.32) | collective-permute-done | bytes 262176 | tf_op jit(solution)/shard_map/ppermute | solution.py:372
  134.2 2.1 %outer.6.refs_10_ = bf16[512,1024]{1,0:T(8,128)(2,1)S(1)} custom-call(s32[6]{0:T(128)S(1)} %stack.80.refs_0_, bf16[2,128,1024]{2,1,0:T(8,128)(2,1)S(1)} %get-tuple-element.60.refs_1_, bf16[2,128,1024]{2,1,0:T(8,128)(2,1)S(1)} %pad_maximum_fusion.refs_1_.refs_2_, bf16[2,1,128,1024]{3,2,1,0:T(8,128)(2,1)S(1)} %copy-done.1, ...), custom_call_target="tpu_custom_call" | custom-call | flops 1 | bytes 1 | tf_op jit(solution)/shard_map/outer/pallas_call | solution.py:51
  138.5 2.0 %collective-permute-done.44 = bf16[256,256]{1,0:T(8,128)(2,1)S(1)} collective-permute-done((bf16[256,256]{1,0:T(8,128)(2,1)S(1)}, bf16[256,256]{1,0:T(8,128)(2,1)S(1)}, u32[]{:S(2)}, u32[]{:S(2)}) %collective-permute-start.44) | collective-permute-done | bytes 131104 | tf_op jit(solution)/shard_map/ppermute | solution.py:372
  140.8 2.1 %outer.7 = f32[512,1024]{1,0:T(8,128)S(1)} custom-call(s32[6]{0:T(128)S(1)} %stack.80.refs_0_, bf16[2,128,1024]{2,1,0:T(8,128)(2,1)S(1)} %get-tuple-element.60.refs_1_, bf16[2,128,1024]{2,1,0:T(8,128)(2,1)S(1)} %pad_maximum_fusion.refs_1_.refs_2_, bf16[2,1,128,1024]{3,2,1,0:T(8,128)(2,1)S(1)} %copy-done.1, ...), custom_call_target="tpu_custom_call" | custom-call | flops 1 | bytes 1 | tf_op jit(solution)/shard_map/outer/pallas_call | solution.py:51
  145.0 1.6 collective-permute-start.45
  148.1 3.4 %back.2 = (bf16[2,2,1,128,2048]{4,3,2,1,0:T(8,128)(2,1)}, bf16[2,2,1,128,256]{4,3,2,1,0:T(8,128)(2,1)}) custom-call(s32[6]{0:T(128)S(1)} %stack.80.refs_0_, bf16[2,2,1,128,2048]{4,3,2,1,0:T(8,128)(2,1)S(1)} %copy-done.2, bf16[2,2,1,128,256]{4,3,2,1,0:T(8,128)(2,1)S(1)} %copy-done.5, bf16[2,2,128,256]{3,2,1,0:T(8,128)(2,1)S(1)} %get-tuple-element.42.refs_4_.refs_3_, ...), custom_call_target="tpu_custom_call" | custom-call | flops 1 | bytes 1 | tf_op jit(solution)/shard_map/back/pallas_call | solution.py:51
  151.5 3.4 %back.3 = (bf16[2,2,1,128,2048]{4,3,2,1,0:T(8,128)(2,1)}, bf16[2,2,1,128,256]{4,3,2,1,0:T(8,128)(2,1)}) custom-call(s32[6]{0:T(128)S(1)} %stack.80.refs_0_, bf16[2,2,1,128,2048]{4,3,2,1,0:T(8,128)(2,1)S(1)} %copy-done.2, bf16[2,2,1,128,256]{4,3,2,1,0:T(8,128)(2,1)S(1)} %copy-done.5, ...), custom_call_target="tpu_custom_call", output_to_operand_aliasing={{0}: (9, {}), {1}: (10, {})} | custom-call | flops 1 | bytes 1 | tf_op jit(solution)/shard_map/back/pallas_call | solution.py:51
  155.0 16.2 %collective-permute-done.45 = bf16[256,256]{1,0:T(8,128)(2,1)S(1)} collective-permute-done((bf16[256,256]{1,0:T(8,128)(2,1)S(1)}, bf16[256,256]{1,0:T(8,128)(2,1)S(1)}, u32[]{:S(2)}, u32[]{:S(2)}) %collective-permute-start.45) | collective-permute-done | bytes 131104 | tf_op jit(solution)/shard_map/ppermute | solution.py:378
  173.1 3.0 %update.1 = (f32[1,512,1024]{2,1,0:T(8,128)}, f32[1,512,1024]{2,1,0:T(8,128)}) custom-call(s32[6]{0:T(128)S(1)} %stack.80.refs_0_, f32[512,1024]{1,0:T(8,128)S(1)} %convert_add_fusion.refs_9_.refs_1_, bf16[512,1024]{1,0:T(8,128)(2,1)S(1)} %collective-permute-done.46.refs_2_, f32[1,512,1024]{2,1,0:T(8,128)S(1)} %copy-done.7, f32[1,512,1024]{2,1,0:T(8,128)S(1)} %copy-done.4, ...), custom_call_target="tpu_custom_call" | custom-call | flops 1 | bytes 1 | tf_op jit(solution)/shard_map/update/pallas_call | solution.py:51
  (157 shorter events, 52.8 us)
Async XLA Ops:
  1.6 9.1 %collective-permute-start.3 = (bf16[256,256]{1,0:T(8,128)(2,1)S(1)}, bf16[256,256]{1,0:T(8,128)(2,1)}, u32[]{:S(2)}, u32[]{:S(2)}) collective-permute-start(bf16[256,256]{1,0:T(8,128)(2,1)S(1)} %convert_bitcast_fusion.refs_2_), channel_id=1, source_target_pairs={{0,28},{4,24},{8,20},{12,16},{16,12},{20,8},{24,4},{28,0},{1,29},{... | collective-permute-start | bytes 393224 | tf_op jit(solution)/shard_map/ppermute | solution.py:378
  3.2 7.5 %collective-permute-start.2 = (bf16[256,256]{1,0:T(8,128)(2,1)S(1)}, bf16[256,256]{1,0:T(8,128)(2,1)S(1)}, u32[]{:S(2)}, u32[]{:S(2)}) collective-permute-start(bf16[256,256]{1,0:T(8,128)(2,1)S(1)} %convert_bitcast_fusion.refs_2_), channel_id=1, source_target_pairs={{0,3},{1,2},{2,1},{3,0},{4,7},{5,6},{6,5},{7,4},{8,11},{9,10},{10,... | collective-permute-start | bytes 393224 | tf_op jit(solution)/shard_map/ppermute | solution.py:372
  3.9 8.0 %collective-permute-start.1 = (bf16[256,256]{1,0:T(8,128)(2,1)S(1)}, bf16[256,256]{1,0:T(8,128)(2,1)S(1)}, u32[]{:S(2)}, u32[]{:S(2)}) collective-permute-start(bf16[256,256]{1,0:T(8,128)(2,1)S(1)} %convert_bitcast_fusion.refs_2_), channel_id=1, source_target_pairs={{0,2},{1,3},{2,0},{3,1},{4,6},{5,7},{6,4},{7,5},{8,10},{9,11},{10,... | collective-permute-start | bytes 393224 | tf_op jit(solution)/shard_map/ppermute | solution.py:372
  4.8 7.8 %collective-permute-start = (bf16[256,256]{1,0:T(8,128)(2,1)S(1)}, bf16[256,256]{1,0:T(8,128)(2,1)S(1)}, u32[]{:S(2)}, u32[]{:S(2)}) collective-permute-start(bf16[256,256]{1,0:T(8,128)(2,1)S(1)} %convert_bitcast_fusion.refs_2_), channel_id=1, source_target_pairs={{0,1},{1,0},{2,3},{3,2},{4,5},{5,4},{6,7},{7,6},{8,9},{9,8},{10,11... | collective-permute-start | bytes 393224 | tf_op jit(solution)/shard_map/ppermute | solution.py:372
  5.1 18.0 %collective-permute-start.7 = (bf16[2,128,1024]{2,1,0:T(8,128)(2,1)}, bf16[2,128,1024]{2,1,0:T(8,128)(2,1)S(1)}, u32[]{:S(2)}, u32[]{:S(2)}) collective-permute-start(bf16[2,128,1024]{2,1,0:T(8,128)(2,1)} %bitcast.73), channel_id=1, source_target_pairs={{0,2},{1,3},{2,0},{3,1},{4,6},{5,7},{6,4},{7,5},{8,10},{9,11},{10,... | collective-permute-start | bytes 1572872 | tf_op jit(solution)/shard_map/ppermute | solution.py:372
  15.1 15.3 %collective-permute-start.12 = (bf16[128,1024]{1,0:T(8,128)(2,1)}, bf16[128,1024]{1,0:T(8,128)(2,1)S(1)}, u32[]{:S(2)}, u32[]{:S(2)}) collective-permute-start(bf16[128,1024]{1,0:T(8,128)(2,1)} %dynamic-slice_bitcast_fusion), channel_id=1, source_target_pairs={{0,2},{1,3},{2,0},{3,1},{28,30},{29,31},{30,28},{31,29}} | collective-permute-start | bytes 786440 | tf_op jit(solution)/shard_map/ppermute | solution.py:392
  15.8 48.6 %collective-permute-start.14 = (bf16[512,1024]{1,0:T(8,128)(2,1)S(1)}, bf16[512,1024]{1,0:T(8,128)(2,1)}, u32[]{:S(2)}, u32[]{:S(2)}) collective-permute-start(bf16[512,1024]{1,0:T(8,128)(2,1)S(1)} %hold.3), channel_id=1, source_target_pairs={{0,28},{4,24},{8,20},{12,16},{16,12},{20,8},{24,4},{28,0},{1,29},{... | collective-permute-start | bytes 3145736 | tf_op jit(solution)/shard_map/ppermute | solution.py:378
  17.5 11.3 %collective-permute-start.6 = (bf16[256,256]{1,0:T(8,128)(2,1)}, bf16[256,256]{1,0:T(8,128)(2,1)}, u32[]{:S(2)}, u32[]{:S(2)}) collective-permute-start(bf16[256,256]{1,0:T(8,128)(2,1)} %collective-permute-done.3.refs_6_.refs_1_), channel_id=1, source_target_pairs={{0,3},{1,2},{2,1},{3,0},{4,7},{5,6},{6,5},{7,4},{8,11},{9,10},{10,... | collective-permute-start | bytes 393224 | tf_op jit(solution)/shard_map/ppermute | solution.py:372
  18.3 12.1 %collective-permute-start.5 = (bf16[256,256]{1,0:T(8,128)(2,1)}, bf16[256,256]{1,0:T(8,128)(2,1)}, u32[]{:S(2)}, u32[]{:S(2)}) collective-permute-start(bf16[256,256]{1,0:T(8,128)(2,1)} %collective-permute-done.3.refs_6_.refs_1_), channel_id=1, source_target_pairs={{0,2},{1,3},{2,0},{3,1},{4,6},{5,7},{6,4},{7,5},{8,10},{9,11},{10,... | collective-permute-start | bytes 393224 | tf_op jit(solution)/shard_map/ppermute | solution.py:372
  23.1 7.3 %collective-permute-start.4 = (bf16[256,256]{1,0:T(8,128)(2,1)}, bf16[256,256]{1,0:T(8,128)(2,1)}, u32[]{:S(2)}, u32[]{:S(2)}) collective-permute-start(bf16[256,256]{1,0:T(8,128)(2,1)} %collective-permute-done.3.refs_6_.refs_1_), channel_id=1, source_target_pairs={{0,1},{1,0},{2,3},{3,2},{4,5},{5,4},{6,7},{7,6},{8,9},{9,8},{10,11... | collective-permute-start | bytes 393224 | tf_op jit(solution)/shard_map/ppermute | solution.py:372
  28.8 11.9 %collective-permute-start.13 = (bf16[1024,128]{1,0:T(8,128)(2,1)S(1)}, bf16[1024,128]{1,0:T(8,128)(2,1)S(1)}, u32[]{:S(2)}, u32[]{:S(2)}) collective-permute-start(bf16[1024,128]{1,0:T(8,128)(2,1)S(1)} %get-tuple-element.44), channel_id=1, source_target_pairs={{0,2},{1,3},{2,0},{3,1},{4,6},{5,7},{6,4},{7,5},{8,10},{9,11},{10,... | collective-permute-start | bytes 786440 | tf_op jit(solution)/shard_map/ppermute | solution.py:372
  35.3 9.3 %collective-permute-start.15 = (bf16[128,1024]{1,0:T(8,128)(2,1)S(1)}, bf16[128,1024]{1,0:T(8,128)(2,1)S(1)}, u32[]{:S(2)}, u32[]{:S(2)}) collective-permute-start(bf16[128,1024]{1,0:T(8,128)(2,1)S(1)} %get-tuple-element.102), channel_id=1, source_target_pairs={{0,2},{1,3},{2,0},{3,1},{4,6},{5,7},{6,4},{7,5},{8,10},{9,11},{10,... | collective-permute-start | bytes 786440 | tf_op jit(solution)/shard_map/ppermute | solution.py:372
  35.8 14.4 %collective-permute-start.16 = (bf16[128,1024]{1,0:T(8,128)(2,1)S(1)}, bf16[128,1024]{1,0:T(8,128)(2,1)S(1)}, u32[]{:S(2)}, u32[]{:S(2)}) collective-permute-start(bf16[128,1024]{1,0:T(8,128)(2,1)S(1)} %get-tuple-element.103), channel_id=1, source_target_pairs={{0,2},{1,3},{2,0},{3,1},{4,6},{5,7},{6,4},{7,5},{8,10},{9,11},{10,... | collective-permute-start | bytes 786440 | tf_op jit(solution)/shard_map/ppermute | solution.py:372
  40.1 15.7 %collective-permute-start.17 = (bf16[128,1024]{1,0:T(8,128)(2,1)S(1)}, bf16[128,1024]{1,0:T(8,128)(2,1)S(1)}, u32[]{:S(2)}, u32[]{:S(2)}) collective-permute-start(bf16[128,1024]{1,0:T(8,128)(2,1)S(1)} %get-tuple-element.100), channel_id=1, source_target_pairs={{0,2},{1,3},{2,0},{3,1},{4,6},{5,7},{6,4},{7,5},{8,10},{9,11},{10,... | collective-permute-start | bytes 786440 | tf_op jit(solution)/shard_map/ppermute | solution.py:372
  40.6 19.6 %collective-permute-start.18 = (bf16[128,1024]{1,0:T(8,128)(2,1)S(1)}, bf16[128,1024]{1,0:T(8,128)(2,1)S(1)}, u32[]{:S(2)}, u32[]{:S(2)}) collective-permute-start(bf16[128,1024]{1,0:T(8,128)(2,1)S(1)} %get-tuple-element.101), channel_id=1, source_target_pairs={{0,2},{1,3},{2,0},{3,1},{4,6},{5,7},{6,4},{7,5},{8,10},{9,11},{10,... | collective-permute-start | bytes 786440 | tf_op jit(solution)/shard_map/ppermute | solution.py:372
  70.2 8.4 %collective-permute-start.23 = (bf16[1024,128]{1,0:T(8,128)(2,1)S(1)}, bf16[1024,128]{1,0:T(8,128)(2,1)S(1)}, u32[]{:S(2)}, u32[]{:S(2)}) collective-permute-start(bf16[1024,128]{1,0:T(8,128)(2,1)S(1)} %get-tuple-element.51), channel_id=1, source_target_pairs={{0,2},{1,3},{2,0},{3,1},{4,6},{5,7},{6,4},{7,5},{8,10},{9,11},{10,... | collective-permute-start | bytes 786440 | tf_op jit(solution)/shard_map/ppermute | solution.py:372
  79.7 13.7 %collective-permute-start.25 = (bf16[128,1024]{1,0:T(8,128)(2,1)S(1)}, bf16[128,1024]{1,0:T(8,128)(2,1)S(1)}, u32[]{:S(2)}, u32[]{:S(2)}) collective-permute-start(bf16[128,1024]{1,0:T(8,128)(2,1)S(1)} %hold.5), channel_id=1, source_target_pairs={{4,2},{5,3},{6,0},{7,1},{8,6},{9,7},{10,4},{11,5},{12,10},{13,11},... | collective-permute-start | bytes 786440 | tf_op jit(solution)/shard_map/ppermute | solution.py:388
  84.1 21.9 %collective-permute-start.24 = (bf16[128,1024]{1,0:T(8,128)(2,1)S(1)}, bf16[128,1024]{1,0:T(8,128)(2,1)S(1)}, u32[]{:S(2)}, u32[]{:S(2)}) collective-permute-start(bf16[128,1024]{1,0:T(8,128)(2,1)S(1)} %hold.5), channel_id=1, source_target_pairs={{4,0},{5,1},{6,2},{7,3},{8,4},{9,5},{10,6},{11,7},{12,8},{13,9},{1... | collective-permute-start | bytes 786440 | tf_op jit(solution)/shard_map/ppermute | solution.py:388
  86.0 19.9 %collective-permute-start.27 = (bf16[128,1024]{1,0:T(8,128)(2,1)S(1)}, bf16[128,1024]{1,0:T(8,128)(2,1)S(1)}, u32[]{:S(2)}, u32[]{:S(2)}) collective-permute-start(bf16[128,1024]{1,0:T(8,128)(2,1)S(1)} %get-tuple-element.52.refs_1_), channel_id=1, source_target_pairs={{0,6},{1,7},{2,4},{3,5},{4,10},{5,11},{6,8},{7,9},{8,14},{9,15},{1... | collective-permute-start | bytes 786440 | tf_op jit(solution)/shard_map/ppermute | solution.py:388
  90.8 17.1 %collective-permute-start.26 = (bf16[128,1024]{1,0:T(8,128)(2,1)S(1)}, bf16[128,1024]{1,0:T(8,128)(2,1)S(1)}, u32[]{:S(2)}, u32[]{:S(2)}) collective-permute-start(bf16[128,1024]{1,0:T(8,128)(2,1)S(1)} %get-tuple-element.52.refs_1_), channel_id=1, source_target_pairs={{0,4},{1,5},{2,6},{3,7},{4,8},{5,9},{6,10},{7,11},{8,12},{9,13},{1... | collective-permute-start | bytes 786440 | tf_op jit(solution)/shard_map/ppermute | solution.py:388
  115.5 6.4 %collective-permute-start.33 = (bf16[512,128]{1,0:T(8,128)(2,1)S(1)}, bf16[512,128]{1,0:T(8,128)(2,1)S(1)}, u32[]{:S(2)}, u32[]{:S(2)}) collective-permute-start(bf16[512,128]{1,0:T(8,128)(2,1)S(1)} %get-tuple-element.111), channel_id=1, source_target_pairs={{0,2},{1,3},{2,0},{3,1},{4,6},{5,7},{6,4},{7,5},{8,10},{9,11},{10,... | collective-permute-start | bytes 393224 | tf_op jit(solution)/shard_map/ppermute | solution.py:372
  116.1 8.4 %collective-permute-start.34 = (bf16[512,128]{1,0:T(8,128)(2,1)S(1)}, bf16[512,128]{1,0:T(8,128)(2,1)S(1)}, u32[]{:S(2)}, u32[]{:S(2)}) collective-permute-start(bf16[512,128]{1,0:T(8,128)(2,1)S(1)} %get-tuple-element.110), channel_id=1, source_target_pairs={{0,2},{1,3},{2,0},{3,1},{4,6},{5,7},{6,4},{7,5},{8,10},{9,11},{10,... | collective-permute-start | bytes 393224 | tf_op jit(solution)/shard_map/ppermute | solution.py:372
  117.6 54.5 %collective-permute-start.46 = (bf16[512,1024]{1,0:T(8,128)(2,1)S(1)}, bf16[512,1024]{1,0:T(8,128)(2,1)S(1)}, u32[]{:S(2)}, u32[]{:S(2)}) collective-permute-start(bf16[512,1024]{1,0:T(8,128)(2,1)S(1)} %add_convert_fusion.refs_13_), channel_id=1, source_target_pairs={{0,28},{4,24},{8,20},{12,16},{16,12},{20,8},{24,4},{28,0},{1,29},{... | collective-permute-start | bytes 3145736 | tf_op jit(solution)/shard_map/ppermute | solution.py:378
  121.3 8.2 %collective-permute-start.32 = (bf16[1024,128]{1,0:T(8,128)(2,1)S(1)}, bf16[1024,128]{1,0:T(8,128)(2,1)S(1)}, u32[]{:S(2)}, u32[]{:S(2)}) collective-permute-start(bf16[1024,128]{1,0:T(8,128)(2,1)S(1)} %get-tuple-element.56), channel_id=1, source_target_pairs={{0,2},{1,3},{2,0},{3,1},{4,6},{5,7},{6,4},{7,5},{8,10},{9,11},{10,... | collective-permute-start | bytes 786440 | tf_op jit(solution)/shard_map/ppermute | solution.py:372
  132.2 6.4 %collective-permute-start.43 = (bf16[256,256]{1,0:T(8,128)(2,1)S(1)}, bf16[256,256]{1,0:T(8,128)(2,1)S(1)}, u32[]{:S(2)}, u32[]{:S(2)}) collective-permute-start(bf16[256,256]{1,0:T(8,128)(2,1)S(1)} %get-tuple-element.107), channel_id=1, source_target_pairs={{0,2},{1,3},{2,0},{3,1},{4,6},{5,7},{6,4},{7,5},{8,10},{9,11},{10,... | collective-permute-start | bytes 393224 | tf_op jit(solution)/shard_map/ppermute | solution.py:372
  132.7 7.8 %collective-permute-start.44 = (bf16[256,256]{1,0:T(8,128)(2,1)S(1)}, bf16[256,256]{1,0:T(8,128)(2,1)S(1)}, u32[]{:S(2)}, u32[]{:S(2)}) collective-permute-start(bf16[256,256]{1,0:T(8,128)(2,1)S(1)} %get-tuple-element.109), channel_id=1, source_target_pairs={{0,3},{1,2},{2,1},{3,0},{4,7},{5,6},{6,5},{7,4},{8,11},{9,10},{10,... | collective-permute-start | bytes 393224 | tf_op jit(solution)/shard_map/ppermute | solution.py:372
  136.4 6.6 %collective-permute-start.35 = (bf16[128,1024]{1,0:T(8,128)(2,1)S(1)}, bf16[128,1024]{1,0:T(8,128)(2,1)S(1)}, u32[]{:S(2)}, u32[]{:S(2)}) collective-permute-start(bf16[128,1024]{1,0:T(8,128)(2,1)S(1)} %get-tuple-element.84), channel_id=1, source_target_pairs={{0,1},{1,0},{2,3},{3,2},{4,5},{5,4},{6,7},{7,6},{8,9},{9,8},{10,11... | collective-permute-start | bytes 786440 | tf_op jit(solution)/shard_map/ppermute | solution.py:372
  136.8 6.6 %collective-permute-start.38 = (bf16[128,1024]{1,0:T(8,128)(2,1)S(1)}, bf16[128,1024]{1,0:T(8,128)(2,1)S(1)}, u32[]{:S(2)}, u32[]{:S(2)}) collective-permute-start(bf16[128,1024]{1,0:T(8,128)(2,1)S(1)} %get-tuple-element.85), channel_id=1, source_target_pairs={{0,1},{1,0},{2,3},{3,2},{4,5},{5,4},{6,7},{7,6},{8,9},{9,8},{10,11... | collective-permute-start | bytes 786440 | tf_op jit(solution)/shard_map/ppermute | solution.py:372
  143.0 11.9 %collective-permute-start.39 = (bf16[256,256]{1,0:T(8,128)(2,1)S(1)}, bf16[256,256]{1,0:T(8,128)(2,1)S(1)}, u32[]{:S(2)}, u32[]{:S(2)}) collective-permute-start(bf16[256,256]{1,0:T(8,128)(2,1)S(1)} %get-tuple-element.104), channel_id=1, source_target_pairs={{0,1},{1,0},{2,3},{3,2},{4,5},{5,4},{6,7},{7,6},{8,9},{9,8},{10,11... | collective-permute-start | bytes 393224 | tf_op jit(solution)/shard_map/ppermute | solution.py:372
  143.4 11.6 %collective-permute-start.40 = (bf16[256,256]{1,0:T(8,128)(2,1)S(1)}, bf16[256,256]{1,0:T(8,128)(2,1)S(1)}, u32[]{:S(2)}, u32[]{:S(2)}) collective-permute-start(bf16[256,256]{1,0:T(8,128)(2,1)S(1)} %get-tuple-element.106), channel_id=1, source_target_pairs={{0,2},{1,3},{2,0},{3,1},{4,6},{5,7},{6,4},{7,5},{8,10},{9,11},{10,... | collective-permute-start | bytes 393224 | tf_op jit(solution)/shard_map/ppermute | solution.py:372
  143.8 11.1 %collective-permute-start.41 = (bf16[256,256]{1,0:T(8,128)(2,1)S(1)}, bf16[256,256]{1,0:T(8,128)(2,1)S(1)}, u32[]{:S(2)}, u32[]{:S(2)}) collective-permute-start(bf16[256,256]{1,0:T(8,128)(2,1)S(1)} %get-tuple-element.108), channel_id=1, source_target_pairs={{0,3},{1,2},{2,1},{3,0},{4,7},{5,6},{6,5},{7,4},{8,11},{9,10},{10,... | collective-permute-start | bytes 393224 | tf_op jit(solution)/shard_map/ppermute | solution.py:372
  145.0 26.2 %collective-permute-start.45 = (bf16[256,256]{1,0:T(8,128)(2,1)S(1)}, bf16[256,256]{1,0:T(8,128)(2,1)S(1)}, u32[]{:S(2)}, u32[]{:S(2)}) collective-permute-start(bf16[256,256]{1,0:T(8,128)(2,1)S(1)} %fusion.2), channel_id=1, source_target_pairs={{0,28},{4,24},{8,20},{12,16},{16,12},{20,8},{24,4},{28,0},{1,29},{... | collective-permute-start | bytes 393224 | tf_op jit(solution)/shard_map/ppermute | solution.py:378
  (37 other events, 227.6 us)

commit v3 on v2

--- a/solution.py
+++ b/solution.py
@@ -293,11 +293,12 @@
     )[0]
 
 
-def update_kernel(lanes, meta, own, back, moment, weight, moment_out, weight_out):
+def update_kernel(lanes, meta, own, back, moment, weight, moment_out, weight_out, done):
     grad = (own[...] + back[...].astype(F32)) / lanes
     new = decay_rate * moment[...] + grad
     moment_out[...] = new
     weight_out[...] = weight[...] - learn_rate * new
+    done[...] = new[:8, :HEAD]
 
 
 def update(lanes, meta, own, back, moment, weight, deps=()):
@@ -310,9 +311,9 @@
         "update",
         [meta],
         [(own, flat), (back, flat), (moment, deep), (weight, deep)],
-        [sds(moment.shape, F32)] * 2,
+        [sds(moment.shape, F32)] * 2 + [sds((8, HEAD), F32)],
         rows // step,
-        [deep, deep],
+        [deep, deep, pl.BlockSpec((8, HEAD), lambda i, m: (0, 0))],
         deps=deps,
     )
 
@@ -424,6 +425,7 @@
     g_par = partner(grad_now[:, 0])
     bounds = jnp.concatenate([bound_now.reshape(-1), bound_new.reshape(-1)])
 
+    d = grad_now.shape[-1]
     own, par = {}, {}
     ga, gv, gi = {}, {}, {}
     probs, mine, came = [None] * 2, [None] * 2, [None] * 2
@@ -446,13 +448,17 @@
 
     def run_middle(r, t, deps=()):
         gv[r, t], gi[r, t], *joined = middle(
-            r, t, meta, own[r, t], probs[r], *ga[r, t], w_value, 0, deps
+            r, t, meta, own[r, t], probs[r], *ga[r, t], w_value, int((r, t) == (0, 0)), deps
         )
         return joined
 
     def run_relay(r):
-        own[r, 1] = [piece(relayed(gi[r, 0], r)), piece(grad_new, r)]
-        par[r, 1] = [piece(relayed(gi[r, 0], r, half)), piece(fresh_par)]
+        x = joined[0] if r == 0 else gi[1, 0]
+        got = [relayed(x, r, k) for k in (0, half)]
+        block = pl.BlockSpec((x.shape[0], d), lambda i, *s: (0, 0))
+        own[r, 1] = [(got[0], block), piece(grad_new, r)]
+        par[r, 1] = [(got[1], block), piece(fresh_par)]
+        return got
 
     def run_outer(r, deps=()):
         gs = own[r, 0] + par[r, 0] + own[r, 1] + par[r, 1]
@@ -464,16 +470,13 @@
     w_value, values = values_of(meta, inputs_saved, parts_value, [ga[0, 0][0], fresh_par])
     run_front(0)
     run_front(1, [probs[0]])
-    run_middle(0, 0, [probs[1]])
+    joined = run_middle(0, 0, [probs[1]])
     mirror_out = hold(mirror_out, [came[0], came[1], gi[0, 0]])
     parts_out.append(with_mates(mirror_out))
     run_ahead(1, 0)
     run_middle(1, 0)
     run_relay(1)
-    gi[0, 0] = hold(gi[0, 0], [gi[1, 0]])
-    run_relay(0)
-    relays = [own[0, 1][0][0], par[0, 1][0][0]]
-    total1 = run_outer(1, relays)
+    total1 = run_outer(1, run_relay(0))
     send_out = total1.astype(BF)
     back_out = mirrored(send_out)
     run_ahead(1, 1, [send_out])
@@ -491,9 +494,10 @@
         0, per, heads, meta, queries_saved, keys_saved, values, probs[0], gas[0], out
     )
     grad_inputs = jnp.stack([jnp.stack([gi[r, t] for t in range(2)]) for r in range(2)])[:, :, None]
-    out_moment_new, out_weight_new = update(
+    out_moment_new, out_weight_new, updated = update(
         lanes, meta, total0, back_out, out_moment, out_weight, [grad_keys]
     )
+    back_value = hold(back_value, [updated])
     mean_value = (total[0] + back_value.astype(F32)) / lanes
     value_moment_new = decay_rate * value_moment + mean_value[None]
     value_weight_new = value_weight - learn_rate * value_moment_new

time: 177 us -> 170 us (0.960)
  waiting for transfers between devices: 75.8 us -> 67.5 us
    ppermute x4, waiting for transfers between devices: 14.5 us -> 7.75 us  [relayed(): return lax.ppermute(x, ('section', 'lane'), pairs)]
    ppermute x4, waiting for transfers between devices: 21.9 us -> 19.4 us  [mirrored(): lax.ppermute(x, 'section', [(i, sections - 1 - i) for i in range(sections)])]
  transfers between devices with their start and end apart: 47 -> 47, of which waited for: 20 -> 19; matrix products, arithmetic and copies ran while one was open for 3% -> 3% of each run, Pallas kernels for 18% -> 21%
where the time goes in v3:
time: 170 us; the launch traced here: 169 us
  waiting for transfers between devices  67.5 us (40%)
  starting transfers between devices  44.4 us (26%)
  Pallas kernels  41.3 us (24%)
  local copies, waits for them, and re-layouts  10.2 us (6%)
  other arithmetic  4.74 us (3%)
    pallas_call x23, Pallas kernels, call(): pl.pallas_call(body, grid_spec=grid, out_shape=shapes, input_output_alias...  41.3 us
    ppermute x38, waiting for transfers between devices, at_lane(): return lax.ppermute(x, 'lane', [(i, i ^ k) for i in range(lanes)])  40.3 us
    ppermute x38, starting transfers between devices, at_lane(): return lax.ppermute(x, 'lane', [(i, i ^ k) for i in range(lanes)])  22.8 us
    ppermute x4, waiting for transfers between devices, mirrored(): lax.ppermute(x, 'section', [(i, sections - 1 - i) for i in range(sections)])  19.4 us
    ppermute x4, starting transfers between devices, relayed(): return lax.ppermute(x, ('section', 'lane'), pairs)  13.8 us
    ppermute x4, waiting for transfers between devices, relayed(): return lax.ppermute(x, ('section', 'lane'), pairs)  7.75 us
    ppermute x4, starting transfers between devices, mirrored(): lax.ppermute(x, 'section', [(i, sections - 1 - i) for i in range(sections)])  7.18 us
    unnamed x46, local copies, waits for them, and re-layouts  6.86 us
  transfers between devices with their start and end apart: 47, of which 19 were waited for; matrix products, arithmetic and copies ran while one was open for 3% of the time, Pallas kernels for 21%

profile of v3, /device:TPU:10, one launch (start us, length us, event | category | flops | bytes accessed | tf_op | source)
XLA Modules:
  0.0 169.4 jit_solution(16228942204153211382)
XLA Ops:
  19.1 4.1 %collective-permute-done.7.refs_2_.refs_4_ = bf16[2,128,1024]{2,1,0:T(8,128)(2,1)S(1)} collective-permute-done((bf16[2,128,1024]{2,1,0:T(8,128)(2,1)}, bf16[2,128,1024]{2,1,0:T(8,128)(2,1)S(1)}, u32[]{:S(2)}, u32[]{:S(2)}) %collective-permute-start.7) | collective-permute-done | bytes 524320 | tf_op jit(solution)/shard_map/ppermute | solution.py:373
  25.7 3.0 %ahead.4 = (bf16[1024,128]{1,0:T(8,128)(2,1)S(1)}, bf16[1024,128]{1,0:T(8,128)(2,1)S(1)}) custom-call(s32[6]{0:T(128)S(1)} %stack.80.refs_0_, bf16[2,1,128,1024]{3,2,1,0:T(8,128)(2,1)S(1)} %copy-done.2, bf16[2,128,1024]{2,1,0:T(8,128)(2,1)S(1)} %collective-permute-done.7.refs_2_.refs_4_, bf16[128,1024]{1,0:T(8,128)(2,1)} %get-tuple-element.103.refs_3_.refs_5_, ...), custom_call_target="tpu_custom_call" | custom-call | flops 1 | bytes 1 | tf_op jit(solution)/shard_map/ahead/pallas_call | solution.py:51
  28.8 1.7 collective-permute-start.13
  30.5 2.1 %values.1 = (bf16[2,1024,256]{2,1,0:T(8,128)(2,1)S(1)}, bf16[2,2,128,256]{3,2,1,0:T(8,128)(2,1)S(1)}) custom-call(s32[6]{0:T(128)S(1)} %stack.80.refs_0_, bf16[2,2,1,128,1024]{4,3,2,1,0:T(8,128)(2,1)S(1)} %copy-done.6, bf16[256,256]{1,0:T(8,128)(2,1)S(1)} %convert_bitcast_fusion.refs_2_, bf16[256,256]{1,0:T(8,128)(2,1)S(1)} %copy-done.17, ...), custom_call_target="tpu_custom_call" | custom-call | flops 1 | bytes 1 | tf_op jit(solution)/shard_map/values/pallas_call | solution.py:51
  32.6 2.7 %front.2 = (bf16[2,2,128,1024]{3,2,1,0:T(8,128)(2,1)S(1)}, bf16[2,128,1024]{2,1,0:T(8,128)(2,1)S(1)}, bf16[2,128,1024]{2,1,0:T(8,128)(2,1)S(1)}) custom-call(s32[6]{0:T(128)S(1)} %stack.80.refs_0_, s32[18]{0:T(128)S(1)} %pad_add_fusion.refs_1_, bf16[2,2,1,128,2048]{4,3,2,1,0:T(8,128)(2,1)S(1)} %copy-done.1, bf16[2,2,1,128,256]{4,3,2,1,0:T(8,128)(2,1)S(1)} %copy-done.5, ...), custom_call_target="tpu_custom_call" | custom-call | flops 1 | bytes 1 | tf_op jit(solution)/shard_map/front/pallas_call | solution.py:51
  37.4 2.7 %front.3 = (bf16[2,2,128,1024]{3,2,1,0:T(8,128)(2,1)S(1)}, bf16[2,128,1024]{2,1,0:T(8,128)(2,1)S(1)}, bf16[2,128,1024]{2,1,0:T(8,128)(2,1)S(1)}) custom-call(s32[6]{0:T(128)S(1)} %stack.80.refs_0_, s32[18]{0:T(128)S(1)} %pad_add_fusion.refs_1_, bf16[2,2,1,128,2048]{4,3,2,1,0:T(8,128)(2,1)S(1)} %copy-done.1, bf16[2,2,1,128,256]{4,3,2,1,0:T(8,128)(2,1)S(1)} %copy-done.5, ...), custom_call_target="tpu_custom_call" | custom-call | flops 1 | bytes 1 | tf_op jit(solution)/shard_map/front/pallas_call | solution.py:51
  44.6 5.6 %collective-permute-done.18 = bf16[128,1024]{1,0:T(8,128)(2,1)S(1)} collective-permute-done((bf16[128,1024]{1,0:T(8,128)(2,1)S(1)}, bf16[128,1024]{1,0:T(8,128)(2,1)S(1)}, u32[]{:S(2)}, u32[]{:S(2)}) %collective-permute-start.18) | collective-permute-done | bytes 262176 | tf_op jit(solution)/shard_map/ppermute | solution.py:373
  50.3 5.6 %collective-permute-done.19 = bf16[128,1024]{1,0:T(8,128)(2,1)S(1)} collective-permute-done((bf16[128,1024]{1,0:T(8,128)(2,1)S(1)}, bf16[128,1024]{1,0:T(8,128)(2,1)S(1)}, u32[]{:S(2)}, u32[]{:S(2)}) %collective-permute-start.19) | collective-permute-done | bytes 262176 | tf_op jit(solution)/shard_map/ppermute | solution.py:373
  55.9 4.3 %collective-permute-done.20 = bf16[128,1024]{1,0:T(8,128)(2,1)S(1)} collective-permute-done((bf16[128,1024]{1,0:T(8,128)(2,1)S(1)}, bf16[128,1024]{1,0:T(8,128)(2,1)S(1)}, u32[]{:S(2)}, u32[]{:S(2)}) %collective-permute-start.20) | collective-permute-done | bytes 262176 | tf_op jit(solution)/shard_map/ppermute | solution.py:373
  60.2 4.2 %collective-permute-done.16.refs_0_ = bf16[512,1024]{1,0:T(8,128)(2,1)} collective-permute-done((bf16[512,1024]{1,0:T(8,128)(2,1)S(1)}, bf16[512,1024]{1,0:T(8,128)(2,1)}, u32[]{:S(2)}, u32[]{:S(2)}) %collective-permute-start.16) | collective-permute-done | bytes 1048608 | tf_op jit(solution)/shard_map/ppermute | solution.py:379
  68.4 1.8 %ahead.5 = (bf16[1024,128]{1,0:T(8,128)(2,1)S(1)}, bf16[1024,128]{1,0:T(8,128)(2,1)S(1)}) custom-call(s32[6]{0:T(128)S(1)} %stack.80.refs_0_, bf16[2,1,128,1024]{3,2,1,0:T(8,128)(2,1)S(1)} %copy-done.2, bf16[2,128,1024]{2,1,0:T(8,128)(2,1)S(1)} %collective-permute-done.7.refs_2_.refs_4_, bf16[128,1024]{1,0:T(8,128)(2,1)S(1)} %get-tuple-element.99.refs_3_.refs_5_, ...), custom_call_target="tpu_custom_call" | custom-call | flops 1 | bytes 1 | tf_op jit(solution)/shard_map/ahead/pallas_call | solution.py:51
  70.2 1.6 collective-permute-start.25
  71.9 3.3 %collective-permute-start.15 = (bf16[128,1280]{1,0:T(8,128)(2,1)S(1)}, bf16[128,1280]{1,0:T(8,128)(2,1)S(1)}, u32[]{:S(2)}, u32[]{:S(2)}) collective-permute-start(bf16[128,1280]{1,0:T(8,128)(2,1)S(1)} %get-tuple-element.50), channel_id=1, source_target_pairs={{4,2},{5,3},{6,0},{7,1},{8,6},{9,7},{10,4},{11,5},{12,10},{13,11},... | collective-permute-start | bytes 983048 | tf_op jit(solution)/shard_map/ppermute | solution.py:389
  75.2 2.0 %collective-permute-start.14 = (bf16[128,1280]{1,0:T(8,128)(2,1)S(1)}, bf16[128,1280]{1,0:T(8,128)(2,1)S(1)}, u32[]{:S(2)}, u32[]{:S(2)}) collective-permute-start(bf16[128,1280]{1,0:T(8,128)(2,1)S(1)} %get-tuple-element.50), channel_id=1, source_target_pairs={{4,0},{5,1},{6,2},{7,3},{8,4},{9,5},{10,6},{11,7},{12,8},{13,9},{1... | collective-permute-start | bytes 983048 | tf_op jit(solution)/shard_map/ppermute | solution.py:389
  77.2 8.0 %collective-permute-done.25.refs_4_.refs_6_ = bf16[1024,128]{1,0:T(8,128)(2,1)S(1)} collective-permute-done((bf16[1024,128]{1,0:T(8,128)(2,1)S(1)}, bf16[1024,128]{1,0:T(8,128)(2,1)S(1)}, u32[]{:S(2)}, u32[]{:S(2)}) %collective-permute-start.25) | collective-permute-done | bytes 262176 | tf_op jit(solution)/shard_map/ppermute | solution.py:373
  86.2 4.9 %collective-permute-start.27 = (bf16[128,1024]{1,0:T(8,128)(2,1)S(1)}, bf16[128,1024]{1,0:T(8,128)(2,1)S(1)}, u32[]{:S(2)}, u32[]{:S(2)}) collective-permute-start(bf16[128,1024]{1,0:T(8,128)(2,1)S(1)} %get-tuple-element.55), channel_id=1, source_target_pairs={{0,6},{1,7},{2,4},{3,5},{4,10},{5,11},{6,8},{7,9},{8,14},{9,15},{1... | collective-permute-start | bytes 786440 | tf_op jit(solution)/shard_map/ppermute | solution.py:389
  91.1 3.6 %collective-permute-start.26 = (bf16[128,1024]{1,0:T(8,128)(2,1)S(1)}, bf16[128,1024]{1,0:T(8,128)(2,1)S(1)}, u32[]{:S(2)}, u32[]{:S(2)}) collective-permute-start(bf16[128,1024]{1,0:T(8,128)(2,1)S(1)} %get-tuple-element.55), channel_id=1, source_target_pairs={{0,4},{1,5},{2,6},{3,7},{4,8},{5,9},{6,10},{7,11},{8,12},{9,13},{1... | collective-permute-start | bytes 786440 | tf_op jit(solution)/shard_map/ppermute | solution.py:389
  94.7 3.6 %collective-permute-done.27.refs_7_.refs_3_ = bf16[128,1024]{1,0:T(8,128)(2,1)S(1)} collective-permute-done((bf16[128,1024]{1,0:T(8,128)(2,1)S(1)}, bf16[128,1024]{1,0:T(8,128)(2,1)S(1)}, u32[]{:S(2)}, u32[]{:S(2)}) %collective-permute-start.27) | collective-permute-done | bytes 262176 | tf_op jit(solution)/shard_map/ppermute | solution.py:389
  98.3 4.2 %collective-permute-done.26.refs_5_.refs_1_ = bf16[128,1024]{1,0:T(8,128)(2,1)S(1)} collective-permute-done((bf16[128,1024]{1,0:T(8,128)(2,1)S(1)}, bf16[128,1024]{1,0:T(8,128)(2,1)S(1)}, u32[]{:S(2)}, u32[]{:S(2)}) %collective-permute-start.26) | collective-permute-done | bytes 262176 | tf_op jit(solution)/shard_map/ppermute | solution.py:389
  102.5 2.1 %outer.4.refs_11_ = bf16[512,1024]{1,0:T(8,128)(2,1)S(1)} custom-call(s32[6]{0:T(128)S(1)} %stack.80.refs_0_, bf16[2,128,1024]{2,1,0:T(8,128)(2,1)S(1)} %get-tuple-element.56.refs_1_, bf16[2,128,1024]{2,1,0:T(8,128)(2,1)S(1)} %pad_maximum_fusion.1.refs_2_, bf16[2,1,128,1024]{3,2,1,0:T(8,128)(2,1)S(1)} %copy-done.2, ...), custom_call_target="tpu_custom_call" | custom-call | flops 1 | bytes 1 | tf_op jit(solution)/shard_map/outer/pallas_call | solution.py:51
  105.8 2.1 %outer.5 = f32[512,1024]{1,0:T(8,128)S(1)} custom-call(s32[6]{0:T(128)S(1)} %stack.80.refs_0_, bf16[2,128,1024]{2,1,0:T(8,128)(2,1)S(1)} %get-tuple-element.56.refs_1_, bf16[2,128,1024]{2,1,0:T(8,128)(2,1)S(1)} %pad_maximum_fusion.1.refs_2_, bf16[2,1,128,1024]{3,2,1,0:T(8,128)(2,1)S(1)} %copy-done.2, ...), custom_call_target="tpu_custom_call" | custom-call | flops 1 | bytes 1 | tf_op jit(solution)/shard_map/outer/pallas_call | solution.py:51
  108.3 1.8 %ahead.6 = (bf16[1024,128]{1,0:T(8,128)(2,1)S(1)}, bf16[1024,128]{1,0:T(8,128)(2,1)S(1)}) custom-call(s32[6]{0:T(128)S(1)} %stack.80.refs_0_, bf16[128,1024]{1,0:T(8,128)(2,1)S(1)} %collective-permute-done.26.refs_5_.refs_1_, bf16[2,128,1024]{2,1,0:T(8,128)(2,1)S(1)} %copy-done, bf16[128,1024]{1,0:T(8,128)(2,1)S(1)} %collective-permute-done.27.refs_7_.refs_3_, ...), custom_call_target="tpu_custom_call" | custom-call | flops 1 | bytes 1 | tf_op jit(solution)/shard_map/ahead/pallas_call | solution.py:51
  112.3 2.7 %collective-permute-start.46 = (bf16[512,1024]{1,0:T(8,128)(2,1)S(1)}, bf16[512,1024]{1,0:T(8,128)(2,1)S(1)}, u32[]{:S(2)}, u32[]{:S(2)}) collective-permute-start(bf16[512,1024]{1,0:T(8,128)(2,1)S(1)} %add_convert_fusion.refs_13_), channel_id=1, source_target_pairs={{0,28},{4,24},{8,20},{12,16},{16,12},{20,8},{24,4},{28,0},{1,29},{... | collective-permute-start | bytes 3145736 | tf_op jit(solution)/shard_map/ppermute | solution.py:379
  114.9 3.1 %ahead.7 = (bf16[1024,128]{1,0:T(8,128)(2,1)S(1)}, bf16[1024,128]{1,0:T(8,128)(2,1)S(1)}) custom-call(s32[6]{0:T(128)S(1)} %stack.80.refs_0_, bf16[128,1280]{1,0:T(8,128)(2,1)S(1)} %collective-permute-done.14.refs_9_.refs_1_.refs_5_, bf16[2,128,1024]{2,1,0:T(8,128)(2,1)S(1)} %copy-done, ...), custom_call_target="tpu_custom_call" | custom-call | flops 1 | bytes 1 | tf_op jit(solution)/shard_map/ahead/pallas_call | solution.py:51
  119.7 5.9 %collective-permute-done.32.refs_5_.refs_8_ = bf16[1024,128]{1,0:T(8,128)(2,1)S(1)} collective-permute-done((bf16[1024,128]{1,0:T(8,128)(2,1)S(1)}, bf16[1024,128]{1,0:T(8,128)(2,1)S(1)}, u32[]{:S(2)}, u32[]{:S(2)}) %collective-permute-start.32) | collective-permute-done | bytes 262176 | tf_op jit(solution)/shard_map/ppermute | solution.py:373
  130.2 2.2 %outer.6.refs_10_ = bf16[512,1024]{1,0:T(8,128)(2,1)S(1)} custom-call(s32[6]{0:T(128)S(1)} %stack.80.refs_0_, bf16[2,128,1024]{2,1,0:T(8,128)(2,1)S(1)} %get-tuple-element.63.refs_1_, bf16[2,128,1024]{2,1,0:T(8,128)(2,1)S(1)} %pad_maximum_fusion.refs_1_.refs_2_, bf16[2,1,128,1024]{3,2,1,0:T(8,128)(2,1)S(1)} %copy-done.2, ...), custom_call_target="tpu_custom_call" | custom-call | flops 1 | bytes 1 | tf_op jit(solution)/shard_map/outer/pallas_call | solution.py:51
  134.5 2.0 %collective-permute-done.44 = bf16[256,256]{1,0:T(8,128)(2,1)S(1)} collective-permute-done((bf16[256,256]{1,0:T(8,128)(2,1)S(1)}, bf16[256,256]{1,0:T(8,128)(2,1)S(1)}, u32[]{:S(2)}, u32[]{:S(2)}) %collective-permute-start.44) | collective-permute-done | bytes 131104 | tf_op jit(solution)/shard_map/ppermute | solution.py:373
  136.8 2.2 %outer.7 = f32[512,1024]{1,0:T(8,128)S(1)} custom-call(s32[6]{0:T(128)S(1)} %stack.80.refs_0_, bf16[2,128,1024]{2,1,0:T(8,128)(2,1)S(1)} %get-tuple-element.63.refs_1_, bf16[2,128,1024]{2,1,0:T(8,128)(2,1)S(1)} %pad_maximum_fusion.refs_1_.refs_2_, bf16[2,1,128,1024]{3,2,1,0:T(8,128)(2,1)S(1)} %copy-done.2, ...), custom_call_target="tpu_custom_call" | custom-call | flops 1 | bytes 1 | tf_op jit(solution)/shard_map/outer/pallas_call | solution.py:51
  143.8 3.4 %back.2 = (bf16[2,2,1,128,2048]{4,3,2,1,0:T(8,128)(2,1)}, bf16[2,2,1,128,256]{4,3,2,1,0:T(8,128)(2,1)}) custom-call(s32[6]{0:T(128)S(1)} %stack.80.refs_0_, bf16[2,2,1,128,2048]{4,3,2,1,0:T(8,128)(2,1)S(1)} %copy-done.1, bf16[2,2,1,128,256]{4,3,2,1,0:T(8,128)(2,1)S(1)} %copy-done.5, bf16[2,2,128,256]{3,2,1,0:T(8,128)(2,1)S(1)} %get-tuple-element.44.refs_4_.refs_3_, ...), custom_call_target="tpu_custom_call" | custom-call | flops 1 | bytes 1 | tf_op jit(solution)/shard_map/back/pallas_call | solution.py:51
  147.2 3.4 %back.3 = (bf16[2,2,1,128,2048]{4,3,2,1,0:T(8,128)(2,1)}, bf16[2,2,1,128,256]{4,3,2,1,0:T(8,128)(2,1)}) custom-call(s32[6]{0:T(128)S(1)} %stack.80.refs_0_, bf16[2,2,1,128,2048]{4,3,2,1,0:T(8,128)(2,1)S(1)} %copy-done.1, bf16[2,2,1,128,256]{4,3,2,1,0:T(8,128)(2,1)S(1)} %copy-done.5, ...), custom_call_target="tpu_custom_call", output_to_operand_aliasing={{0}: (9, {}), {1}: (10, {})} | custom-call | flops 1 | bytes 1 | tf_op jit(solution)/shard_map/back/pallas_call | solution.py:51
  150.6 13.7 %collective-permute-done.46.refs_2_ = bf16[512,1024]{1,0:T(8,128)(2,1)S(1)} collective-permute-done((bf16[512,1024]{1,0:T(8,128)(2,1)S(1)}, bf16[512,1024]{1,0:T(8,128)(2,1)S(1)}, u32[]{:S(2)}, u32[]{:S(2)}) %collective-permute-start.46) | collective-permute-done | bytes 1048608 | tf_op jit(solution)/shard_map/ppermute | solution.py:379
  165.3 3.1 %update.1 = (f32[1,512,1024]{2,1,0:T(8,128)}, f32[1,512,1024]{2,1,0:T(8,128)}, f32[8,128]{1,0:T(8,128)S(1)}) custom-call(s32[6]{0:T(128)S(1)} %stack.80.refs_0_, f32[512,1024]{1,0:T(8,128)S(1)} %convert_add_fusion.refs_9_.refs_1_, bf16[512,1024]{1,0:T(8,128)(2,1)S(1)} %collective-permute-done.46.refs_2_, f32[1,512,1024]{2,1,0:T(8,128)S(1)} %copy-done.7, ...), custom_call_target="tpu_custom_call" | custom-call | flops 1 | bytes 1 | tf_op jit(solution)/shard_map/update/pallas_call | solution.py:51
  (157 shorter events, 51.7 us)
Async XLA Ops:
  1.6 9.1 %collective-permute-start.3 = (bf16[256,256]{1,0:T(8,128)(2,1)S(1)}, bf16[256,256]{1,0:T(8,128)(2,1)}, u32[]{:S(2)}, u32[]{:S(2)}) collective-permute-start(bf16[256,256]{1,0:T(8,128)(2,1)S(1)} %convert_bitcast_fusion.refs_2_), channel_id=1, source_target_pairs={{0,28},{4,24},{8,20},{12,16},{16,12},{20,8},{24,4},{28,0},{1,29},{... | collective-permute-start | bytes 393224 | tf_op jit(solution)/shard_map/ppermute | solution.py:379
  3.2 7.5 %collective-permute-start.2 = (bf16[256,256]{1,0:T(8,128)(2,1)S(1)}, bf16[256,256]{1,0:T(8,128)(2,1)S(1)}, u32[]{:S(2)}, u32[]{:S(2)}) collective-permute-start(bf16[256,256]{1,0:T(8,128)(2,1)S(1)} %convert_bitcast_fusion.refs_2_), channel_id=1, source_target_pairs={{0,3},{1,2},{2,1},{3,0},{4,7},{5,6},{6,5},{7,4},{8,11},{9,10},{10,... | collective-permute-start | bytes 393224 | tf_op jit(solution)/shard_map/ppermute | solution.py:373
  3.9 8.0 %collective-permute-start.1 = (bf16[256,256]{1,0:T(8,128)(2,1)S(1)}, bf16[256,256]{1,0:T(8,128)(2,1)S(1)}, u32[]{:S(2)}, u32[]{:S(2)}) collective-permute-start(bf16[256,256]{1,0:T(8,128)(2,1)S(1)} %convert_bitcast_fusion.refs_2_), channel_id=1, source_target_pairs={{0,2},{1,3},{2,0},{3,1},{4,6},{5,7},{6,4},{7,5},{8,10},{9,11},{10,... | collective-permute-start | bytes 393224 | tf_op jit(solution)/shard_map/ppermute | solution.py:373
  4.8 7.8 %collective-permute-start = (bf16[256,256]{1,0:T(8,128)(2,1)S(1)}, bf16[256,256]{1,0:T(8,128)(2,1)S(1)}, u32[]{:S(2)}, u32[]{:S(2)}) collective-permute-start(bf16[256,256]{1,0:T(8,128)(2,1)S(1)} %convert_bitcast_fusion.refs_2_), channel_id=1, source_target_pairs={{0,1},{1,0},{2,3},{3,2},{4,5},{5,4},{6,7},{7,6},{8,9},{9,8},{10,11... | collective-permute-start | bytes 393224 | tf_op jit(solution)/shard_map/ppermute | solution.py:373
  5.1 18.0 %collective-permute-start.7 = (bf16[2,128,1024]{2,1,0:T(8,128)(2,1)}, bf16[2,128,1024]{2,1,0:T(8,128)(2,1)S(1)}, u32[]{:S(2)}, u32[]{:S(2)}) collective-permute-start(bf16[2,128,1024]{2,1,0:T(8,128)(2,1)} %bitcast.73), channel_id=1, source_target_pairs={{0,2},{1,3},{2,0},{3,1},{4,6},{5,7},{6,4},{7,5},{8,10},{9,11},{10,... | collective-permute-start | bytes 1572872 | tf_op jit(solution)/shard_map/ppermute | solution.py:373
  15.1 15.3 %collective-permute-start.12 = (bf16[128,1024]{1,0:T(8,128)(2,1)}, bf16[128,1024]{1,0:T(8,128)(2,1)S(1)}, u32[]{:S(2)}, u32[]{:S(2)}) collective-permute-start(bf16[128,1024]{1,0:T(8,128)(2,1)} %dynamic-slice_bitcast_fusion), channel_id=1, source_target_pairs={{0,2},{1,3},{2,0},{3,1},{28,30},{29,31},{30,28},{31,29}} | collective-permute-start | bytes 786440 | tf_op jit(solution)/shard_map/ppermute | solution.py:393
  15.8 48.6 %collective-permute-start.16 = (bf16[512,1024]{1,0:T(8,128)(2,1)S(1)}, bf16[512,1024]{1,0:T(8,128)(2,1)}, u32[]{:S(2)}, u32[]{:S(2)}) collective-permute-start(bf16[512,1024]{1,0:T(8,128)(2,1)S(1)} %hold.3), channel_id=1, source_target_pairs={{0,28},{4,24},{8,20},{12,16},{16,12},{20,8},{24,4},{28,0},{1,29},{... | collective-permute-start | bytes 3145736 | tf_op jit(solution)/shard_map/ppermute | solution.py:379
  17.5 11.3 %collective-permute-start.6 = (bf16[256,256]{1,0:T(8,128)(2,1)}, bf16[256,256]{1,0:T(8,128)(2,1)}, u32[]{:S(2)}, u32[]{:S(2)}) collective-permute-start(bf16[256,256]{1,0:T(8,128)(2,1)} %collective-permute-done.3.refs_6_.refs_1_), channel_id=1, source_target_pairs={{0,3},{1,2},{2,1},{3,0},{4,7},{5,6},{6,5},{7,4},{8,11},{9,10},{10,... | collective-permute-start | bytes 393224 | tf_op jit(solution)/shard_map/ppermute | solution.py:373
  18.3 12.1 %collective-permute-start.5 = (bf16[256,256]{1,0:T(8,128)(2,1)}, bf16[256,256]{1,0:T(8,128)(2,1)}, u32[]{:S(2)}, u32[]{:S(2)}) collective-permute-start(bf16[256,256]{1,0:T(8,128)(2,1)} %collective-permute-done.3.refs_6_.refs_1_), channel_id=1, source_target_pairs={{0,2},{1,3},{2,0},{3,1},{4,6},{5,7},{6,4},{7,5},{8,10},{9,11},{10,... | collective-permute-start | bytes 393224 | tf_op jit(solution)/shard_map/ppermute | solution.py:373
  23.1 7.3 %collective-permute-start.4 = (bf16[256,256]{1,0:T(8,128)(2,1)}, bf16[256,256]{1,0:T(8,128)(2,1)}, u32[]{:S(2)}, u32[]{:S(2)}) collective-permute-start(bf16[256,256]{1,0:T(8,128)(2,1)} %collective-permute-done.3.refs_6_.refs_1_), channel_id=1, source_target_pairs={{0,1},{1,0},{2,3},{3,2},{4,5},{5,4},{6,7},{7,6},{8,9},{9,8},{10,11... | collective-permute-start | bytes 393224 | tf_op jit(solution)/shard_map/ppermute | solution.py:373
  28.8 11.9 %collective-permute-start.13 = (bf16[1024,128]{1,0:T(8,128)(2,1)S(1)}, bf16[1024,128]{1,0:T(8,128)(2,1)S(1)}, u32[]{:S(2)}, u32[]{:S(2)}) collective-permute-start(bf16[1024,128]{1,0:T(8,128)(2,1)S(1)} %get-tuple-element.46), channel_id=1, source_target_pairs={{0,2},{1,3},{2,0},{3,1},{4,6},{5,7},{6,4},{7,5},{8,10},{9,11},{10,... | collective-permute-start | bytes 786440 | tf_op jit(solution)/shard_map/ppermute | solution.py:373
  35.3 9.3 %collective-permute-start.17 = (bf16[128,1024]{1,0:T(8,128)(2,1)S(1)}, bf16[128,1024]{1,0:T(8,128)(2,1)S(1)}, u32[]{:S(2)}, u32[]{:S(2)}) collective-permute-start(bf16[128,1024]{1,0:T(8,128)(2,1)S(1)} %get-tuple-element.106), channel_id=1, source_target_pairs={{0,2},{1,3},{2,0},{3,1},{4,6},{5,7},{6,4},{7,5},{8,10},{9,11},{10,... | collective-permute-start | bytes 786440 | tf_op jit(solution)/shard_map/ppermute | solution.py:373
  35.8 14.4 %collective-permute-start.18 = (bf16[128,1024]{1,0:T(8,128)(2,1)S(1)}, bf16[128,1024]{1,0:T(8,128)(2,1)S(1)}, u32[]{:S(2)}, u32[]{:S(2)}) collective-permute-start(bf16[128,1024]{1,0:T(8,128)(2,1)S(1)} %get-tuple-element.107), channel_id=1, source_target_pairs={{0,2},{1,3},{2,0},{3,1},{4,6},{5,7},{6,4},{7,5},{8,10},{9,11},{10,... | collective-permute-start | bytes 786440 | tf_op jit(solution)/shard_map/ppermute | solution.py:373
  40.1 15.7 %collective-permute-start.19 = (bf16[128,1024]{1,0:T(8,128)(2,1)S(1)}, bf16[128,1024]{1,0:T(8,128)(2,1)S(1)}, u32[]{:S(2)}, u32[]{:S(2)}) collective-permute-start(bf16[128,1024]{1,0:T(8,128)(2,1)S(1)} %get-tuple-element.104), channel_id=1, source_target_pairs={{0,2},{1,3},{2,0},{3,1},{4,6},{5,7},{6,4},{7,5},{8,10},{9,11},{10,... | collective-permute-start | bytes 786440 | tf_op jit(solution)/shard_map/ppermute | solution.py:373
  40.6 19.6 %collective-permute-start.20 = (bf16[128,1024]{1,0:T(8,128)(2,1)S(1)}, bf16[128,1024]{1,0:T(8,128)(2,1)S(1)}, u32[]{:S(2)}, u32[]{:S(2)}) collective-permute-start(bf16[128,1024]{1,0:T(8,128)(2,1)S(1)} %get-tuple-element.105), channel_id=1, source_target_pairs={{0,2},{1,3},{2,0},{3,1},{4,6},{5,7},{6,4},{7,5},{8,10},{9,11},{10,... | collective-permute-start | bytes 786440 | tf_op jit(solution)/shard_map/ppermute | solution.py:373
  70.2 14.9 %collective-permute-start.25 = (bf16[1024,128]{1,0:T(8,128)(2,1)S(1)}, bf16[1024,128]{1,0:T(8,128)(2,1)S(1)}, u32[]{:S(2)}, u32[]{:S(2)}) collective-permute-start(bf16[1024,128]{1,0:T(8,128)(2,1)S(1)} %get-tuple-element.54), channel_id=1, source_target_pairs={{0,2},{1,3},{2,0},{3,1},{4,6},{5,7},{6,4},{7,5},{8,10},{9,11},{10,... | collective-permute-start | bytes 786440 | tf_op jit(solution)/shard_map/ppermute | solution.py:373
  71.9 22.9 %collective-permute-start.15 = (bf16[128,1280]{1,0:T(8,128)(2,1)S(1)}, bf16[128,1280]{1,0:T(8,128)(2,1)S(1)}, u32[]{:S(2)}, u32[]{:S(2)}) collective-permute-start(bf16[128,1280]{1,0:T(8,128)(2,1)S(1)} %get-tuple-element.50), channel_id=1, source_target_pairs={{4,2},{5,3},{6,0},{7,1},{8,6},{9,7},{10,4},{11,5},{12,10},{13,11},... | collective-permute-start | bytes 983048 | tf_op jit(solution)/shard_map/ppermute | solution.py:389
  75.2 19.6 %collective-permute-start.14 = (bf16[128,1280]{1,0:T(8,128)(2,1)S(1)}, bf16[128,1280]{1,0:T(8,128)(2,1)S(1)}, u32[]{:S(2)}, u32[]{:S(2)}) collective-permute-start(bf16[128,1280]{1,0:T(8,128)(2,1)S(1)} %get-tuple-element.50), channel_id=1, source_target_pairs={{4,0},{5,1},{6,2},{7,3},{8,4},{9,5},{10,6},{11,7},{12,8},{13,9},{1... | collective-permute-start | bytes 983048 | tf_op jit(solution)/shard_map/ppermute | solution.py:389
  86.2 12.1 %collective-permute-start.27 = (bf16[128,1024]{1,0:T(8,128)(2,1)S(1)}, bf16[128,1024]{1,0:T(8,128)(2,1)S(1)}, u32[]{:S(2)}, u32[]{:S(2)}) collective-permute-start(bf16[128,1024]{1,0:T(8,128)(2,1)S(1)} %get-tuple-element.55), channel_id=1, source_target_pairs={{0,6},{1,7},{2,4},{3,5},{4,10},{5,11},{6,8},{7,9},{8,14},{9,15},{1... | collective-permute-start | bytes 786440 | tf_op jit(solution)/shard_map/ppermute | solution.py:389
  91.1 11.3 %collective-permute-start.26 = (bf16[128,1024]{1,0:T(8,128)(2,1)S(1)}, bf16[128,1024]{1,0:T(8,128)(2,1)S(1)}, u32[]{:S(2)}, u32[]{:S(2)}) collective-permute-start(bf16[128,1024]{1,0:T(8,128)(2,1)S(1)} %get-tuple-element.55), channel_id=1, source_target_pairs={{0,4},{1,5},{2,6},{3,7},{4,8},{5,9},{6,10},{7,11},{8,12},{9,13},{1... | collective-permute-start | bytes 786440 | tf_op jit(solution)/shard_map/ppermute | solution.py:389
  110.2 8.1 %collective-permute-start.33 = (bf16[512,128]{1,0:T(8,128)(2,1)S(1)}, bf16[512,128]{1,0:T(8,128)(2,1)S(1)}, u32[]{:S(2)}, u32[]{:S(2)}) collective-permute-start(bf16[512,128]{1,0:T(8,128)(2,1)S(1)} %get-tuple-element.115), channel_id=1, source_target_pairs={{0,2},{1,3},{2,0},{3,1},{4,6},{5,7},{6,4},{7,5},{8,10},{9,11},{10,... | collective-permute-start | bytes 393224 | tf_op jit(solution)/shard_map/ppermute | solution.py:373
  111.6 6.9 %collective-permute-start.34 = (bf16[512,128]{1,0:T(8,128)(2,1)S(1)}, bf16[512,128]{1,0:T(8,128)(2,1)S(1)}, u32[]{:S(2)}, u32[]{:S(2)}) collective-permute-start(bf16[512,128]{1,0:T(8,128)(2,1)S(1)} %get-tuple-element.114), channel_id=1, source_target_pairs={{0,2},{1,3},{2,0},{3,1},{4,6},{5,7},{6,4},{7,5},{8,10},{9,11},{10,... | collective-permute-start | bytes 393224 | tf_op jit(solution)/shard_map/ppermute | solution.py:373
  112.3 52.1 %collective-permute-start.46 = (bf16[512,1024]{1,0:T(8,128)(2,1)S(1)}, bf16[512,1024]{1,0:T(8,128)(2,1)S(1)}, u32[]{:S(2)}, u32[]{:S(2)}) collective-permute-start(bf16[512,1024]{1,0:T(8,128)(2,1)S(1)} %add_convert_fusion.refs_13_), channel_id=1, source_target_pairs={{0,28},{4,24},{8,20},{12,16},{16,12},{20,8},{24,4},{28,0},{1,29},{... | collective-permute-start | bytes 3145736 | tf_op jit(solution)/shard_map/ppermute | solution.py:379
  118.0 7.5 %collective-permute-start.32 = (bf16[1024,128]{1,0:T(8,128)(2,1)S(1)}, bf16[1024,128]{1,0:T(8,128)(2,1)S(1)}, u32[]{:S(2)}, u32[]{:S(2)}) collective-permute-start(bf16[1024,128]{1,0:T(8,128)(2,1)S(1)} %get-tuple-element.59), channel_id=1, source_target_pairs={{0,2},{1,3},{2,0},{3,1},{4,6},{5,7},{6,4},{7,5},{8,10},{9,11},{10,... | collective-permute-start | bytes 786440 | tf_op jit(solution)/shard_map/ppermute | solution.py:373
  128.2 6.4 %collective-permute-start.43 = (bf16[256,256]{1,0:T(8,128)(2,1)S(1)}, bf16[256,256]{1,0:T(8,128)(2,1)S(1)}, u32[]{:S(2)}, u32[]{:S(2)}) collective-permute-start(bf16[256,256]{1,0:T(8,128)(2,1)S(1)} %get-tuple-element.111), channel_id=1, source_target_pairs={{0,2},{1,3},{2,0},{3,1},{4,6},{5,7},{6,4},{7,5},{8,10},{9,11},{10,... | collective-permute-start | bytes 393224 | tf_op jit(solution)/shard_map/ppermute | solution.py:373
  128.6 7.9 %collective-permute-start.44 = (bf16[256,256]{1,0:T(8,128)(2,1)S(1)}, bf16[256,256]{1,0:T(8,128)(2,1)S(1)}, u32[]{:S(2)}, u32[]{:S(2)}) collective-permute-start(bf16[256,256]{1,0:T(8,128)(2,1)S(1)} %get-tuple-element.113), channel_id=1, source_target_pairs={{0,3},{1,2},{2,1},{3,0},{4,7},{5,6},{6,5},{7,4},{8,11},{9,10},{10,... | collective-permute-start | bytes 393224 | tf_op jit(solution)/shard_map/ppermute | solution.py:373
  132.4 6.6 %collective-permute-start.35 = (bf16[128,1024]{1,0:T(8,128)(2,1)S(1)}, bf16[128,1024]{1,0:T(8,128)(2,1)S(1)}, u32[]{:S(2)}, u32[]{:S(2)}) collective-permute-start(bf16[128,1024]{1,0:T(8,128)(2,1)S(1)} %get-tuple-element.88), channel_id=1, source_target_pairs={{0,1},{1,0},{2,3},{3,2},{4,5},{5,4},{6,7},{7,6},{8,9},{9,8},{10,11... | collective-permute-start | bytes 786440 | tf_op jit(solution)/shard_map/ppermute | solution.py:373
  132.8 6.6 %collective-permute-start.38 = (bf16[128,1024]{1,0:T(8,128)(2,1)S(1)}, bf16[128,1024]{1,0:T(8,128)(2,1)S(1)}, u32[]{:S(2)}, u32[]{:S(2)}) collective-permute-start(bf16[128,1024]{1,0:T(8,128)(2,1)S(1)} %get-tuple-element.89), channel_id=1, source_target_pairs={{0,1},{1,0},{2,3},{3,2},{4,5},{5,4},{6,7},{7,6},{8,9},{9,8},{10,11... | collective-permute-start | bytes 786440 | tf_op jit(solution)/shard_map/ppermute | solution.py:373
  139.1 29.3 %collective-permute-start.39 = (bf16[256,256]{1,0:T(8,128)(2,1)S(1)}, bf16[256,256]{1,0:T(8,128)(2,1)S(1)}, u32[]{:S(2)}, u32[]{:S(2)}) collective-permute-start(bf16[256,256]{1,0:T(8,128)(2,1)S(1)} %get-tuple-element.108), channel_id=1, source_target_pairs={{0,1},{1,0},{2,3},{3,2},{4,5},{5,4},{6,7},{7,6},{8,9},{9,8},{10,11... | collective-permute-start | bytes 393224 | tf_op jit(solution)/shard_map/ppermute | solution.py:373
  139.4 29.0 %collective-permute-start.40 = (bf16[256,256]{1,0:T(8,128)(2,1)S(1)}, bf16[256,256]{1,0:T(8,128)(2,1)S(1)}, u32[]{:S(2)}, u32[]{:S(2)}) collective-permute-start(bf16[256,256]{1,0:T(8,128)(2,1)S(1)} %get-tuple-element.110), channel_id=1, source_target_pairs={{0,2},{1,3},{2,0},{3,1},{4,6},{5,7},{6,4},{7,5},{8,10},{9,11},{10,... | collective-permute-start | bytes 393224 | tf_op jit(solution)/shard_map/ppermute | solution.py:373
  139.8 28.6 %collective-permute-start.41 = (bf16[256,256]{1,0:T(8,128)(2,1)S(1)}, bf16[256,256]{1,0:T(8,128)(2,1)S(1)}, u32[]{:S(2)}, u32[]{:S(2)}) collective-permute-start(bf16[256,256]{1,0:T(8,128)(2,1)S(1)} %get-tuple-element.112), channel_id=1, source_target_pairs={{0,3},{1,2},{2,1},{3,0},{4,7},{5,6},{6,5},{7,4},{8,11},{9,10},{10,... | collective-permute-start | bytes 393224 | tf_op jit(solution)/shard_map/ppermute | solution.py:373
  141.0 27.4 %collective-permute-start.45 = (bf16[256,256]{1,0:T(8,128)(2,1)S(1)}, bf16[256,256]{1,0:T(8,128)(2,1)S(1)}, u32[]{:S(2)}, u32[]{:S(2)}) collective-permute-start(bf16[256,256]{1,0:T(8,128)(2,1)S(1)} %fusion.2), channel_id=1, source_target_pairs={{0,28},{4,24},{8,20},{12,16},{16,12},{20,8},{24,4},{28,0},{1,29},{... | collective-permute-start | bytes 393224 | tf_op jit(solution)/shard_map/ppermute | solution.py:379
  (37 other events, 189.6 us)

commit v4 on v3

--- a/solution.py
+++ b/solution.py
@@ -454,11 +454,11 @@
 
     def run_relay(r):
         x = joined[0] if r == 0 else gi[1, 0]
-        got = [relayed(x, r, k) for k in (0, half)]
-        block = pl.BlockSpec((x.shape[0], d), lambda i, *s: (0, 0))
-        own[r, 1] = [(got[0], block), piece(grad_new, r)]
-        par[r, 1] = [(got[1], block), piece(fresh_par)]
-        return got
+        got = relayed(x, r)
+        far = partner(got[:, :d]) if r == 0 else relayed(x, r, half)
+        own[r, 1] = [(got, pl.BlockSpec((x.shape[0], d), lambda i, *s: (0, 0))), piece(grad_new, r)]
+        par[r, 1] = [piece(far), piece(fresh_par)]
+        return [got]
 
     def run_outer(r, deps=()):
         gs = own[r, 0] + par[r, 0] + own[r, 1] + par[r, 1]
@@ -471,7 +471,7 @@
     run_front(0)
     run_front(1, [probs[0]])
     joined = run_middle(0, 0, [probs[1]])
-    mirror_out = hold(mirror_out, [came[0], came[1], gi[0, 0]])
+    mirror_out = hold(mirror_out, [came[0], came[1]])
     parts_out.append(with_mates(mirror_out))
     run_ahead(1, 0)
     run_middle(1, 0)

time: 170 us -> 168 us (0.988)
  starting transfers between devices: 44.4 us -> 39.6 us
  waiting for transfers between devices: 67.5 us -> 70.1 us
    ppermute x38 -> x39, waiting for transfers between devices: 40.3 us -> 44.9 us  [at_lane(): return lax.ppermute(x, 'lane', [(i, i ^ k) for i in range(lanes)])]
    ppermute x4, waiting for transfers between devices: 19.4 us -> 15 us  [mirrored(): lax.ppermute(x, 'section', [(i, sections - 1 - i) for i in range(sections)])]
    ppermute x4 -> x3, starting transfers between devices: 13.8 us -> 10.5 us  [relayed(): return lax.ppermute(x, ('section', 'lane'), pairs)]
    ppermute x4, starting transfers between devices: 7.18 us -> 4.2 us  [mirrored(): lax.ppermute(x, 'section', [(i, sections - 1 - i) for i in range(sections)])]
    ppermute x4 -> x3, waiting for transfers between devices: 7.75 us -> 10.2 us  [relayed(): return lax.ppermute(x, ('section', 'lane'), pairs)]
    ppermute x38 -> x39, starting transfers between devices: 22.8 us -> 24.3 us  [at_lane(): return lax.ppermute(x, 'lane', [(i, i ^ k) for i in range(lanes)])]
  transfers between devices with their start and end apart: 47 -> 47, of which waited for: 19 -> 18; matrix products, arithmetic and copies ran while one was open for 3% -> 3% of each run, Pallas kernels for 21% -> 23%
where the time goes in v4:
time: 168 us; the launch traced here: 167 us
  waiting for transfers between devices  70.1 us (42%)
  Pallas kernels  41.3 us (25%)
  starting transfers between devices  39.6 us (24%)
  local copies, waits for them, and re-layouts  10.2 us (6%)
  other arithmetic  4.75 us (3%)
    ppermute x39, waiting for transfers between devices, at_lane(): return lax.ppermute(x, 'lane', [(i, i ^ k) for i in range(lanes)])  44.9 us
    pallas_call x23, Pallas kernels, call(): pl.pallas_call(body, grid_spec=grid, out_shape=shapes, input_output_alias...  41.3 us
    ppermute x39, starting transfers between devices, at_lane(): return lax.ppermute(x, 'lane', [(i, i ^ k) for i in range(lanes)])  24.3 us
    ppermute x4, waiting for transfers between devices, mirrored(): lax.ppermute(x, 'section', [(i, sections - 1 - i) for i in range(sections)])  15 us
    ppermute x3, starting transfers between devices, relayed(): return lax.ppermute(x, ('section', 'lane'), pairs)  10.5 us
    ppermute x3, waiting for transfers between devices, relayed(): return lax.ppermute(x, ('section', 'lane'), pairs)  10.2 us
    unnamed x46, local copies, waits for them, and re-layouts  6.86 us
    ppermute x4, starting transfers between devices, mirrored(): lax.ppermute(x, 'section', [(i, sections - 1 - i) for i in range(sections)])  4.2 us
  transfers between devices with their start and end apart: 47, of which 18 were waited for; matrix products, arithmetic and copies ran while one was open for 3% of the time, Pallas kernels for 23%

profile of v4, /device:TPU:10, one launch (start us, length us, event | category | flops | bytes accessed | tf_op | source)
XLA Modules:
  0.0 167.2 jit_solution(13164271893418330932)
XLA Ops:
  1.6 1.6 collective-permute-start.3
  15.8 1.6 collective-permute-start.16
  19.1 4.5 %collective-permute-done.7.refs_2_.refs_4_ = bf16[2,128,1024]{2,1,0:T(8,128)(2,1)S(1)} collective-permute-done((bf16[2,128,1024]{2,1,0:T(8,128)(2,1)}, bf16[2,128,1024]{2,1,0:T(8,128)(2,1)S(1)}, u32[]{:S(2)}, u32[]{:S(2)}) %collective-permute-start.7) | collective-permute-done | bytes 524320 | tf_op jit(solution)/shard_map/ppermute | solution.py:373
  26.6 3.1 %ahead.4 = (bf16[1024,128]{1,0:T(8,128)(2,1)S(1)}, bf16[1024,128]{1,0:T(8,128)(2,1)S(1)}) custom-call(s32[6]{0:T(128)S(1)} %stack.80.refs_0_, bf16[2,1,128,1024]{3,2,1,0:T(8,128)(2,1)S(1)} %copy-done.2, bf16[2,128,1024]{2,1,0:T(8,128)(2,1)S(1)} %collective-permute-done.7.refs_2_.refs_4_, bf16[128,1024]{1,0:T(8,128)(2,1)} %get-tuple-element.103.refs_3_.refs_5_, ...), custom_call_target="tpu_custom_call" | custom-call | flops 1 | bytes 1 | tf_op jit(solution)/shard_map/ahead/pallas_call | solution.py:51
  29.8 2.2 %values.1 = (bf16[2,1024,256]{2,1,0:T(8,128)(2,1)S(1)}, bf16[2,2,128,256]{3,2,1,0:T(8,128)(2,1)S(1)}) custom-call(s32[6]{0:T(128)S(1)} %stack.80.refs_0_, bf16[2,2,1,128,1024]{4,3,2,1,0:T(8,128)(2,1)S(1)} %copy-done.6, bf16[256,256]{1,0:T(8,128)(2,1)S(1)} %convert_bitcast_fusion.refs_2_, bf16[256,256]{1,0:T(8,128)(2,1)S(1)} %copy-done.13, ...), custom_call_target="tpu_custom_call" | custom-call | flops 1 | bytes 1 | tf_op jit(solution)/shard_map/values/pallas_call | solution.py:51
  32.0 2.7 %front.2 = (bf16[2,2,128,1024]{3,2,1,0:T(8,128)(2,1)S(1)}, bf16[2,128,1024]{2,1,0:T(8,128)(2,1)S(1)}, bf16[2,128,1024]{2,1,0:T(8,128)(2,1)S(1)}) custom-call(s32[6]{0:T(128)S(1)} %stack.80.refs_0_, s32[18]{0:T(128)S(1)} %pad_add_fusion.refs_1_, bf16[2,2,1,128,2048]{4,3,2,1,0:T(8,128)(2,1)S(1)} %copy-done.1, bf16[2,2,1,128,256]{4,3,2,1,0:T(8,128)(2,1)S(1)} %copy-done.5, ...), custom_call_target="tpu_custom_call" | custom-call | flops 1 | bytes 1 | tf_op jit(solution)/shard_map/front/pallas_call | solution.py:51
  34.6 2.7 %front.3 = (bf16[2,2,128,1024]{3,2,1,0:T(8,128)(2,1)S(1)}, bf16[2,128,1024]{2,1,0:T(8,128)(2,1)S(1)}, bf16[2,128,1024]{2,1,0:T(8,128)(2,1)S(1)}) custom-call(s32[6]{0:T(128)S(1)} %stack.80.refs_0_, s32[18]{0:T(128)S(1)} %pad_add_fusion.refs_1_, bf16[2,2,1,128,2048]{4,3,2,1,0:T(8,128)(2,1)S(1)} %copy-done.1, bf16[2,2,1,128,256]{4,3,2,1,0:T(8,128)(2,1)S(1)} %copy-done.5, ...), custom_call_target="tpu_custom_call" | custom-call | flops 1 | bytes 1 | tf_op jit(solution)/shard_map/front/pallas_call | solution.py:51
  41.6 4.9 %collective-permute-done.19 = bf16[128,1024]{1,0:T(8,128)(2,1)S(1)} collective-permute-done((bf16[128,1024]{1,0:T(8,128)(2,1)S(1)}, bf16[128,1024]{1,0:T(8,128)(2,1)S(1)}, u32[]{:S(2)}, u32[]{:S(2)}) %collective-permute-start.19) | collective-permute-done | bytes 262176 | tf_op jit(solution)/shard_map/ppermute | solution.py:373
  46.5 5.6 %collective-permute-done.20 = bf16[128,1024]{1,0:T(8,128)(2,1)S(1)} collective-permute-done((bf16[128,1024]{1,0:T(8,128)(2,1)S(1)}, bf16[128,1024]{1,0:T(8,128)(2,1)S(1)}, u32[]{:S(2)}, u32[]{:S(2)}) %collective-permute-start.20) | collective-permute-done | bytes 262176 | tf_op jit(solution)/shard_map/ppermute | solution.py:373
  52.2 5.6 %collective-permute-done.17 = bf16[128,1024]{1,0:T(8,128)(2,1)S(1)} collective-permute-done((bf16[128,1024]{1,0:T(8,128)(2,1)S(1)}, bf16[128,1024]{1,0:T(8,128)(2,1)S(1)}, u32[]{:S(2)}, u32[]{:S(2)}) %collective-permute-start.17) | collective-permute-done | bytes 262176 | tf_op jit(solution)/shard_map/ppermute | solution.py:373
  57.7 5.6 %collective-permute-done.18 = bf16[128,1024]{1,0:T(8,128)(2,1)S(1)} collective-permute-done((bf16[128,1024]{1,0:T(8,128)(2,1)S(1)}, bf16[128,1024]{1,0:T(8,128)(2,1)S(1)}, u32[]{:S(2)}, u32[]{:S(2)}) %collective-permute-start.18) | collective-permute-done | bytes 262176 | tf_op jit(solution)/shard_map/ppermute | solution.py:373
  68.5 1.8 %ahead.5 = (bf16[1024,128]{1,0:T(8,128)(2,1)S(1)}, bf16[1024,128]{1,0:T(8,128)(2,1)S(1)}) custom-call(s32[6]{0:T(128)S(1)} %stack.80.refs_0_, bf16[2,1,128,1024]{3,2,1,0:T(8,128)(2,1)S(1)} %copy-done.2, bf16[2,128,1024]{2,1,0:T(8,128)(2,1)S(1)} %collective-permute-done.7.refs_2_.refs_4_, bf16[128,1024]{1,0:T(8,128)(2,1)S(1)} %get-tuple-element.99.refs_3_.refs_5_, ...), custom_call_target="tpu_custom_call" | custom-call | flops 1 | bytes 1 | tf_op jit(solution)/shard_map/ahead/pallas_call | solution.py:51
  71.8 4.1 %collective-permute-done.13.refs_4_.refs_6_ = bf16[1024,128]{1,0:T(8,128)(2,1)S(1)} collective-permute-done((bf16[1024,128]{1,0:T(8,128)(2,1)S(1)}, bf16[1024,128]{1,0:T(8,128)(2,1)S(1)}, u32[]{:S(2)}, u32[]{:S(2)}) %collective-permute-start.13) | collective-permute-done | bytes 262176 | tf_op jit(solution)/shard_map/ppermute | solution.py:373
  77.0 2.5 %collective-permute-start.14 = (bf16[128,1280]{1,0:T(8,128)(2,1)S(1)}, bf16[128,1280]{1,0:T(8,128)(2,1)S(1)}, u32[]{:S(2)}, u32[]{:S(2)}) collective-permute-start(bf16[128,1280]{1,0:T(8,128)(2,1)S(1)} %get-tuple-element.50), channel_id=1, source_target_pairs={{4,0},{5,1},{6,2},{7,3},{8,4},{9,5},{10,6},{11,7},{12,8},{13,9},{1... | collective-permute-start | bytes 983048 | tf_op jit(solution)/shard_map/ppermute | solution.py:389
  81.8 3.5 %collective-permute-start.26 = (bf16[128,1024]{1,0:T(8,128)(2,1)S(1)}, bf16[128,1024]{1,0:T(8,128)(2,1)S(1)}, u32[]{:S(2)}, u32[]{:S(2)}) collective-permute-start(bf16[128,1024]{1,0:T(8,128)(2,1)S(1)} %get-tuple-element.55), channel_id=1, source_target_pairs={{0,4},{1,5},{2,6},{3,7},{4,8},{5,9},{6,10},{7,11},{8,12},{9,13},{1... | collective-permute-start | bytes 786440 | tf_op jit(solution)/shard_map/ppermute | solution.py:389
  85.2 4.5 %collective-permute-start.27 = (bf16[128,1024]{1,0:T(8,128)(2,1)S(1)}, bf16[128,1024]{1,0:T(8,128)(2,1)S(1)}, u32[]{:S(2)}, u32[]{:S(2)}) collective-permute-start(bf16[128,1024]{1,0:T(8,128)(2,1)S(1)} %get-tuple-element.55), channel_id=1, source_target_pairs={{0,6},{1,7},{2,4},{3,5},{4,10},{5,11},{6,8},{7,9},{8,14},{9,15},{1... | collective-permute-start | bytes 786440 | tf_op jit(solution)/shard_map/ppermute | solution.py:389
  89.8 3.7 %collective-permute-done.26.refs_5_.refs_1_ = bf16[128,1024]{1,0:T(8,128)(2,1)S(1)} collective-permute-done((bf16[128,1024]{1,0:T(8,128)(2,1)S(1)}, bf16[128,1024]{1,0:T(8,128)(2,1)S(1)}, u32[]{:S(2)}, u32[]{:S(2)}) %collective-permute-start.26) | collective-permute-done | bytes 262176 | tf_op jit(solution)/shard_map/ppermute | solution.py:389
  93.5 6.5 %collective-permute-done.27.refs_7_.refs_3_ = bf16[128,1024]{1,0:T(8,128)(2,1)S(1)} collective-permute-done((bf16[128,1024]{1,0:T(8,128)(2,1)S(1)}, bf16[128,1024]{1,0:T(8,128)(2,1)S(1)}, u32[]{:S(2)}, u32[]{:S(2)}) %collective-permute-start.27) | collective-permute-done | bytes 262176 | tf_op jit(solution)/shard_map/ppermute | solution.py:389
  100.0 2.1 %outer.4.refs_10_ = bf16[512,1024]{1,0:T(8,128)(2,1)S(1)} custom-call(s32[6]{0:T(128)S(1)} %stack.80.refs_0_, bf16[2,128,1024]{2,1,0:T(8,128)(2,1)S(1)} %get-tuple-element.56.refs_1_, bf16[2,128,1024]{2,1,0:T(8,128)(2,1)S(1)} %pad_maximum_fusion.1.refs_2_, bf16[2,1,128,1024]{3,2,1,0:T(8,128)(2,1)S(1)} %copy-done.2, ...), custom_call_target="tpu_custom_call" | custom-call | flops 1 | bytes 1 | tf_op jit(solution)/shard_map/outer/pallas_call | solution.py:51
  103.3 2.1 %outer.5 = f32[512,1024]{1,0:T(8,128)S(1)} custom-call(s32[6]{0:T(128)S(1)} %stack.80.refs_0_, bf16[2,128,1024]{2,1,0:T(8,128)(2,1)S(1)} %get-tuple-element.56.refs_1_, bf16[2,128,1024]{2,1,0:T(8,128)(2,1)S(1)} %pad_maximum_fusion.1.refs_2_, bf16[2,1,128,1024]{3,2,1,0:T(8,128)(2,1)S(1)} %copy-done.2, ...), custom_call_target="tpu_custom_call" | custom-call | flops 1 | bytes 1 | tf_op jit(solution)/shard_map/outer/pallas_call | solution.py:51
  106.4 1.8 %ahead.6 = (bf16[1024,128]{1,0:T(8,128)(2,1)S(1)}, bf16[1024,128]{1,0:T(8,128)(2,1)S(1)}) custom-call(s32[6]{0:T(128)S(1)} %stack.80.refs_0_, bf16[128,1024]{1,0:T(8,128)(2,1)S(1)} %collective-permute-done.26.refs_5_.refs_1_, bf16[2,128,1024]{2,1,0:T(8,128)(2,1)S(1)} %copy-done, bf16[128,1024]{1,0:T(8,128)(2,1)S(1)} %collective-permute-done.27.refs_7_.refs_3_, ...), custom_call_target="tpu_custom_call" | custom-call | flops 1 | bytes 1 | tf_op jit(solution)/shard_map/ahead/pallas_call | solution.py:51
  111.1 4.0 %collective-permute-done.15.refs_3_.refs_7_ = bf16[128,1024]{1,0:T(8,128)(2,1)S(1)} collective-permute-done((bf16[128,1024]{1,0:T(8,128)(2,1)S(1)}, bf16[128,1024]{1,0:T(8,128)(2,1)S(1)}, u32[]{:S(2)}, u32[]{:S(2)}) %collective-permute-start.15) | collective-permute-done | bytes 262176 | tf_op jit(solution)/shard_map/ppermute | solution.py:373
  115.1 3.1 %ahead.7 = (bf16[1024,128]{1,0:T(8,128)(2,1)S(1)}, bf16[1024,128]{1,0:T(8,128)(2,1)S(1)}) custom-call(s32[6]{0:T(128)S(1)} %stack.80.refs_0_, bf16[128,1280]{1,0:T(8,128)(2,1)S(1)} %collective-permute-done.14.refs_9_.refs_1_.refs_5_, bf16[2,128,1024]{2,1,0:T(8,128)(2,1)S(1)} %copy-done, bf16[128,1024]{1,0:T(8,128)(2,1)S(1)} %collective-permute-done.15.refs_3_.refs_7_, ...), custom_call_target="tpu_custom_call" | custom-call | flops 1 | bytes 1 | tf_op jit(solution)/shard_map/ahead/pallas_call | solution.py:51
  118.8 1.7 collective-permute-done.34
  121.5 3.9 %collective-permute-done.32.refs_5_.refs_8_ = bf16[1024,128]{1,0:T(8,128)(2,1)S(1)} collective-permute-done((bf16[1024,128]{1,0:T(8,128)(2,1)S(1)}, bf16[1024,128]{1,0:T(8,128)(2,1)S(1)}, u32[]{:S(2)}, u32[]{:S(2)}) %collective-permute-start.32) | collective-permute-done | bytes 262176 | tf_op jit(solution)/shard_map/ppermute | solution.py:373
  130.1 2.2 %outer.6.refs_10_ = bf16[512,1024]{1,0:T(8,128)(2,1)S(1)} custom-call(s32[6]{0:T(128)S(1)} %stack.80.refs_0_, bf16[2,128,1024]{2,1,0:T(8,128)(2,1)S(1)} %get-tuple-element.63.refs_1_, bf16[2,128,1024]{2,1,0:T(8,128)(2,1)S(1)} %pad_maximum_fusion.refs_1_.refs_2_, bf16[2,1,128,1024]{3,2,1,0:T(8,128)(2,1)S(1)} %copy-done.2, ...), custom_call_target="tpu_custom_call" | custom-call | flops 1 | bytes 1 | tf_op jit(solution)/shard_map/outer/pallas_call | solution.py:51
  134.5 2.0 %collective-permute-done.44 = bf16[256,256]{1,0:T(8,128)(2,1)S(1)} collective-permute-done((bf16[256,256]{1,0:T(8,128)(2,1)S(1)}, bf16[256,256]{1,0:T(8,128)(2,1)S(1)}, u32[]{:S(2)}, u32[]{:S(2)}) %collective-permute-start.44) | collective-permute-done | bytes 131104 | tf_op jit(solution)/shard_map/ppermute | solution.py:373
  137.0 2.2 %outer.7 = f32[512,1024]{1,0:T(8,128)S(1)} custom-call(s32[6]{0:T(128)S(1)} %stack.80.refs_0_, bf16[2,128,1024]{2,1,0:T(8,128)(2,1)S(1)} %get-tuple-element.63.refs_1_, bf16[2,128,1024]{2,1,0:T(8,128)(2,1)S(1)} %pad_maximum_fusion.refs_1_.refs_2_, bf16[2,1,128,1024]{3,2,1,0:T(8,128)(2,1)S(1)} %copy-done.2, ...), custom_call_target="tpu_custom_call" | custom-call | flops 1 | bytes 1 | tf_op jit(solution)/shard_map/outer/pallas_call | solution.py:51
  143.0 3.4 %back.2 = (bf16[2,2,1,128,2048]{4,3,2,1,0:T(8,128)(2,1)}, bf16[2,2,1,128,256]{4,3,2,1,0:T(8,128)(2,1)}) custom-call(s32[6]{0:T(128)S(1)} %stack.80.refs_0_, bf16[2,2,1,128,2048]{4,3,2,1,0:T(8,128)(2,1)S(1)} %copy-done.1, bf16[2,2,1,128,256]{4,3,2,1,0:T(8,128)(2,1)S(1)} %copy-done.5, bf16[2,2,128,256]{3,2,1,0:T(8,128)(2,1)S(1)} %get-tuple-element.44.refs_4_.refs_3_, ...), custom_call_target="tpu_custom_call" | custom-call | flops 1 | bytes 1 | tf_op jit(solution)/shard_map/back/pallas_call | solution.py:51
  146.4 3.4 %back.3 = (bf16[2,2,1,128,2048]{4,3,2,1,0:T(8,128)(2,1)}, bf16[2,2,1,128,256]{4,3,2,1,0:T(8,128)(2,1)}) custom-call(s32[6]{0:T(128)S(1)} %stack.80.refs_0_, bf16[2,2,1,128,2048]{4,3,2,1,0:T(8,128)(2,1)S(1)} %copy-done.1, bf16[2,2,1,128,256]{4,3,2,1,0:T(8,128)(2,1)S(1)} %copy-done.5, ...), custom_call_target="tpu_custom_call", output_to_operand_aliasing={{0}: (9, {}), {1}: (10, {})} | custom-call | flops 1 | bytes 1 | tf_op jit(solution)/shard_map/back/pallas_call | solution.py:51
  149.8 12.4 %collective-permute-done.46.refs_2_ = bf16[512,1024]{1,0:T(8,128)(2,1)S(1)} collective-permute-done((bf16[512,1024]{1,0:T(8,128)(2,1)S(1)}, bf16[512,1024]{1,0:T(8,128)(2,1)S(1)}, u32[]{:S(2)}, u32[]{:S(2)}) %collective-permute-start.46) | collective-permute-done | bytes 1048608 | tf_op jit(solution)/shard_map/ppermute | solution.py:379
  163.2 3.0 %update.1 = (f32[1,512,1024]{2,1,0:T(8,128)}, f32[1,512,1024]{2,1,0:T(8,128)}, f32[8,128]{1,0:T(8,128)S(1)}) custom-call(s32[6]{0:T(128)S(1)} %stack.80.refs_0_, f32[512,1024]{1,0:T(8,128)S(1)} %convert_add_fusion.refs_9_.refs_1_, bf16[512,1024]{1,0:T(8,128)(2,1)S(1)} %collective-permute-done.46.refs_2_, f32[1,512,1024]{2,1,0:T(8,128)S(1)} %copy-done.7, ...), custom_call_target="tpu_custom_call" | custom-call | flops 1 | bytes 1 | tf_op jit(solution)/shard_map/update/pallas_call | solution.py:51
  (158 shorter events, 52.2 us)
Async XLA Ops:
  1.6 9.1 %collective-permute-start.3 = (bf16[256,256]{1,0:T(8,128)(2,1)S(1)}, bf16[256,256]{1,0:T(8,128)(2,1)}, u32[]{:S(2)}, u32[]{:S(2)}) collective-permute-start(bf16[256,256]{1,0:T(8,128)(2,1)S(1)} %convert_bitcast_fusion.refs_2_), channel_id=1, source_target_pairs={{0,28},{4,24},{8,20},{12,16},{16,12},{20,8},{24,4},{28,0},{1,29},{... | collective-permute-start | bytes 393224 | tf_op jit(solution)/shard_map/ppermute | solution.py:379
  3.2 7.5 %collective-permute-start = (bf16[256,256]{1,0:T(8,128)(2,1)S(1)}, bf16[256,256]{1,0:T(8,128)(2,1)S(1)}, u32[]{:S(2)}, u32[]{:S(2)}) collective-permute-start(bf16[256,256]{1,0:T(8,128)(2,1)S(1)} %convert_bitcast_fusion.refs_2_), channel_id=1, source_target_pairs={{0,1},{1,0},{2,3},{3,2},{4,5},{5,4},{6,7},{7,6},{8,9},{9,8},{10,11... | collective-permute-start | bytes 393224 | tf_op jit(solution)/shard_map/ppermute | solution.py:373
  3.2 8.7 %collective-permute-start.1 = (bf16[256,256]{1,0:T(8,128)(2,1)S(1)}, bf16[256,256]{1,0:T(8,128)(2,1)S(1)}, u32[]{:S(2)}, u32[]{:S(2)}) collective-permute-start(bf16[256,256]{1,0:T(8,128)(2,1)S(1)} %convert_bitcast_fusion.refs_2_), channel_id=1, source_target_pairs={{0,2},{1,3},{2,0},{3,1},{4,6},{5,7},{6,4},{7,5},{8,10},{9,11},{10,... | collective-permute-start | bytes 393224 | tf_op jit(solution)/shard_map/ppermute | solution.py:373
  4.7 7.8 %collective-permute-start.2 = (bf16[256,256]{1,0:T(8,128)(2,1)S(1)}, bf16[256,256]{1,0:T(8,128)(2,1)S(1)}, u32[]{:S(2)}, u32[]{:S(2)}) collective-permute-start(bf16[256,256]{1,0:T(8,128)(2,1)S(1)} %convert_bitcast_fusion.refs_2_), channel_id=1, source_target_pairs={{0,3},{1,2},{2,1},{3,0},{4,7},{5,6},{6,5},{7,4},{8,11},{9,10},{10,... | collective-permute-start | bytes 393224 | tf_op jit(solution)/shard_map/ppermute | solution.py:373
  5.1 18.5 %collective-permute-start.7 = (bf16[2,128,1024]{2,1,0:T(8,128)(2,1)}, bf16[2,128,1024]{2,1,0:T(8,128)(2,1)S(1)}, u32[]{:S(2)}, u32[]{:S(2)}) collective-permute-start(bf16[2,128,1024]{2,1,0:T(8,128)(2,1)} %bitcast.73), channel_id=1, source_target_pairs={{0,2},{1,3},{2,0},{3,1},{4,6},{5,7},{6,4},{7,5},{8,10},{9,11},{10,... | collective-permute-start | bytes 1572872 | tf_op jit(solution)/shard_map/ppermute | solution.py:373
  15.1 14.5 %collective-permute-start.12 = (bf16[128,1024]{1,0:T(8,128)(2,1)}, bf16[128,1024]{1,0:T(8,128)(2,1)S(1)}, u32[]{:S(2)}, u32[]{:S(2)}) collective-permute-start(bf16[128,1024]{1,0:T(8,128)(2,1)} %dynamic-slice_bitcast_fusion), channel_id=1, source_target_pairs={{0,2},{1,3},{2,0},{3,1},{28,30},{29,31},{30,28},{31,29}} | collective-permute-start | bytes 786440 | tf_op jit(solution)/shard_map/ppermute | solution.py:393
  15.8 48.6 %collective-permute-start.16 = (bf16[512,1024]{1,0:T(8,128)(2,1)S(1)}, bf16[512,1024]{1,0:T(8,128)(2,1)}, u32[]{:S(2)}, u32[]{:S(2)}) collective-permute-start(bf16[512,1024]{1,0:T(8,128)(2,1)S(1)} %hold.3), channel_id=1, source_target_pairs={{0,28},{4,24},{8,20},{12,16},{16,12},{20,8},{24,4},{28,0},{1,29},{... | collective-permute-start | bytes 3145736 | tf_op jit(solution)/shard_map/ppermute | solution.py:379
  17.5 12.2 %collective-permute-start.4 = (bf16[256,256]{1,0:T(8,128)(2,1)}, bf16[256,256]{1,0:T(8,128)(2,1)}, u32[]{:S(2)}, u32[]{:S(2)}) collective-permute-start(bf16[256,256]{1,0:T(8,128)(2,1)} %collective-permute-done.3.refs_6_.refs_1_), channel_id=1, source_target_pairs={{0,1},{1,0},{2,3},{3,2},{4,5},{5,4},{6,7},{7,6},{8,9},{9,8},{10,11... | collective-permute-start | bytes 393224 | tf_op jit(solution)/shard_map/ppermute | solution.py:373
  17.5 12.2 %collective-permute-start.5 = (bf16[256,256]{1,0:T(8,128)(2,1)}, bf16[256,256]{1,0:T(8,128)(2,1)}, u32[]{:S(2)}, u32[]{:S(2)}) collective-permute-start(bf16[256,256]{1,0:T(8,128)(2,1)} %collective-permute-done.3.refs_6_.refs_1_), channel_id=1, source_target_pairs={{0,2},{1,3},{2,0},{3,1},{4,6},{5,7},{6,4},{7,5},{8,10},{9,11},{10,... | collective-permute-start | bytes 393224 | tf_op jit(solution)/shard_map/ppermute | solution.py:373
  23.6 6.1 %collective-permute-start.6 = (bf16[256,256]{1,0:T(8,128)(2,1)}, bf16[256,256]{1,0:T(8,128)(2,1)}, u32[]{:S(2)}, u32[]{:S(2)}) collective-permute-start(bf16[256,256]{1,0:T(8,128)(2,1)} %collective-permute-done.3.refs_6_.refs_1_), channel_id=1, source_target_pairs={{0,3},{1,2},{2,1},{3,0},{4,7},{5,6},{6,5},{7,4},{8,11},{9,10},{10,... | collective-permute-start | bytes 393224 | tf_op jit(solution)/shard_map/ppermute | solution.py:373
  37.3 9.1 %collective-permute-start.19 = (bf16[128,1024]{1,0:T(8,128)(2,1)S(1)}, bf16[128,1024]{1,0:T(8,128)(2,1)S(1)}, u32[]{:S(2)}, u32[]{:S(2)}) collective-permute-start(bf16[128,1024]{1,0:T(8,128)(2,1)S(1)} %get-tuple-element.104), channel_id=1, source_target_pairs={{0,2},{1,3},{2,0},{3,1},{4,6},{5,7},{6,4},{7,5},{8,10},{9,11},{10,... | collective-permute-start | bytes 786440 | tf_op jit(solution)/shard_map/ppermute | solution.py:373
  38.4 13.7 %collective-permute-start.20 = (bf16[128,1024]{1,0:T(8,128)(2,1)S(1)}, bf16[128,1024]{1,0:T(8,128)(2,1)S(1)}, u32[]{:S(2)}, u32[]{:S(2)}) collective-permute-start(bf16[128,1024]{1,0:T(8,128)(2,1)S(1)} %get-tuple-element.105), channel_id=1, source_target_pairs={{0,2},{1,3},{2,0},{3,1},{4,6},{5,7},{6,4},{7,5},{8,10},{9,11},{10,... | collective-permute-start | bytes 786440 | tf_op jit(solution)/shard_map/ppermute | solution.py:373
  39.5 18.3 %collective-permute-start.17 = (bf16[128,1024]{1,0:T(8,128)(2,1)S(1)}, bf16[128,1024]{1,0:T(8,128)(2,1)S(1)}, u32[]{:S(2)}, u32[]{:S(2)}) collective-permute-start(bf16[128,1024]{1,0:T(8,128)(2,1)S(1)} %get-tuple-element.106), channel_id=1, source_target_pairs={{0,2},{1,3},{2,0},{3,1},{4,6},{5,7},{6,4},{7,5},{8,10},{9,11},{10,... | collective-permute-start | bytes 786440 | tf_op jit(solution)/shard_map/ppermute | solution.py:373
  40.6 22.8 %collective-permute-start.18 = (bf16[128,1024]{1,0:T(8,128)(2,1)S(1)}, bf16[128,1024]{1,0:T(8,128)(2,1)S(1)}, u32[]{:S(2)}, u32[]{:S(2)}) collective-permute-start(bf16[128,1024]{1,0:T(8,128)(2,1)S(1)} %get-tuple-element.107), channel_id=1, source_target_pairs={{0,2},{1,3},{2,0},{3,1},{4,6},{5,7},{6,4},{7,5},{8,10},{9,11},{10,... | collective-permute-start | bytes 786440 | tf_op jit(solution)/shard_map/ppermute | solution.py:373
  66.8 9.2 %collective-permute-start.13 = (bf16[1024,128]{1,0:T(8,128)(2,1)S(1)}, bf16[1024,128]{1,0:T(8,128)(2,1)S(1)}, u32[]{:S(2)}, u32[]{:S(2)}) collective-permute-start(bf16[1024,128]{1,0:T(8,128)(2,1)S(1)} %get-tuple-element.46), channel_id=1, source_target_pairs={{0,2},{1,3},{2,0},{3,1},{4,6},{5,7},{6,4},{7,5},{8,10},{9,11},{10,... | collective-permute-start | bytes 786440 | tf_op jit(solution)/shard_map/ppermute | solution.py:373
  70.3 10.5 %collective-permute-start.25 = (bf16[1024,128]{1,0:T(8,128)(2,1)S(1)}, bf16[1024,128]{1,0:T(8,128)(2,1)S(1)}, u32[]{:S(2)}, u32[]{:S(2)}) collective-permute-start(bf16[1024,128]{1,0:T(8,128)(2,1)S(1)} %get-tuple-element.54), channel_id=1, source_target_pairs={{0,2},{1,3},{2,0},{3,1},{4,6},{5,7},{6,4},{7,5},{8,10},{9,11},{10,... | collective-permute-start | bytes 786440 | tf_op jit(solution)/shard_map/ppermute | solution.py:373
  77.0 12.8 %collective-permute-start.14 = (bf16[128,1280]{1,0:T(8,128)(2,1)S(1)}, bf16[128,1280]{1,0:T(8,128)(2,1)S(1)}, u32[]{:S(2)}, u32[]{:S(2)}) collective-permute-start(bf16[128,1280]{1,0:T(8,128)(2,1)S(1)} %get-tuple-element.50), channel_id=1, source_target_pairs={{4,0},{5,1},{6,2},{7,3},{8,4},{9,5},{10,6},{11,7},{12,8},{13,9},{1... | collective-permute-start | bytes 983048 | tf_op jit(solution)/shard_map/ppermute | solution.py:389
  81.8 11.7 %collective-permute-start.26 = (bf16[128,1024]{1,0:T(8,128)(2,1)S(1)}, bf16[128,1024]{1,0:T(8,128)(2,1)S(1)}, u32[]{:S(2)}, u32[]{:S(2)}) collective-permute-start(bf16[128,1024]{1,0:T(8,128)(2,1)S(1)} %get-tuple-element.55), channel_id=1, source_target_pairs={{0,4},{1,5},{2,6},{3,7},{4,8},{5,9},{6,10},{7,11},{8,12},{9,13},{1... | collective-permute-start | bytes 786440 | tf_op jit(solution)/shard_map/ppermute | solution.py:389
  85.2 14.7 %collective-permute-start.27 = (bf16[128,1024]{1,0:T(8,128)(2,1)S(1)}, bf16[128,1024]{1,0:T(8,128)(2,1)S(1)}, u32[]{:S(2)}, u32[]{:S(2)}) collective-permute-start(bf16[128,1024]{1,0:T(8,128)(2,1)S(1)} %get-tuple-element.55), channel_id=1, source_target_pairs={{0,6},{1,7},{2,4},{3,5},{4,10},{5,11},{6,8},{7,9},{8,14},{9,15},{1... | collective-permute-start | bytes 786440 | tf_op jit(solution)/shard_map/ppermute | solution.py:389
  105.9 9.2 %collective-permute-start.15 = (bf16[128,1024]{1,0:T(8,128)(2,1)S(1)}, bf16[128,1024]{1,0:T(8,128)(2,1)S(1)}, u32[]{:S(2)}, u32[]{:S(2)}) collective-permute-start(bf16[128,1024]{1,0:T(8,128)(2,1)S(1)} %slice.128), channel_id=1, source_target_pairs={{0,2},{1,3},{2,0},{3,1},{4,6},{5,7},{6,4},{7,5},{8,10},{9,11},{10,... | collective-permute-start | bytes 786440 | tf_op jit(solution)/shard_map/ppermute | solution.py:373
  108.3 10.5 %collective-permute-start.33 = (bf16[512,128]{1,0:T(8,128)(2,1)S(1)}, bf16[512,128]{1,0:T(8,128)(2,1)S(1)}, u32[]{:S(2)}, u32[]{:S(2)}) collective-permute-start(bf16[512,128]{1,0:T(8,128)(2,1)S(1)} %get-tuple-element.115), channel_id=1, source_target_pairs={{0,2},{1,3},{2,0},{3,1},{4,6},{5,7},{6,4},{7,5},{8,10},{9,11},{10,... | collective-permute-start | bytes 393224 | tf_op jit(solution)/shard_map/ppermute | solution.py:373
  109.9 10.6 %collective-permute-start.34 = (bf16[512,128]{1,0:T(8,128)(2,1)S(1)}, bf16[512,128]{1,0:T(8,128)(2,1)S(1)}, u32[]{:S(2)}, u32[]{:S(2)}) collective-permute-start(bf16[512,128]{1,0:T(8,128)(2,1)S(1)} %get-tuple-element.114), channel_id=1, source_target_pairs={{0,2},{1,3},{2,0},{3,1},{4,6},{5,7},{6,4},{7,5},{8,10},{9,11},{10,... | collective-permute-start | bytes 393224 | tf_op jit(solution)/shard_map/ppermute | solution.py:373
  110.4 51.9 %collective-permute-start.46 = (bf16[512,1024]{1,0:T(8,128)(2,1)S(1)}, bf16[512,1024]{1,0:T(8,128)(2,1)S(1)}, u32[]{:S(2)}, u32[]{:S(2)}) collective-permute-start(bf16[512,1024]{1,0:T(8,128)(2,1)S(1)} %add_convert_fusion.refs_13_), channel_id=1, source_target_pairs={{0,28},{4,24},{8,20},{12,16},{16,12},{20,8},{24,4},{28,0},{1,29},{... | collective-permute-start | bytes 3145736 | tf_op jit(solution)/shard_map/ppermute | solution.py:379
  118.2 7.3 %collective-permute-start.32 = (bf16[1024,128]{1,0:T(8,128)(2,1)S(1)}, bf16[1024,128]{1,0:T(8,128)(2,1)S(1)}, u32[]{:S(2)}, u32[]{:S(2)}) collective-permute-start(bf16[1024,128]{1,0:T(8,128)(2,1)S(1)} %get-tuple-element.59), channel_id=1, source_target_pairs={{0,2},{1,3},{2,0},{3,1},{4,6},{5,7},{6,4},{7,5},{8,10},{9,11},{10,... | collective-permute-start | bytes 786440 | tf_op jit(solution)/shard_map/ppermute | solution.py:373
  128.1 6.4 %collective-permute-start.43 = (bf16[256,256]{1,0:T(8,128)(2,1)S(1)}, bf16[256,256]{1,0:T(8,128)(2,1)S(1)}, u32[]{:S(2)}, u32[]{:S(2)}) collective-permute-start(bf16[256,256]{1,0:T(8,128)(2,1)S(1)} %get-tuple-element.111), channel_id=1, source_target_pairs={{0,2},{1,3},{2,0},{3,1},{4,6},{5,7},{6,4},{7,5},{8,10},{9,11},{10,... | collective-permute-start | bytes 393224 | tf_op jit(solution)/shard_map/ppermute | solution.py:373
  128.7 7.8 %collective-permute-start.44 = (bf16[256,256]{1,0:T(8,128)(2,1)S(1)}, bf16[256,256]{1,0:T(8,128)(2,1)S(1)}, u32[]{:S(2)}, u32[]{:S(2)}) collective-permute-start(bf16[256,256]{1,0:T(8,128)(2,1)S(1)} %get-tuple-element.113), channel_id=1, source_target_pairs={{0,3},{1,2},{2,1},{3,0},{4,7},{5,6},{6,5},{7,4},{8,11},{9,10},{10,... | collective-permute-start | bytes 393224 | tf_op jit(solution)/shard_map/ppermute | solution.py:373
  132.3 6.9 %collective-permute-start.35 = (bf16[128,1024]{1,0:T(8,128)(2,1)S(1)}, bf16[128,1024]{1,0:T(8,128)(2,1)S(1)}, u32[]{:S(2)}, u32[]{:S(2)}) collective-permute-start(bf16[128,1024]{1,0:T(8,128)(2,1)S(1)} %get-tuple-element.88), channel_id=1, source_target_pairs={{0,1},{1,0},{2,3},{3,2},{4,5},{5,4},{6,7},{7,6},{8,9},{9,8},{10,11... | collective-permute-start | bytes 786440 | tf_op jit(solution)/shard_map/ppermute | solution.py:373
  132.7 6.7 %collective-permute-start.36 = (bf16[128,1024]{1,0:T(8,128)(2,1)S(1)}, bf16[128,1024]{1,0:T(8,128)(2,1)S(1)}, u32[]{:S(2)}, u32[]{:S(2)}) collective-permute-start(bf16[128,1024]{1,0:T(8,128)(2,1)S(1)} %get-tuple-element.91), channel_id=1, source_target_pairs={{0,1},{1,0},{2,3},{3,2},{4,5},{5,4},{6,7},{7,6},{8,9},{9,8},{10,11... | collective-permute-start | bytes 786440 | tf_op jit(solution)/shard_map/ppermute | solution.py:373
  139.3 27.0 %collective-permute-start.39 = (bf16[256,256]{1,0:T(8,128)(2,1)S(1)}, bf16[256,256]{1,0:T(8,128)(2,1)S(1)}, u32[]{:S(2)}, u32[]{:S(2)}) collective-permute-start(bf16[256,256]{1,0:T(8,128)(2,1)S(1)} %get-tuple-element.108), channel_id=1, source_target_pairs={{0,1},{1,0},{2,3},{3,2},{4,5},{5,4},{6,7},{7,6},{8,9},{9,8},{10,11... | collective-permute-start | bytes 393224 | tf_op jit(solution)/shard_map/ppermute | solution.py:373
  139.4 26.9 %collective-permute-start.40 = (bf16[256,256]{1,0:T(8,128)(2,1)S(1)}, bf16[256,256]{1,0:T(8,128)(2,1)S(1)}, u32[]{:S(2)}, u32[]{:S(2)}) collective-permute-start(bf16[256,256]{1,0:T(8,128)(2,1)S(1)} %get-tuple-element.110), channel_id=1, source_target_pairs={{0,2},{1,3},{2,0},{3,1},{4,6},{5,7},{6,4},{7,5},{8,10},{9,11},{10,... | collective-permute-start | bytes 393224 | tf_op jit(solution)/shard_map/ppermute | solution.py:373
  140.0 26.3 %collective-permute-start.41 = (bf16[256,256]{1,0:T(8,128)(2,1)S(1)}, bf16[256,256]{1,0:T(8,128)(2,1)S(1)}, u32[]{:S(2)}, u32[]{:S(2)}) collective-permute-start(bf16[256,256]{1,0:T(8,128)(2,1)S(1)} %get-tuple-element.112), channel_id=1, source_target_pairs={{0,3},{1,2},{2,1},{3,0},{4,7},{5,6},{6,5},{7,4},{8,11},{9,10},{10,... | collective-permute-start | bytes 393224 | tf_op jit(solution)/shard_map/ppermute | solution.py:373
  141.2 25.0 %collective-permute-start.45 = (bf16[256,256]{1,0:T(8,128)(2,1)S(1)}, bf16[256,256]{1,0:T(8,128)(2,1)S(1)}, u32[]{:S(2)}, u32[]{:S(2)}) collective-permute-start(bf16[256,256]{1,0:T(8,128)(2,1)S(1)} %fusion.2), channel_id=1, source_target_pairs={{0,28},{4,24},{8,20},{12,16},{16,12},{20,8},{24,4},{28,0},{1,29},{... | collective-permute-start | bytes 393224 | tf_op jit(solution)/shard_map/ppermute | solution.py:379
  (37 other events, 184.3 us)
